TPU v7x, 32 devices: a whole 2x2x4 slice. The times are simulated.
32 devices in a mesh: tile: 8 (over z, y), frame: 4 (over x, core).
Axes of the slice: x: 2, y: 2, z: 4, core: 2. Of those that a mesh axis runs over, the one named last changes fastest.
Arguments:
- movie: bfloat16 [32, 512, 256], P(('frame', 'tile')), may hold values from -6 to 6
- footprints: bfloat16 [512, 256, 384], P('tile'), may hold values from -0.09375 to 0.09375
- support: int32 [64, 384], P('tile'), may hold values 0 or 1
- traces: bfloat16 [3072, 32], P('tile', 'frame'), may hold values from 0 to 2
- border_weight: float32 [512, 256], P('tile'), may hold values from 1 to 4
- border_offsets: int32 [64, 2], replicated, may hold values from -16 to 16, as said below
Outputs:
- new_traces: float32 [3072, 32], P('tile', 'frame')
- trace_gram: float32 [3072, 384], P('tile')
- remainder: bfloat16 [32, 512, 256], P(('frame', 'tile'))
Inputs may be any that keep to these rules, and one draw needn't show every extreme that they name: `border_offsets`: the 64 rows are distinct offsets (row, column) on the boundary of the square of half-side 16; (-16, -16) and (16, 16) are among them.
All inputs are finite; a program needn't handle non-finite values. No bound on the sum of `support` on one device may be relied on, other than what follows from the above.
Results may differ from a plain program's by a relative error of at most 0.009.
Values may be sent and summed in bfloat16 or wider, within the bound.
No kernel may reach another device: no remote copies, remote signals or barrier semaphores. Data moves between devices by JAX's collectives and lax.ppermute only.
A program may use at most 128 MiB of HBM per device.

v0:
```python
import math

import jax
import jax.numpy as jnp
from jax import lax
from jax.sharding import PartitionSpec as P

RR = 16
GR = 4
BR = 8
SWEEPS = 3
NR = 64
HALO = 20


def padded_2(cells, sides, width):
    for axis, dim in sides:
        count = lax.axis_size(axis)
        ends = count - 1
        head = lax.slice_in_dim(cells, 0, width, axis=dim)
        tail = lax.slice_in_dim(cells, cells.shape[dim] - width, cells.shape[dim], axis=dim)
        cells = jnp.concatenate(
            [
                lax.ppermute(tail, axis, [(i, (i + 1) % count) for i in range(ends)]),
                cells,
                lax.ppermute(head, axis, [((i + 1) % count, i) for i in range(ends)]),
            ],
            axis=dim,
        )
    return cells


def gaussian_taps(radius):
    spots = jnp.arange(-radius, radius + 1).astype(jnp.float32)
    raw_weights = jnp.exp(-2.0 * spots * spots / float(radius * radius))
    return raw_weights / jnp.sum(raw_weights)


def smooth_columns(values_in, taps_table, radius):
    extent = values_in.shape[2]
    padded = jnp.pad(values_in, ((0, 0), (0, 0), (radius, radius)))
    running = jnp.zeros(values_in.shape, jnp.float32)
    for offset_step in range(2 * radius + 1):
        running = (
            running + taps_table[offset_step] * padded[:, :, offset_step : offset_step + extent]
        )
    return running


def per_device(movie, footprints, support, traces, border_weight, border_offsets):
    tile_count = lax.axis_size("tile")
    tile_index = lax.axis_index("tile")
    tile_rows = footprints.shape[0]
    columns = footprints.shape[1]
    components = footprints.shape[2]
    strip_movie = lax.all_to_all(movie, "tile", split_axis=1, concat_axis=0, tiled=True)
    frame_count = strip_movie.shape[0]
    pixel_count = tile_rows * columns
    block_masks = jnp.repeat(support, BR, axis=0).astype(jnp.bfloat16)
    shaped = (footprints * block_masks[:, None, :]).reshape(pixel_count, components)
    movie_flat = strip_movie.reshape(frame_count, pixel_count)
    fitted = jnp.einsum("kf,pk->fp", traces, shaped, preferred_element_type=jnp.float32)
    first = (
        (movie_flat.astype(jnp.float32) - fitted)
        .astype(jnp.bfloat16)
        .reshape(frame_count, tile_rows, columns)
    )
    extended = padded_2(first, (("tile", 1),), HALO).astype(jnp.float32)
    taps_table = gaussian_taps(GR)
    span_rows = tile_rows + 2 * RR
    row_smooth = jnp.zeros((frame_count, span_rows, columns), jnp.float32)
    for offset_step in range(2 * GR + 1):
        row_smooth = (
            row_smooth
            + taps_table[offset_step] * extended[:, offset_step : offset_step + span_rows, :]
        )
    both_smooth = smooth_columns(row_smooth, taps_table, GR)
    global_rows = tile_index * tile_rows - RR + jnp.arange(span_rows)
    inside = (global_rows >= 0) & (global_rows < tile_count * tile_rows)
    smooth = jnp.where(inside[None, :, None], both_smooth, 0.0).astype(jnp.bfloat16)
    shifts = jnp.arange(-RR, RR + 1)
    rows_hot = (border_offsets[:, 0:1] == shifts[None, :]).astype(jnp.float32)
    cols_hot = (border_offsets[:, 1:2] == shifts[None, :]).astype(jnp.float32)
    counts = jnp.dot(rows_hot.T, cols_hot, precision=lax.Precision.HIGHEST)
    spread = jnp.arange(columns)[:, None] - jnp.arange(columns)[None, :]
    band = (spread[None, :, :] == shifts[:, None, None]).astype(jnp.float32)
    table = jnp.einsum("dk,kvx->dvx", counts, band, precision=lax.Precision.HIGHEST).astype(
        jnp.bfloat16
    )
    block_frames = math.gcd(frame_count, 16)

    def border_block(frame_block):
        stacked = jnp.stack(
            [
                frame_block[:, offset_step : offset_step + tile_rows, :]
                for offset_step in range(2 * RR + 1)
            ]
        )
        return jnp.einsum("dfyv,dvx->fyx", stacked, table, preferred_element_type=jnp.float32)

    summed = lax.map(
        border_block, smooth.reshape(frame_count // block_frames, block_frames, span_rows, columns)
    )
    summed = summed.reshape(frame_count, tile_rows, columns)
    background = border_weight[None, :, :] * summed / math.sqrt(NR)
    cleaned = (strip_movie.astype(jnp.float32) - background).astype(jnp.bfloat16)
    cleaned_flat = cleaned.reshape(frame_count, pixel_count)
    projected = jnp.einsum("pk,fp->kf", shaped, cleaned_flat, preferred_element_type=jnp.float32)
    coupling = jnp.einsum("pk,pq->kq", shaped, shaped, preferred_element_type=jnp.float32)
    floor_t = jnp.maximum(jnp.diagonal(coupling), 1.0)
    trace_state = traces.astype(jnp.float32)
    for sweep_index in range(SWEEPS):
        moved = jnp.dot(coupling, trace_state, precision=lax.Precision.HIGHEST)
        trace_state = jnp.maximum(trace_state + (projected - moved) / floor_t[:, None], 0.0)
    all_traces = lax.all_gather(
        trace_state.astype(jnp.bfloat16), "frame", axis=1, tiled=True
    ).astype(trace_state.dtype)
    trace_gram = jnp.dot(all_traces, all_traces.T, precision=lax.Precision.HIGHEST)
    rounded = trace_state.astype(jnp.bfloat16)
    refit = jnp.einsum("kf,pk->fp", rounded, shaped, preferred_element_type=jnp.float32)
    leftover = (
        (cleaned_flat.astype(jnp.float32) - refit)
        .astype(jnp.bfloat16)
        .reshape(frame_count, tile_rows, columns)
    )
    remainder = lax.all_to_all(leftover, "tile", split_axis=0, concat_axis=1, tiled=True)
    return (trace_state, trace_gram, remainder)


def solution(mesh):
    return jax.shard_map(
        per_device,
        mesh=mesh,
        in_specs=(
            P(("frame", "tile"), None, None),
            P("tile", None, None),
            P("tile", None),
            P("tile", "frame"),
            P("tile", None),
            P(),
        ),
        out_specs=(P("tile", "frame"), P("tile", None), P(("frame", "tile"), None, None)),
        check_vma=False,
    )
```

profile of v0, /device:TPU:0, one launch (start us, length us, event | category | flops | bytes accessed | tf_op | source)
XLA Modules:
  0.0 106.6 jit_solution(2406745508609148343)
XLA Ops:
  0.6 1.4 %copy.180 = bf16[1,512,256]{2,0,1:T(2,128)(2,1)S(1)} copy(bf16[1,512,256]{2,1,0:T(8,128)(2,1)} %param.6) | data formatting | bytes 524288 | tf_op args[0]
  2.5 2.2 %reduce.2 = bf16[512,256]{1,0:T(8,128)(2,1)S(1)} reduce(bf16[512,1,256]{2,1,0:T(2,128)(2,1)S(1)} %bitcast.275, bf16[]{:T(256)} %broadcast.93), dimensions={1}, to_apply=%bitcast.266.reduce_sub_computation | reduce | bytes 524290
  5.5 7.3 %all-to-all-start = ((bf16[8,2,8192]{2,1,0:T(2,128)(2,1)}), bf16[8,2,8192]{2,1,0:T(2,128)(2,1)S(1)}, u32[]{:S(2)}, u32[]{:S(2)}) async-start(bf16[8,2,8192]{2,1,0:T(2,128)(2,1)} %reshape.94), calls=%async_computation | async-start | bytes 524288 | tf_op jit(solution)/shard_map/all_to_all | solution.py:56
  15.6 6.5 %broadcast_multiply_fusion = bf16[64,256,384]{2,1,0:T(8,128)(2,1)S(1)} fusion(bf16[64,256,384]{2,1,0:T(8,128)(2,1)} %param.7, bf16[64,384]{1,0:T(8,128)(2,1)S(1)} %broadcast_bitcast_fusion), kind=kLoop, calls=%fused_computation.8 | loop fusion | flops 6291456 | bytes 25214976 | tf_op jit(solution)/shard_map/mul | solution.py:60
  22.2 4.5 %copy-done = bf16[64,256,384]{2,1,0:T(8,128)(2,1)} copy-done((bf16[64,256,384]{2,1,0:T(8,128)(2,1)}, bf16[64,256,384]{2,1,0:T(8,128)(2,1)S(1)}, u32[]{:S(2)}) %copy-start) | copy-done | bytes 12582936
  26.7 6.7 %convolution_bitcast_fusion.1 = f32[384,384]{1,0:T(8,128)S(1)} fusion(bf16[64,256,384]{2,1,0:T(8,128)(2,1)S(1)} %broadcast_multiply_fusion), kind=kOutput, calls=%fused_computation.23 | convolution fusion | flops 4831838208 | bytes 13172736 | tf_op jit(solution)/shard_map/pk,pq->kq/dot_general | solution.py:109
  33.3 3.4 %gather_fusion = f32[384]{0:T(512)S(1)} fusion(f32[384,384]{1,0:T(8,128)S(1)} %convolution_bitcast_fusion.1, s32[384]{0:T(512)S(1)} %or_reduce_fusion), kind=kCustom, calls=%fused_computation | custom fusion | bytes 6144 | tf_op jit(solution)/shard_map/jit(diagonal)/cond/branch_0_fun/gather | solution.py:110
  37.8 6.5 %fusion.10 = bf16[33,256,256]{2,0,1:T(8,128)(2,1)} fusion(f32[33,33,1]{1,0,2:T(8,128)S(1)} %convolution_bitcast_fusion.2, s32[256,256]{1,0:T(8,128)S(1)} %iota_subtract_fusion, s32[33]{0:T(128)S(1)} %iota_add_fusion), kind=kOutput, calls=%fused_computation.14 | convolution fusion | flops 860749824 | bytes 4592008 | tf_op jit(solution)/shard_map/dk,kvx->dvx/dot_general | solution.py:87
  44.7 7.9 %fusion.2 = bf16[8,16384]{1,0:T(8,128)(2,1)S(1)} fusion(f32[8,16384]{1,0:T(8,128)S(1)} %reshape.81, bf16[16384,384]{1,0:T(8,128)(2,1)} %bitcast.267, bf16[384,8]{0,1:T(8,128)(2,1)S(1)} %copy-done.2), kind=kOutput, calls=%fused_computation.5 | convolution fusion | flops 100925440 | bytes 13375488 | tf_op jit(solution)/shard_map/kf,pk->fp/dot_general | solution.py:62
  52.8 3.9 %collective-permute-start = (bf16[8,20,256]{2,1,0:T(8,128)(2,1)S(1)}, bf16[8,20,256]{2,1,0:T(8,128)(2,1)S(1)}, u32[]{:S(2)}, u32[]{:S(2)}) collective-permute-start(bf16[8,20,256]{2,1,0:T(8,128)(2,1)S(1)} %get-tuple-element.11), channel_id=1, source_target_pairs={{0,4},{4,8},{8,12},{12,16},{16,20},{20,24},{24,28},{1,5},{5,9},{9,... | collective-permute-start | bytes 245768 | tf_op jit(solution)/shard_map/ppermute | solution.py:24
  56.7 1.5 %collective-permute-start.1 = (bf16[8,20,256]{2,1,0:T(8,128)(2,1)S(1)}, bf16[8,20,256]{2,1,0:T(8,128)(2,1)S(1)}, u32[]{:S(2)}, u32[]{:S(2)}) collective-permute-start(bf16[8,20,256]{2,1,0:T(8,128)(2,1)S(1)} %get-tuple-element.16), channel_id=1, source_target_pairs={{4,0},{8,4},{12,8},{16,12},{20,16},{24,20},{28,24},{5,1},{9,5},{13... | collective-permute-start | bytes 245768 | tf_op jit(solution)/shard_map/ppermute | solution.py:26
  58.9 4.3 %collective-permute-done.1 = bf16[8,20,256]{2,1,0:T(8,128)(2,1)S(1)} collective-permute-done((bf16[8,20,256]{2,1,0:T(8,128)(2,1)S(1)}, bf16[8,20,256]{2,1,0:T(8,128)(2,1)S(1)}, u32[]{:S(2)}, u32[]{:S(2)}) %collective-permute-start.1) | collective-permute-done | bytes 81952 | tf_op jit(solution)/shard_map/ppermute | solution.py:26
  63.3 6.5 %fusion.40 = f32[8,96,256]{2,1,0:T(8,128)S(1)} fusion(f32[8,104,256]{2,1,0:T(8,128)S(1)} %maximum_convert_fusion, f32[]{:T(128)} %bitcast.13, f32[]{:T(128)} %bitcast.12, f32[]{:T(128)} %bitcast.11, f32[]{:T(128)} %bitcast.10, f32[]{:T(128)} %bitcast.9, f32[]{:T(128)} %bitcast.8, f32[]{:T(128)} %bitcast.7, f32[]{:T(128)} %bitcast.6, f32[]{:T(128)} %bitcast.2), kind=kLoop, calls=%fused_computation.57 | loop fusion | flops 3342336 | bytes 7864356 | tf_op jit(solution)/shard_map/add | solution.py:74
  69.8 7.4 %fusion.32 = bf16[8,96,256]{2,1,0:T(8,128)(2,1)S(1)} fusion(f32[8,96,256]{2,1,0:T(8,128)S(1)} %fusion.40, f32[]{:T(128)} %bitcast.13, f32[]{:T(128)} %bitcast.12, f32[]{:T(128)} %bitcast.11, f32[]{:T(128)} %bitcast.10, f32[]{:T(128)} %bitcast.9, f32[]{:T(128)} %bitcast.8, f32[]{:T(128)} %bitcast.7, f32[]{:T(128)} %bitcast.6, f32[]{:T(128)} %bitcast.2, ...), kind=kLoop, calls=%fused_computation.48 | loop fusion | flops 3735552 | bytes 1179780 | tf_op jit(solution)/shard_map/convert_element_type | solution.py:80
  79.9 2.4 %fusion.50 = (bf16[8,64,256]{2,1,0:T(8,128)(2,1)S(1)}, f32[8,64,256,1]{2,1,3,0:T(8,128)S(1)}) fusion(f32[8,64,256]{2,1,0:T(8,128)S(1)} %bitcast.274, f32[64,256]{1,0:T(8,128)S(1)} %copy-done.1, bf16[33,8,64,256]{3,2,0,1:T(8,128)(2,1)S(1)} %fusion.51, bf16[33,256,256]{2,0,1:T(8,128)(2,1)S(1)} %bitcast.272), kind=kOutput, calls=%fused_computation.76 | convolution fusion | flops 2215116800 | bytes 14352384 | tf_op jit(solution)/shard_map/while/body/eval_jaxpr/dfyv,dvx->fyx/dot_general | solution.py:99
  82.5 1.2 %slice-done.2 = s8[4194304]{0:T(1024)(128)(4,1)S(1)} async-done(((s8[12582912]{0:T(1024)(128)(4,1)}), s8[4194304]{0:T(1024)(128)(4,1)S(1)}, s32[]{:S(2)}) %slice-start.2) | async-done | bytes 4194328
  83.6 1.8 %convolution_bitcast_fusion.3 = f32[384,8]{0,1:T(8,128)S(1)} fusion(bf16[64,256,384]{2,1,0:T(8,128)(2,1)S(1)} %bitcast.269, bf16[8,64,256]{2,1,0:T(8,128)(2,1)S(1)} %get-tuple-element.28), kind=kOutput, calls=%fused_computation.29 | convolution fusion | flops 100663296 | bytes 12857344 | tf_op jit(solution)/shard_map/pk,fp->kf/dot_general | solution.py:108
  86.5 1.3 %fusion.95 = (bf16[384,8]{0,1:T(8,128)(2,1)S(1)}, f32[384,8]{0,1:T(8,128)}) fusion(f32[384,8]{0,1:T(8,128)S(1)} %fusion.21, f32[384]{0:T(512)S(1)} %broadcast_maximum_fusion, f32[384,8]{0,1:T(8,128)S(1)} %convolution_bitcast_fusion.3, f32[384,384]{1,0:T(8,128)S(1)} %convolution_bitcast_fusion.1), kind=kOutput, calls=%fused_computation.167 | convolution fusion | flops 14171136 | bytes 634368 | tf_op jit(solution)/shard_map/dot_general | solution.py:113
  88.1 3.3 %fusion = bf16[8,16384]{1,0:T(8,128)(2,1)S(1)} fusion(bf16[384,8]{0,1:T(8,128)(2,1)S(1)} %get-tuple-element.30, bf16[16384,384]{1,0:T(8,128)(2,1)S(1)} %bitcast.270, f32[8,16384]{1,0:T(8,128)S(1)} %reshape.81, f32[8,16384]{1,0:T(8,128)S(1)} %bitcast.273, f32[16384]{0:T(1024)S(1)} %bitcast.281), kind=kOutput, calls=%fused_computation.3 | convolution fusion | flops 101580800 | bytes 13965312 | tf_op jit(solution)/shard_map/kf,pk->fp/dot_general | solution.py:120
  91.4 0.8 copy.165
  92.2 5.4 %all-to-all-start.1 = ((bf16[8,64,256]{2,1,0:T(8,128)(2,1)}), bf16[8,64,256]{2,1,0:T(8,128)(2,1)S(1)}, u32[]{:S(2)}, u32[]{:S(2)}) async-start(bf16[8,64,256]{2,1,0:T(8,128)(2,1)} %copy.165), calls=%async_computation.1 | async-start | bytes 524288 | tf_op jit(solution)/shard_map/all_to_all | solution.py:126
  97.6 5.2 %all_gather.3 = bf16[384,32]{0,1:T(8,128)(2,1)S(1)} all-gather(bf16[384,8]{0,1:T(8,128)(2,1)S(1)} %get-tuple-element.30), channel_id=1, replica_groups=mesh['tile'=8,'frame'=4] {'frame'}, dimensions={1}, use_global_device_ids=true | all-gather | bytes 30720 | tf_op jit(solution)/shard_map/all_gather | solution.py:115
  102.8 1.1 %fusion.96 = f32[384,384]{1,0:T(8,128)} fusion(bf16[384,32]{0,1:T(8,128)(2,1)S(1)} %all_gather.3), kind=kOutput, calls=%fused_computation.169 | convolution fusion | flops 9437184 | bytes 614400 | tf_op jit(solution)/shard_map/dot_general | solution.py:118
  103.9 2.0 %all-to-all-done.1 = bf16[8,64,256]{2,1,0:T(8,128)(2,1)S(1)} async-done(((bf16[8,64,256]{2,1,0:T(8,128)(2,1)}), bf16[8,64,256]{2,1,0:T(8,128)(2,1)S(1)}, u32[]{:S(2)}, u32[]{:S(2)}) %all-to-all-start.1) | async-done | bytes 262176 | tf_op jit(solution)/shard_map/all_to_all | solution.py:126
  (76 shorter events, 10.9 us)
Async XLA Ops:
  5.5 38.8 %all-to-all-start = ((bf16[8,2,8192]{2,1,0:T(2,128)(2,1)}), bf16[8,2,8192]{2,1,0:T(2,128)(2,1)S(1)}, u32[]{:S(2)}, u32[]{:S(2)}) async-start(bf16[8,2,8192]{2,1,0:T(2,128)(2,1)} %reshape.94), calls=%async_computation | async-start | bytes 524288 | tf_op jit(solution)/shard_map/all_to_all | solution.py:56
  22.1 4.5 %copy-start = (bf16[64,256,384]{2,1,0:T(8,128)(2,1)}, bf16[64,256,384]{2,1,0:T(8,128)(2,1)S(1)}, u32[]{:S(2)}) copy-start(bf16[64,256,384]{2,1,0:T(8,128)(2,1)S(1)} %broadcast_multiply_fusion) | copy-start | bytes 37748740
  26.7 10.1 %copy-start.1 = (f32[64,256]{1,0:T(8,128)S(1)}, f32[64,256]{1,0:T(8,128)}, u32[]{:S(2)}) copy-start(f32[64,256]{1,0:T(8,128)} %param.10) | copy-start | bytes 196612
  33.3 11.4 %copy-start.2 = (bf16[384,8]{0,1:T(8,128)(2,1)S(1)}, bf16[384,8]{0,1:T(8,128)(2,1)}, u32[]{:S(2)}) copy-start(bf16[384,8]{0,1:T(8,128)(2,1)} %param.9) | copy-start | bytes 18436
  52.8 6.1 %collective-permute-start = (bf16[8,20,256]{2,1,0:T(8,128)(2,1)S(1)}, bf16[8,20,256]{2,1,0:T(8,128)(2,1)S(1)}, u32[]{:S(2)}, u32[]{:S(2)}) collective-permute-start(bf16[8,20,256]{2,1,0:T(8,128)(2,1)S(1)} %get-tuple-element.11), channel_id=1, source_target_pairs={{0,4},{4,8},{8,12},{12,16},{16,20},{20,24},{24,28},{1,5},{5,9},{9,... | collective-permute-start | bytes 245768 | tf_op jit(solution)/shard_map/ppermute | solution.py:24
  56.7 6.5 %collective-permute-start.1 = (bf16[8,20,256]{2,1,0:T(8,128)(2,1)S(1)}, bf16[8,20,256]{2,1,0:T(8,128)(2,1)S(1)}, u32[]{:S(2)}, u32[]{:S(2)}) collective-permute-start(bf16[8,20,256]{2,1,0:T(8,128)(2,1)S(1)} %get-tuple-element.16), channel_id=1, source_target_pairs={{4,0},{8,4},{12,8},{16,12},{20,16},{24,20},{28,24},{5,1},{9,5},{13... | collective-permute-start | bytes 245768 | tf_op jit(solution)/shard_map/ppermute | solution.py:26
  77.2 2.2 %slice-start.3 = ((s8[5242880]{0:T(1024)(128)(4,1)}), s8[4194304]{0:T(1024)(128)(4,1)S(1)}, s32[]{:S(2)}) async-start(s8[5242880]{0:T(1024)(128)(4,1)} %bitcast.271), calls=%async_computation.5 | async-start | bytes 8388608
  78.3 1.6 %slice-start.4 = ((s8[5242880]{0:T(1024)(128)(4,1)}), s8[1048576]{0:T(1024)(128)(4,1)S(1)}, s32[]{:S(2)}) async-start(s8[5242880]{0:T(1024)(128)(4,1)} %bitcast.271), calls=%async_computation.6 | async-start | bytes 2097152
  78.9 3.5 %slice-start = ((s8[12582912]{0:T(1024)(128)(4,1)}), s8[4194304]{0:T(1024)(128)(4,1)S(1)}, s32[]{:S(2)}) async-start(s8[12582912]{0:T(1024)(128)(4,1)} %bitcast.268), calls=%async_computation.2 | async-start | bytes 8388608
  79.9 2.6 %slice-start.1 = ((s8[12582912]{0:T(1024)(128)(4,1)}), s8[4194304]{0:T(1024)(128)(4,1)S(1)}, s32[]{:S(2)}) async-start(s8[12582912]{0:T(1024)(128)(4,1)} %bitcast.268), calls=%async_computation.3 | async-start | bytes 8388608
  79.9 3.7 %slice-start.2 = ((s8[12582912]{0:T(1024)(128)(4,1)}), s8[4194304]{0:T(1024)(128)(4,1)S(1)}, s32[]{:S(2)}) async-start(s8[12582912]{0:T(1024)(128)(4,1)} %bitcast.268), calls=%async_computation.4 | async-start | bytes 8388608
  92.2 13.7 %all-to-all-start.1 = ((bf16[8,64,256]{2,1,0:T(8,128)(2,1)}), bf16[8,64,256]{2,1,0:T(8,128)(2,1)S(1)}, u32[]{:S(2)}, u32[]{:S(2)}) async-start(bf16[8,64,256]{2,1,0:T(8,128)(2,1)} %copy.165), calls=%async_computation.1 | async-start | bytes 524288 | tf_op jit(solution)/shard_map/all_to_all | solution.py:126
where the time goes:
time: 107 us
  matrix products  32.3 us (30%)
  other arithmetic  24.8 us (23%)
  starting transfers between devices  18.2 us (17%)
  local copies, waits for them, and re-layouts  18.1 us (17%)
  waiting for transfers between devices  6.95 us (6%)
  blocking collectives  5.18 us (5%)
  between operations  1.09 us (1%)
    unnamed x55, local copies, waits for them, and re-layouts  12.2 us
    dot_general x1, matrix products, per_device(): jnp.einsum('kf,pk->fp', traces, shaped, preferred_element_type=jnp.float32)  7.92 us
    convert_element_type x1, other arithmetic, per_device(): jnp.where(inside[None, :, None], both_smooth, 0.0).astype(jnp.bfloat16)  7.38 us
    all_to_all x1, starting transfers between devices, per_device(): lax.all_to_all(movie, 'tile', split_axis=1, concat_axis=0, tiled=True)  7.28 us
    dot_general x1, matrix products, per_device(): jnp.einsum('pk,pq->kq', shaped, shaped, preferred_element_type=jnp.float32)  6.65 us
    mul x1, other arithmetic, per_device(): footprints * block_masks[:, None, :]  6.54 us
    dot_general x1, matrix products, per_device(): jnp.einsum('dk,kvx->dvx', counts, band, precision=lax.Precision.HIGHEST)  6.5 us
    add x1, other arithmetic, per_device(): row_smooth + taps_table[offset_step] * extended[:, offset_step:offset_ste...  6.47 us
  transfers between devices with their start and end apart: 4, of which 3 were waited for; matrix products, arithmetic and copies ran while one was open for 26% of the time, Pallas kernels for 0%

commit v1 on v0

v1 whole, which is shorter than its diff:
```python
import functools
import math

import jax
import jax.numpy as jnp
import numpy as np
from jax import lax
from jax.experimental import pallas as pl
from jax.experimental.pallas import tpu as pltpu
from jax.sharding import PartitionSpec as P

RR = 16
GR = 4
BR = 8
SWEEPS = 3
NR = 64
HALO = 24
LANES = 128
VMEM = pl.BlockSpec(memory_space=pltpu.VMEM)
SMEM = pl.BlockSpec(memory_space=pltpu.SMEM)


def split_high_low(values):
    high = values.astype(jnp.bfloat16)
    low = (values - high.astype(jnp.float32)).astype(jnp.bfloat16)
    return high, low


def filter_bands(tile_rows, columns):
    spots = np.arange(-GR, GR + 1).astype(np.float32)
    raw = np.exp(np.float32(-2.0) * spots * spots / np.float32(GR * GR)).astype(np.float32)
    taps = (raw / raw.sum(dtype=np.float32)).astype(np.float32)

    def band(count_out, count_in, shift):
        distance = np.arange(count_in)[None, :] - np.arange(count_out)[:, None] - shift
        inside = np.abs(distance) <= GR
        return np.where(inside, taps[np.clip(distance + GR, 0, 2 * GR)], np.float32(0.0))

    def parts(matrix):
        high = matrix.astype(jnp.bfloat16)
        low = (matrix - high.astype(np.float32)).astype(jnp.bfloat16)
        return high, low

    rows_high, rows_low = parts(band(tile_rows + 2 * RR, tile_rows + 2 * HALO, HALO - RR))
    cols_high, cols_low = parts(band(columns, columns, 0))
    return (
        jnp.asarray(np.concatenate([rows_high, rows_low], axis=1)),
        jnp.asarray(np.concatenate([cols_high, cols_high, cols_low], axis=0)),
    )


def border_tables(offsets_ref, table_ref, sides_ref):
    columns = table_ref.shape[1]
    tile_rows = sides_ref.shape[0] // 2
    places = lax.broadcasted_iota(jnp.int32, (8, columns), 0) * columns + lax.broadcasted_iota(
        jnp.int32, (8, columns), 1
    )
    base = jnp.zeros((8, columns), jnp.float32)
    for entry in range(offsets_ref.shape[1]):
        row = offsets_ref[0, entry]
        col = offsets_ref[1, entry]
        along_top = row == -RR
        along_row = along_top | (row == RR)
        first_lane = jnp.where(col > 0, columns - col, -col)
        kind = jnp.where(along_row, jnp.where(along_top, 0, 1), jnp.where(col < 0, 2, 3))
        lane = jnp.where(along_row, first_lane, row + RR)
        base = base + jnp.where(places == kind * columns + lane, 1.0, 0.0)
    distance = lax.broadcasted_iota(jnp.int32, (columns, columns), 0) - lax.broadcasted_iota(
        jnp.int32, (columns, columns), 1
    )
    near = jnp.abs(distance) <= RR
    for kind in range(2):
        spread = jnp.broadcast_to(base[kind : kind + 1, :], (columns, columns))
        turned = pltpu.roll(spread, 0, 1, stride=1, stride_axis=0)
        table_ref[kind * columns : (kind + 1) * columns, :] = jnp.where(near, turned, 0.0).astype(
            jnp.bfloat16
        )
    width = sides_ref.shape[1]
    for kind in range(2):
        spread = jnp.broadcast_to(base[2 + kind : 3 + kind, :width], (tile_rows, width))
        turned = pltpu.roll(spread, 0, 1, stride=1, stride_axis=0)
        sides_ref[kind * tile_rows : (kind + 1) * tile_rows, :] = turned.astype(jnp.bfloat16)


def kernel_components(
    footprints_ref,
    support_ref,
    traces_ref,
    offsets_ref,
    fitted_ref,
    edge_a_ref,
    edge_b_ref,
    coupling_ref,
    turned_ref,
    table_ref,
    sides_ref,
    lined_ref,
):
    tile_rows, columns, components = footprints_ref.shape
    frames = traces_ref.shape[0]
    halves = columns // LANES
    block = BR * columns
    split = components // 256 * 256
    traces = traces_ref[...]
    for b in range(tile_rows // BR):
        mask = support_ref[b : b + 1, :].astype(jnp.bfloat16)
        shaped = footprints_ref[b * BR : (b + 1) * BR].reshape(block, components) * mask
        turned_ref[:, b * block : (b + 1) * block] = shaped.T
        turned = turned_ref[:, b * block : (b + 1) * block]
        fitted = jnp.dot(traces, turned, preferred_element_type=jnp.float32)
        for row in range(BR):
            for half in range(halves):
                start = row * columns + half * LANES
                lined_ref[half, pl.ds(b * BR + row, frames, stride=tile_rows), :] = fitted[
                    :, start : start + LANES
                ]
        left = jnp.dot(turned, shaped[:, :split], preferred_element_type=jnp.float32)
        right = jnp.dot(turned[split:], shaped[:, split:], preferred_element_type=jnp.float32)
        if b == 0:
            coupling_ref[:, :split] = left
            coupling_ref[split:, split:] = right
        else:
            coupling_ref[:, :split] += left
            coupling_ref[split:, split:] += right
    coupling_ref[:split, split:] = coupling_ref[split:, :split].T
    odd = lax.axis_index("tile") % 2 == 1
    for half in range(halves):
        lanes = slice(half * LANES, (half + 1) * LANES)
        for frame in range(frames):
            lines = lined_ref[half, frame * tile_rows : (frame + 1) * tile_rows, :]
            fitted_ref[frame, :, lanes] = lines
            top = lines[:HALO]
            bottom = lines[tile_rows - HALO :]
            edge_a_ref[frame, :, lanes] = jnp.where(odd, top, bottom).astype(jnp.bfloat16)
            edge_b_ref[frame, :, lanes] = jnp.where(odd, bottom, top).astype(jnp.bfloat16)
    border_tables(offsets_ref, table_ref, sides_ref)


def kernel_frames(
    tile_count,
    movie_ref,
    fitted_ref,
    edge_a_ref,
    edge_b_ref,
    footprints_ref,
    support_ref,
    traces_ref,
    weight_ref,
    coupling_ref,
    turned_ref,
    table_ref,
    sides_ref,
    row_filter_ref,
    col_filter_ref,
    new_traces_ref,
    rounded_ref,
    remainder_ref,
    cleaned_ref,
    refit_ref,
):
    tile_rows, columns, components = footprints_ref.shape
    frames = traces_ref.shape[0]
    halves = columns // LANES
    span = tile_rows + 2 * RR
    tile = lax.axis_index("tile")
    odd = tile % 2 == 1

    row_number = tile * tile_rows - RR + lax.broadcasted_iota(jnp.int32, (span, 1), 0)
    inside = (row_number >= 0) & (row_number < tile_count * tile_rows)
    row_filter = jnp.where(inside, row_filter_ref[...].astype(jnp.float32), 0.0).astype(
        jnp.bfloat16
    )
    tall = []
    for frame in range(frames):
        edge_a = edge_a_ref[frame].astype(jnp.float32)
        edge_b = edge_b_ref[frame].astype(jnp.float32)
        fitted = jnp.concatenate(
            [
                jnp.where(odd, edge_a, edge_b),
                fitted_ref[frame],
                jnp.where(odd, edge_b, edge_a),
            ],
            axis=0,
        )
        first = (movie_ref[frame].astype(jnp.float32) - fitted).astype(jnp.bfloat16)
        tall.append(
            jnp.dot(
                row_filter,
                jnp.concatenate([first, first], axis=0),
                preferred_element_type=jnp.float32,
            )
        )
    high, low = split_high_low(jnp.concatenate(tall, axis=0))
    smooth = jnp.dot(
        jnp.concatenate([high, low, high], axis=1),
        col_filter_ref[...],
        preferred_element_type=jnp.float32,
    ).astype(jnp.bfloat16)
    sides = sides_ref[:, :span]
    lane = lax.broadcasted_iota(jnp.int32, (tile_rows, columns), 1)
    weight = weight_ref[...]
    for frame in range(frames):
        lines = smooth[frame * span : (frame + 1) * span]
        ends = jnp.concatenate([lines[:tile_rows], lines[2 * RR :]], axis=1)
        summed = jnp.dot(ends, table_ref[...], preferred_element_type=jnp.float32)
        mixed = jnp.dot(sides, lines, preferred_element_type=jnp.float32)
        west = pltpu.roll(mixed[:tile_rows], RR, 1)
        east = pltpu.roll(mixed[tile_rows:], columns - RR, 1)
        summed = summed + jnp.where(lane >= RR, west, 0.0)
        summed = summed + jnp.where(lane < columns - RR, east, 0.0)
        background = weight * summed * (1.0 / math.sqrt(NR))
        movie = movie_ref[frame, HALO : HALO + tile_rows, :].astype(jnp.float32)
        cleaned = (movie - background).astype(jnp.bfloat16).astype(jnp.float32)
        for half in range(halves):
            cleaned_ref[half, frame * tile_rows : (frame + 1) * tile_rows, :] = cleaned[
                :, half * LANES : (half + 1) * LANES
            ]

    projected = jnp.zeros((frames, components), jnp.float32)
    for b in range(tile_rows // BR):
        part = jnp.zeros((frames, components), jnp.float32)
        for row in range(b * BR, (b + 1) * BR):
            pixels = jnp.concatenate(
                [
                    cleaned_ref[half, pl.ds(row, frames, stride=tile_rows), :]
                    for half in range(halves)
                ],
                axis=1,
            ).astype(jnp.bfloat16)
            part = part + jnp.dot(
                pixels, footprints_ref[row], preferred_element_type=jnp.float32
            )
        projected = projected + part * support_ref[b : b + 1, :].astype(jnp.float32)

    coupling = coupling_ref[...]
    diagonal = lax.broadcasted_iota(jnp.int32, coupling.shape, 0) == lax.broadcasted_iota(
        jnp.int32, coupling.shape, 1
    )
    floor = jnp.maximum(
        jnp.sum(jnp.where(diagonal, coupling, 0.0), axis=0, keepdims=True), 1.0
    )
    coupling_high, coupling_low = split_high_low(coupling)
    state = traces_ref[...].astype(jnp.float32)
    for _ in range(SWEEPS):
        state_high, state_low = split_high_low(state)
        by_high = jnp.dot(
            jnp.concatenate([state_high, state_low], axis=0),
            coupling_high,
            preferred_element_type=jnp.float32,
        )
        by_low = jnp.dot(state_high, coupling_low, preferred_element_type=jnp.float32)
        moved = by_high[:frames] + (by_high[frames:] + by_low)
        state = jnp.maximum(state + (projected - moved) / floor, 0.0)
    rounded = state.astype(jnp.bfloat16)
    new_traces_ref[...] = state
    rounded_ref[...] = rounded

    block = BR * columns
    for b in range(tile_rows // BR):
        refit = jnp.dot(
            rounded,
            turned_ref[:, b * block : (b + 1) * block],
            preferred_element_type=jnp.float32,
        )
        for row in range(BR):
            for half in range(halves):
                start = row * columns + half * LANES
                refit_ref[half, pl.ds(b * BR + row, frames, stride=tile_rows), :] = refit[
                    :, start : start + LANES
                ]
    for frame in range(frames):
        rows = slice(frame * tile_rows, (frame + 1) * tile_rows)
        for half in range(halves):
            remainder_ref[frame, :, half * LANES : (half + 1) * LANES] = (
                cleaned_ref[half, rows, :] - refit_ref[half, rows, :]
            ).astype(jnp.bfloat16)


def per_device(movie, footprints, support, traces, border_weight, border_offsets):
    tile_count = lax.axis_size("tile")
    tile_rows, columns, components = footprints.shape
    own_frames = movie.shape[0]
    frames = own_frames * tile_count
    pixels = tile_rows * columns
    halves = columns // LANES
    span = tile_rows + 2 * RR
    extended = tile_rows + 2 * HALO

    padded = jnp.pad(movie, ((0, 0), (HALO, HALO), (0, 0)))
    pieces = jnp.concatenate(
        [
            lax.slice_in_dim(padded, t * tile_rows, t * tile_rows + extended, axis=1)
            for t in range(tile_count)
        ],
        axis=0,
    )
    strip_movie = lax.all_to_all(pieces, "tile", split_axis=0, concat_axis=0, tiled=True)

    traces_rows = traces.T
    fitted, edge_a, edge_b, coupling, turned, table, sides = pl.pallas_call(
        kernel_components,
        out_shape=[
            jax.ShapeDtypeStruct((frames, tile_rows, columns), jnp.float32),
            jax.ShapeDtypeStruct((frames, HALO, columns), jnp.bfloat16),
            jax.ShapeDtypeStruct((frames, HALO, columns), jnp.bfloat16),
            jax.ShapeDtypeStruct((components, components), jnp.float32),
            jax.ShapeDtypeStruct((components, pixels), jnp.bfloat16),
            jax.ShapeDtypeStruct((2 * columns, columns), jnp.bfloat16),
            jax.ShapeDtypeStruct((2 * tile_rows, LANES), jnp.bfloat16),
        ],
        in_specs=[VMEM, VMEM, VMEM, SMEM],
        out_specs=[VMEM] * 7,
        scratch_shapes=[pltpu.VMEM((halves, frames * tile_rows, LANES), jnp.float32)],
        compiler_params=pltpu.CompilerParams(vmem_limit_bytes=12 << 20),
        cost_estimate=pl.CostEstimate(
            flops=2 * pixels * components * components,
            bytes_accessed=4 * pixels * components,
            transcendentals=0,
        ),
        name="components",
    )(footprints, support, traces_rows, border_offsets.T)

    evens = [(i, i + 1) for i in range(0, tile_count - 1, 2)]
    odds = [(i, i + 1) for i in range(1, tile_count - 1, 2)]
    edge_a = lax.ppermute(edge_a, "tile", evens + [(j, i) for i, j in evens])
    edge_b = lax.ppermute(edge_b, "tile", odds + [(j, i) for i, j in odds])

    row_filter, col_filter = filter_bands(tile_rows, columns)
    new_traces, rounded, leftover = pl.pallas_call(
        functools.partial(kernel_frames, tile_count),
        out_shape=[
            jax.ShapeDtypeStruct((frames, components), jnp.float32),
            jax.ShapeDtypeStruct((frames, components), jnp.bfloat16),
            jax.ShapeDtypeStruct((frames, tile_rows, columns), jnp.bfloat16),
        ],
        in_specs=[VMEM] * 14,
        out_specs=[VMEM] * 3,
        scratch_shapes=[pltpu.VMEM((halves, frames * tile_rows, LANES), jnp.float32)] * 2,
        compiler_params=pltpu.CompilerParams(vmem_limit_bytes=16 << 20),
        cost_estimate=pl.CostEstimate(
            flops=8 * frames * pixels * components,
            bytes_accessed=4 * pixels * components,
            transcendentals=0,
        ),
        name="frames",
    )(
        strip_movie,
        fitted,
        edge_a,
        edge_b,
        footprints,
        support,
        traces_rows,
        border_weight,
        coupling,
        turned,
        table,
        sides,
        row_filter,
        col_filter,
    )

    remainder = lax.all_to_all(leftover, "tile", split_axis=0, concat_axis=0, tiled=True)
    remainder = (
        remainder.reshape(tile_count, own_frames, tile_rows, columns)
        .transpose(1, 0, 2, 3)
        .reshape(own_frames, tile_count * tile_rows, columns)
    )
    all_traces = lax.all_gather(rounded, "frame", axis=0, tiled=True)
    trace_gram = lax.dot_general(
        all_traces, all_traces, (((0,), (0,)), ((), ())), preferred_element_type=jnp.float32
    )
    return (new_traces.T, trace_gram, remainder)


def solution(mesh):
    return jax.shard_map(
        per_device,
        mesh=mesh,
        in_specs=(
            P(("frame", "tile"), None, None),
            P("tile", None, None),
            P("tile", None),
            P("tile", "frame"),
            P("tile", None),
            P(),
        ),
        out_specs=(P("tile", "frame"), P("tile", None), P(("frame", "tile"), None, None)),
        check_vma=False,
    )
```

time: 107 us -> 77.7 us (0.73)
  matrix products: 32.3 us -> 1.07 us
  other arithmetic: 24.8 us -> 0 us
  local copies, waits for them, and re-layouts: 18.1 us -> 32.6 us
  Pallas kernels: 0 us -> 14 us
  waiting for transfers between devices: 6.95 us -> 3.73 us
  starting transfers between devices: 18.2 us -> 19.5 us
    dot_general x11 -> x1, matrix products: 32.3 us -> 1.07 us  [per_device(): lax.dot_general(all_traces, all_traces, (((0,), (0,)), ((), ())), preferr...]
    unnamed x55 -> x32, local copies, waits for them, and re-layouts: 12.2 us -> 31.2 us
    pallas_call x0 -> x2, Pallas kernels: none -> 14 us  [the longest x1 7.59 us: per_device(): pl.pallas_call(kernel_components, out_shape=[jax.ShapeDtypeStruct((frames...]
    convert_element_type x4 -> x0, other arithmetic: 8.22 us -> none  [the longest x1 7.38 us: per_device(): jnp.where(inside[None, :, None], both_smooth, 0.0).astype(jnp.bfloat16)]
    mul x1 -> x0, other arithmetic: 6.54 us -> none  [per_device(): footprints * block_masks[:, None, :]]
    add x2 -> x0, other arithmetic: 6.48 us -> none  [the longest x1 6.47 us: per_device(): row_smooth + taps_table[offset_step] * extended[:, offset_step:offset_ste...]
    all_to_all x2, starting transfers between devices: 12.7 us -> 16.6 us  [the longest x1 9.33 us: per_device(): lax.all_to_all(leftover, 'tile', split_axis=0, concat_axis=0, tiled=True)]
    gather x1 -> x0, local copies, waits for them, and re-layouts: 3.45 us -> none  [per_device(): floor_t = jnp.maximum(jnp.diagonal(coupling), 1.0)]
  transfers between devices with their start and end apart: 4 -> 4, of which waited for: 3 -> 2; matrix products, arithmetic and copies ran while one was open for 26% -> 1% of each run, Pallas kernels for 0% -> 10%
where the time goes in v1:
time: 77.7 us; the launch traced here: 76.8 us
  local copies, waits for them, and re-layouts  32.6 us (42%)
  starting transfers between devices  19.5 us (25%)
  Pallas kernels  14 us (18%)
  blocking collectives  5.18 us (7%)
  waiting for transfers between devices  3.73 us (5%)
  matrix products  1.07 us (1%)
    unnamed x32, local copies, waits for them, and re-layouts  31.2 us
    all_to_all x1, starting transfers between devices, per_device(): lax.all_to_all(leftover, 'tile', split_axis=0, concat_axis=0, tiled=True)  9.33 us
    pallas_call x1, Pallas kernels, per_device(): pl.pallas_call(kernel_components, out_shape=[jax.ShapeDtypeStruct((frames...  7.59 us
    all_to_all x1, starting transfers between devices, per_device(): lax.all_to_all(pieces, 'tile', split_axis=0, concat_axis=0, tiled=True)  7.28 us
    pallas_call x1, Pallas kernels, per_device(): pl.pallas_call(functools.partial(kernel_frames, tile_count), out_shape=[j...  6.41 us
    all_gather x1, blocking collectives, per_device(): all_traces = lax.all_gather(rounded, 'frame', axis=0, tiled=True)  5.18 us
    ppermute x1, starting transfers between devices, per_device(): edge_a = lax.ppermute(edge_a, 'tile', evens + [(j, i) for i, j in evens])  2.02 us
    all_to_all x1, waiting for transfers between devices, per_device(): lax.all_to_all(leftover, 'tile', split_axis=0, concat_axis=0, tiled=True)  1.97 us
  transfers between devices with their start and end apart: 4, of which 2 were waited for; matrix products, arithmetic and copies ran while one was open for 1% of the time, Pallas kernels for 10%

profile of v1, /device:TPU:0, one launch (start us, length us, event | category | flops | bytes accessed | tf_op | source)
XLA Modules:
  0.0 76.8 jit_solution(17222374219350074373)
XLA Ops:
  0.7 1.5 %fusion = bf16[8,112,256]{2,1,0:T(8,128)(2,1)} fusion(bf16[1,512,256]{2,1,0:T(8,128)(2,1)} %param.8), kind=kLoop, calls=%fused_computation.2 | loop fusion | bytes 319488
  2.1 1.4 %slice_dynamic-update-slice_fusion.5 = bf16[8,112,256]{2,1,0:T(8,128)(2,1)} fusion(bf16[8,112,256]{2,1,0:T(8,128)(2,1)} %fusion, bf16[1,512,256]{2,1,0:T(8,128)(2,1)} %param.8), kind=kLoop, calls=%fused_computation.9 | loop fusion | bytes 114688
  3.6 1.4 %slice_dynamic-update-slice_fusion.4 = bf16[8,112,256]{2,1,0:T(8,128)(2,1)} fusion(bf16[8,112,256]{2,1,0:T(8,128)(2,1)} %slice_dynamic-update-slice_fusion.5, bf16[1,512,256]{2,1,0:T(8,128)(2,1)} %param.8), kind=kLoop, calls=%fused_computation.8 | loop fusion | bytes 114688
  5.0 1.4 %slice_dynamic-update-slice_fusion.3 = bf16[8,112,256]{2,1,0:T(8,128)(2,1)} fusion(bf16[8,112,256]{2,1,0:T(8,128)(2,1)} %slice_dynamic-update-slice_fusion.4, bf16[1,512,256]{2,1,0:T(8,128)(2,1)} %param.8), kind=kLoop, calls=%fused_computation.7 | loop fusion | bytes 114688
  6.5 1.4 %slice_dynamic-update-slice_fusion.2 = bf16[8,112,256]{2,1,0:T(8,128)(2,1)} fusion(bf16[8,112,256]{2,1,0:T(8,128)(2,1)} %slice_dynamic-update-slice_fusion.3, bf16[1,512,256]{2,1,0:T(8,128)(2,1)} %param.8), kind=kLoop, calls=%fused_computation.6 | loop fusion | bytes 114688
  7.9 1.4 %slice_dynamic-update-slice_fusion.1 = bf16[8,112,256]{2,1,0:T(8,128)(2,1)} fusion(bf16[8,112,256]{2,1,0:T(8,128)(2,1)} %slice_dynamic-update-slice_fusion.2, bf16[1,512,256]{2,1,0:T(8,128)(2,1)} %param.8), kind=kLoop, calls=%fused_computation.5 | loop fusion | bytes 114688
  9.4 1.4 %slice_dynamic-update-slice_fusion = bf16[8,112,256]{2,1,0:T(8,128)(2,1)} fusion(bf16[8,112,256]{2,1,0:T(8,128)(2,1)} %slice_dynamic-update-slice_fusion.1, bf16[1,512,256]{2,1,0:T(8,128)(2,1)} %param.8), kind=kLoop, calls=%fused_computation.4 | loop fusion | bytes 114688
  10.8 1.4 %fusion.1 = bf16[8,112,256]{2,1,0:T(8,128)(2,1)} fusion(bf16[8,112,256]{2,1,0:T(8,128)(2,1)} %slice_dynamic-update-slice_fusion, bf16[1,512,256]{2,1,0:T(8,128)(2,1)} %param.8), kind=kLoop, calls=%fused_computation.3 | loop fusion | bytes 319488 | tf_op jit(solution)/shard_map/concatenate | solution.py:290
  12.2 7.3 %all-to-all-start = ((bf16[8,112,256]{2,1,0:T(8,128)(2,1)}), bf16[8,112,256]{2,1,0:T(8,128)(2,1)S(1)}, u32[]{:S(2)}, u32[]{:S(2)}) async-start(bf16[8,112,256]{2,1,0:T(8,128)(2,1)} %fusion.1), calls=%async_computation | async-start | bytes 917504 | tf_op jit(solution)/shard_map/all_to_all | solution.py:297
  19.5 4.6 %copy-done = bf16[64,256,384]{2,1,0:T(8,128)(2,1)S(1)} copy-done((bf16[64,256,384]{2,1,0:T(8,128)(2,1)S(1)}, bf16[64,256,384]{2,1,0:T(8,128)(2,1)}, u32[]{:S(2)}) %copy-start) | copy-done | bytes 12582936
  24.1 0.7 copy-done.7
  26.2 7.6 %components.1 = (f32[8,64,256]{2,1,0:T(8,128)S(1)}, bf16[8,24,256]{2,1,0:T(8,128)(2,1)S(1)}, bf16[8,24,256]{2,1,0:T(8,128)(2,1)S(1)}, f32[384,384]{1,0:T(8,128)S...) custom-call(bf16[64,256,384]{2,1,0:T(8,128)(2,1)S(1)} %copy-done, ...), custom_call_target="tpu_custom_call" | custom-call | flops 4831838208 | bytes 25165824 | tf_op jit(solution)/shard_map/components/pallas_call | solution.py:300
  33.8 4.5 %copy-done.2 = bf16[384,16384]{1,0:T(8,128)(2,1)} copy-done((bf16[384,16384]{1,0:T(8,128)(2,1)}, bf16[384,16384]{1,0:T(8,128)(2,1)S(1)}, u32[]{:S(2)}) %copy-start.2) | copy-done | bytes 12582936
  38.3 2.0 %collective-permute-start = (bf16[8,24,256]{2,1,0:T(8,128)(2,1)S(1)}, bf16[8,24,256]{2,1,0:T(8,128)(2,1)S(1)}, u32[]{:S(2)}, u32[]{:S(2)}) collective-permute-start(bf16[8,24,256]{2,1,0:T(8,128)(2,1)S(1)} %get-tuple-element.14), channel_id=1, source_target_pairs={{0,4},{8,12},{16,20},{24,28},{4,0},{12,8},{20,16},{28,24},{1,5},{9... | collective-permute-start | bytes 294920 | tf_op jit(solution)/shard_map/ppermute | solution.py:325
  40.3 0.8 %collective-permute-start.1 = (bf16[8,24,256]{2,1,0:T(8,128)(2,1)S(1)}, bf16[8,24,256]{2,1,0:T(8,128)(2,1)S(1)}, u32[]{:S(2)}, u32[]{:S(2)}) collective-permute-start(bf16[8,24,256]{2,1,0:T(8,128)(2,1)S(1)} %get-tuple-element.15), channel_id=1, source_target_pairs={{4,8},{12,16},{20,24},{8,4},{16,12},{24,20},{5,9},{13,17},{21,25},... | collective-permute-start | bytes 294920 | tf_op jit(solution)/shard_map/ppermute | solution.py:326
  41.2 1.8 %collective-permute-done.edge_a_ref = bf16[8,24,256]{2,1,0:T(8,128)(2,1)S(1)} collective-permute-done((bf16[8,24,256]{2,1,0:T(8,128)(2,1)S(1)}, bf16[8,24,256]{2,1,0:T(8,128)(2,1)S(1)}, u32[]{:S(2)}, u32[]{:S(2)}) %collective-permute-start) | collective-permute-done | bytes 98336 | tf_op jit(solution)/shard_map/ppermute | solution.py:325
  43.0 4.6 %copy-done.1 = bf16[64,256,384]{2,1,0:T(8,128)(2,1)S(1)} copy-done((bf16[64,256,384]{2,1,0:T(8,128)(2,1)S(1)}, bf16[64,256,384]{2,1,0:T(8,128)(2,1)}, u32[]{:S(2)}) %copy-start.1) | copy-done | bytes 12582936
  47.5 4.6 %copy-done.3 = bf16[384,16384]{1,0:T(8,128)(2,1)S(1)} copy-done((bf16[384,16384]{1,0:T(8,128)(2,1)S(1)}, bf16[384,16384]{1,0:T(8,128)(2,1)}, u32[]{:S(2)}) %copy-start.3) | copy-done | bytes 12582936
  52.1 6.4 %frames.1 = (f32[8,384]{1,0:T(8,128)}, bf16[8,384]{1,0:T(8,128)(2,1)S(1)}, bf16[8,64,256]{2,1,0:T(8,128)(2,1)}) custom-call(bf16[8,112,256]{2,1,0:T(8,128)(2,1)S(1)} %all-to-all-done.movie_ref, f32[8,64,256]{2,1,0:T(8,128)S(1)} %get-tuple-element.13.fitted_ref, bf16[8,24,256]{2,1,0:T(8,128)(2,1)S(1)} %collective-permute-done.edge_a_ref, ...), custom_call_target="tpu_custom_call" | custom-call | flops 402653184 | bytes 25165824 | tf_op jit(solution)/shard_map/frames/pallas_call | solution.py:329
  58.5 9.3 %all-to-all-start.1 = ((bf16[8,64,256]{2,1,0:T(8,128)(2,1)}), bf16[8,64,256]{2,1,0:T(8,128)(2,1)S(1)}, u32[]{:S(2)}, u32[]{:S(2)}) async-start(bf16[8,64,256]{2,1,0:T(8,128)(2,1)} %get-tuple-element.22), calls=%async_computation.1 | async-start | bytes 524288 | tf_op jit(solution)/shard_map/all_to_all | solution.py:363
  67.9 5.2 %all_gather.3 = bf16[32,384]{1,0:T(8,128)(2,1)S(1)} all-gather(bf16[8,384]{1,0:T(8,128)(2,1)S(1)} %get-tuple-element.21), channel_id=1, replica_groups=mesh['tile'=8,'frame'=4] {'frame'}, dimensions={0}, use_global_device_ids=true | all-gather | bytes 30720 | tf_op jit(solution)/shard_map/all_gather | solution.py:369
  73.0 1.1 %fusion.2 = f32[384,384]{1,0:T(8,128)} fusion(bf16[32,384]{1,0:T(8,128)(2,1)S(1)} %all_gather.3), kind=kOutput, calls=%fused_computation.10 | convolution fusion | flops 9437184 | bytes 614400 | tf_op jit(solution)/shard_map/dot_general | solution.py:370
  74.1 2.0 %all-to-all-done.1 = bf16[8,64,256]{2,1,0:T(8,128)(2,1)S(1)} async-done(((bf16[8,64,256]{2,1,0:T(8,128)(2,1)}), bf16[8,64,256]{2,1,0:T(8,128)(2,1)S(1)}, u32[]{:S(2)}, u32[]{:S(2)}) %all-to-all-start.1) | async-done | bytes 262176 | tf_op jit(solution)/shard_map/all_to_all | solution.py:363
  76.1 0.7 copy.19
  (21 shorter events, 1.4 us)
Async XLA Ops:
  0.6 42.3 %copy-start.4 = (bf16[768,256]{1,0:T(8,128)(2,1)S(1)}, bf16[768,256]{1,0:T(8,128)(2,1)}, u32[]{:S(2)}) copy-start(bf16[768,256]{1,0:T(8,128)(2,1)} %constant.8.clone.col_filter_ref) | copy-start | bytes 1179652
  0.6 42.3 %copy-start.6 = (bf16[96,224]{1,0:T(8,128)(2,1)S(1)}, bf16[96,224]{1,0:T(8,128)(2,1)}, u32[]{:S(2)}) copy-start(bf16[96,224]{1,0:T(8,128)(2,1)} %constant.7.clone.row_filter_ref) | copy-start | bytes 129028
  0.7 42.3 %copy-start.8 = (s32[8,384]{1,0:T(8,128)S(1)}, s32[8,384]{1,0:T(8,128)}, u32[]{:S(2)}) copy-start(s32[8,384]{1,0:T(8,128)} %support_ref.3) | copy-start | bytes 36868
  0.7 42.3 %copy-start.10 = (bf16[384,8]{0,1:T(8,128)(2,1)S(1)}, bf16[384,8]{0,1:T(8,128)(2,1)}, u32[]{:S(2)}) copy-start(bf16[384,8]{0,1:T(8,128)(2,1)} %param.11) | copy-start | bytes 18436
  0.7 42.3 %copy-start.5 = (f32[64,256]{1,0:T(8,128)S(1)}, f32[64,256]{1,0:T(8,128)}, u32[]{:S(2)}) copy-start(f32[64,256]{1,0:T(8,128)} %weight_ref.1) | copy-start | bytes 196612
  12.2 30.7 %all-to-all-start = ((bf16[8,112,256]{2,1,0:T(8,128)(2,1)}), bf16[8,112,256]{2,1,0:T(8,128)(2,1)S(1)}, u32[]{:S(2)}, u32[]{:S(2)}) async-start(bf16[8,112,256]{2,1,0:T(8,128)(2,1)} %fusion.1), calls=%async_computation | async-start | bytes 917504 | tf_op jit(solution)/shard_map/all_to_all | solution.py:297
  19.5 4.6 %copy-start = (bf16[64,256,384]{2,1,0:T(8,128)(2,1)S(1)}, bf16[64,256,384]{2,1,0:T(8,128)(2,1)}, u32[]{:S(2)}) copy-start(bf16[64,256,384]{2,1,0:T(8,128)(2,1)} %footprints_ref.3) | copy-start | bytes 37748740
  24.1 0.7 copy-start.7
  24.8 0.7 copy-start.9
  25.5 0.7 copy-start.11
  33.8 4.5 %copy-start.2 = (bf16[384,16384]{1,0:T(8,128)(2,1)}, bf16[384,16384]{1,0:T(8,128)(2,1)S(1)}, u32[]{:S(2)}) copy-start(bf16[384,16384]{1,0:T(8,128)(2,1)S(1)} %get-tuple-element.17.turned_ref) | copy-start | bytes 37748740
  38.3 4.6 %collective-permute-start = (bf16[8,24,256]{2,1,0:T(8,128)(2,1)S(1)}, bf16[8,24,256]{2,1,0:T(8,128)(2,1)S(1)}, u32[]{:S(2)}, u32[]{:S(2)}) collective-permute-start(bf16[8,24,256]{2,1,0:T(8,128)(2,1)S(1)} %get-tuple-element.14), channel_id=1, source_target_pairs={{0,4},{8,12},{16,20},{24,28},{4,0},{12,8},{20,16},{28,24},{1,5},{9... | collective-permute-start | bytes 294920 | tf_op jit(solution)/shard_map/ppermute | solution.py:325
  40.3 2.6 %collective-permute-start.1 = (bf16[8,24,256]{2,1,0:T(8,128)(2,1)S(1)}, bf16[8,24,256]{2,1,0:T(8,128)(2,1)S(1)}, u32[]{:S(2)}, u32[]{:S(2)}) collective-permute-start(bf16[8,24,256]{2,1,0:T(8,128)(2,1)S(1)} %get-tuple-element.15), channel_id=1, source_target_pairs={{4,8},{12,16},{20,24},{8,4},{16,12},{24,20},{5,9},{13,17},{21,25},... | collective-permute-start | bytes 294920 | tf_op jit(solution)/shard_map/ppermute | solution.py:326
  43.0 4.6 %copy-start.1 = (bf16[64,256,384]{2,1,0:T(8,128)(2,1)S(1)}, bf16[64,256,384]{2,1,0:T(8,128)(2,1)}, u32[]{:S(2)}) copy-start(bf16[64,256,384]{2,1,0:T(8,128)(2,1)} %footprints_ref.3) | copy-start | bytes 37748740
  47.5 4.6 %copy-start.3 = (bf16[384,16384]{1,0:T(8,128)(2,1)S(1)}, bf16[384,16384]{1,0:T(8,128)(2,1)}, u32[]{:S(2)}) copy-start(bf16[384,16384]{1,0:T(8,128)(2,1)} %copy-done.2) | copy-start | bytes 37748740
  58.5 17.6 %all-to-all-start.1 = ((bf16[8,64,256]{2,1,0:T(8,128)(2,1)}), bf16[8,64,256]{2,1,0:T(8,128)(2,1)S(1)}, u32[]{:S(2)}, u32[]{:S(2)}) async-start(bf16[8,64,256]{2,1,0:T(8,128)(2,1)} %get-tuple-element.22), calls=%async_computation.1 | async-start | bytes 524288 | tf_op jit(solution)/shard_map/all_to_all | solution.py:363

commit v2 on v1

--- a/solution.py
+++ b/solution.py
@@ -17,7 +17,7 @@
 HALO = 24
 LANES = 128
 VMEM = pl.BlockSpec(memory_space=pltpu.VMEM)
-SMEM = pl.BlockSpec(memory_space=pltpu.SMEM)
+ANY = pl.BlockSpec(memory_space=pl.ANY)
 
 
 def split_high_low(values):
@@ -49,64 +49,117 @@
     )
 
 
-def border_tables(offsets_ref, table_ref, sides_ref):
+def border_tables(offsets, table_ref, sides_ref):
     columns = table_ref.shape[1]
     tile_rows = sides_ref.shape[0] // 2
-    places = lax.broadcasted_iota(jnp.int32, (8, columns), 0) * columns + lax.broadcasted_iota(
-        jnp.int32, (8, columns), 1
-    )
-    base = jnp.zeros((8, columns), jnp.float32)
-    for entry in range(offsets_ref.shape[1]):
-        row = offsets_ref[0, entry]
-        col = offsets_ref[1, entry]
-        along_top = row == -RR
-        along_row = along_top | (row == RR)
-        first_lane = jnp.where(col > 0, columns - col, -col)
-        kind = jnp.where(along_row, jnp.where(along_top, 0, 1), jnp.where(col < 0, 2, 3))
-        lane = jnp.where(along_row, first_lane, row + RR)
-        base = base + jnp.where(places == kind * columns + lane, 1.0, 0.0)
+    row = offsets[0:1, :]
+    col = offsets[1:2, :]
+    count = row.shape[1]
+    along_top = row == -RR
+    along_row = along_top | (row == RR)
+    turned_lane = jnp.where(col > 0, columns - col, -col)
+    kind = jnp.where(along_row, jnp.where(along_top, 0, 1), jnp.where(col < 0, 2, 3))
+    lane = jnp.where(along_row, turned_lane, row + RR)
+    kind_hot = jnp.where(kind == lax.broadcasted_iota(jnp.int32, (8, count), 0), 1.0, 0.0)
+    lane_hot = jnp.where(lane == lax.broadcasted_iota(jnp.int32, (columns, count), 0), 1.0, 0.0)
+    base = lax.dot_general(
+        kind_hot.astype(jnp.bfloat16),
+        lane_hot.astype(jnp.bfloat16),
+        (((1,), (1,)), ((), ())),
+        preferred_element_type=jnp.float32,
+    )
     distance = lax.broadcasted_iota(jnp.int32, (columns, columns), 0) - lax.broadcasted_iota(
         jnp.int32, (columns, columns), 1
     )
     near = jnp.abs(distance) <= RR
-    for kind in range(2):
-        spread = jnp.broadcast_to(base[kind : kind + 1, :], (columns, columns))
+    for kind_at in range(2):
+        spread = jnp.broadcast_to(base[kind_at : kind_at + 1, :], (columns, columns))
         turned = pltpu.roll(spread, 0, 1, stride=1, stride_axis=0)
-        table_ref[kind * columns : (kind + 1) * columns, :] = jnp.where(near, turned, 0.0).astype(
+        table_ref[kind_at * columns : (kind_at + 1) * columns, :] = jnp.where(
+            near, turned, 0.0
+        ).astype(jnp.bfloat16)
+    width = sides_ref.shape[1]
+    for kind_at in range(2):
+        spread = jnp.broadcast_to(base[2 + kind_at : 3 + kind_at, :width], (tile_rows, width))
+        turned = pltpu.roll(spread, 0, 1, stride=1, stride_axis=0)
+        sides_ref[kind_at * tile_rows : (kind_at + 1) * tile_rows, :] = turned.astype(
             jnp.bfloat16
         )
-    width = sides_ref.shape[1]
-    for kind in range(2):
-        spread = jnp.broadcast_to(base[2 + kind : 3 + kind, :width], (tile_rows, width))
-        turned = pltpu.roll(spread, 0, 1, stride=1, stride_axis=0)
-        sides_ref[kind * tile_rows : (kind + 1) * tile_rows, :] = turned.astype(jnp.bfloat16)
+
+
+def kernel_pieces(tile_rows, movie_ref, pieces_ref):
+    frames, image_rows, columns = movie_ref.shape
+    count = image_rows // tile_rows
+    for tile in range(count):
+        for frame in range(frames):
+            start = max(tile * tile_rows - HALO, 0)
+            stop = min((tile + 1) * tile_rows + HALO, image_rows)
+            rows = movie_ref[frame, start:stop, :]
+            blank = jnp.zeros((tile_rows + 2 * HALO - (stop - start), columns), movie_ref.dtype)
+            if tile == 0:
+                rows = jnp.concatenate([blank, rows], axis=0)
+            elif tile == count - 1:
+                rows = jnp.concatenate([rows, blank], axis=0)
+            pieces_ref[tile * frames + frame] = rows
+
+
+def start_footprints(footprints_hbm, footprints_ref, arrived):
+    copies = []
+    for b in range(footprints_ref.shape[0] // BR):
+        rows = pl.ds(b * BR, BR)
+        copies.append(
+            pltpu.make_async_copy(footprints_hbm.at[rows], footprints_ref.at[rows], arrived.at[b])
+        )
+        copies[-1].start()
+    return copies
 
 
 def kernel_components(
+    footprints_hbm,
+    support_hbm,
+    traces_hbm,
+    offsets_hbm,
+    fitted_ref,
+    edge_a_ref,
+    edge_b_ref,
+    coupling_ref,
+    table_ref,
+    sides_ref,
     footprints_ref,
     support_ref,
     traces_ref,
     offsets_ref,
-    fitted_ref,
-    edge_a_ref,
-    edge_b_ref,
-    coupling_ref,
-    turned_ref,
-    table_ref,
-    sides_ref,
     lined_ref,
+    arrived,
+    arrived_small,
 ):
+    small = [
+        pltpu.make_async_copy(source, target, arrived_small.at[i])
+        for i, (source, target) in enumerate(
+            [
+                (offsets_hbm, offsets_ref),
+                (support_hbm, support_ref),
+                (traces_hbm, traces_ref),
+            ]
+        )
+    ]
+    for copy in small:
+        copy.start()
+    copies = start_footprints(footprints_hbm, footprints_ref, arrived)
     tile_rows, columns, components = footprints_ref.shape
     frames = traces_ref.shape[0]
     halves = columns // LANES
     block = BR * columns
     split = components // 256 * 256
+    for copy in small:
+        copy.wait()
+    border_tables(offsets_ref[...], table_ref, sides_ref)
     traces = traces_ref[...]
     for b in range(tile_rows // BR):
+        copies[b].wait()
         mask = support_ref[b : b + 1, :].astype(jnp.bfloat16)
         shaped = footprints_ref[b * BR : (b + 1) * BR].reshape(block, components) * mask
-        turned_ref[:, b * block : (b + 1) * block] = shaped.T
-        turned = turned_ref[:, b * block : (b + 1) * block]
+        turned = shaped.T
         fitted = jnp.dot(traces, turned, preferred_element_type=jnp.float32)
         for row in range(BR):
             for half in range(halves):
@@ -133,7 +186,6 @@
             bottom = lines[tile_rows - HALO :]
             edge_a_ref[frame, :, lanes] = jnp.where(odd, top, bottom).astype(jnp.bfloat16)
             edge_b_ref[frame, :, lanes] = jnp.where(odd, bottom, top).astype(jnp.bfloat16)
-    border_tables(offsets_ref, table_ref, sides_ref)
 
 
 def kernel_frames(
@@ -142,12 +194,11 @@
     fitted_ref,
     edge_a_ref,
     edge_b_ref,
-    footprints_ref,
+    footprints_hbm,
     support_ref,
     traces_ref,
     weight_ref,
     coupling_ref,
-    turned_ref,
     table_ref,
     sides_ref,
     row_filter_ref,
@@ -157,7 +208,11 @@
     remainder_ref,
     cleaned_ref,
     refit_ref,
+    footprints_ref,
+    turned_ref,
+    arrived,
 ):
+    copies = start_footprints(footprints_hbm, footprints_ref, arrived)
     tile_rows, columns, components = footprints_ref.shape
     frames = traces_ref.shape[0]
     halves = columns // LANES
@@ -216,8 +271,15 @@
                 :, half * LANES : (half + 1) * LANES
             ]
 
+    block = BR * columns
     projected = jnp.zeros((frames, components), jnp.float32)
     for b in range(tile_rows // BR):
+        copies[b].wait()
+        mask = support_ref[b : b + 1, :]
+        shaped = footprints_ref[b * BR : (b + 1) * BR].reshape(
+            block, components
+        ) * mask.astype(jnp.bfloat16)
+        turned_ref[:, b * block : (b + 1) * block] = shaped.T
         part = jnp.zeros((frames, components), jnp.float32)
         for row in range(b * BR, (b + 1) * BR):
             pixels = jnp.concatenate(
@@ -230,7 +292,7 @@
             part = part + jnp.dot(
                 pixels, footprints_ref[row], preferred_element_type=jnp.float32
             )
-        projected = projected + part * support_ref[b : b + 1, :].astype(jnp.float32)
+        projected = projected + part * mask.astype(jnp.float32)
 
     coupling = coupling_ref[...]
     diagonal = lax.broadcasted_iota(jnp.int32, coupling.shape, 0) == lax.broadcasted_iota(
@@ -255,7 +317,6 @@
     new_traces_ref[...] = state
     rounded_ref[...] = rounded
 
-    block = BR * columns
     for b in range(tile_rows // BR):
         refit = jnp.dot(
             rounded,
@@ -276,6 +337,19 @@
             ).astype(jnp.bfloat16)
 
 
+def pairs(count, turn):
+    if count & (count - 1):
+        return [(i, (i + turn) % count) for i in range(count)]
+    return [(i, i ^ turn) for i in range(count)]
+
+
+def kernel_gram(*refs):
+    traces = jnp.concatenate([ref[...] for ref in refs[:-1]], axis=0)
+    refs[-1][...] = lax.dot_general(
+        traces, traces, (((0,), (0,)), ((), ())), preferred_element_type=jnp.float32
+    )
+
+
 def per_device(movie, footprints, support, traces, border_weight, border_offsets):
     tile_count = lax.axis_size("tile")
     tile_rows, columns, components = footprints.shape
@@ -283,35 +357,41 @@
     frames = own_frames * tile_count
     pixels = tile_rows * columns
     halves = columns // LANES
-    span = tile_rows + 2 * RR
     extended = tile_rows + 2 * HALO
-
-    padded = jnp.pad(movie, ((0, 0), (HALO, HALO), (0, 0)))
-    pieces = jnp.concatenate(
-        [
-            lax.slice_in_dim(padded, t * tile_rows, t * tile_rows + extended, axis=1)
-            for t in range(tile_count)
-        ],
-        axis=0,
-    )
+    lined = pltpu.VMEM((halves, frames * tile_rows, LANES), jnp.float32)
+
+    pieces = pl.pallas_call(
+        functools.partial(kernel_pieces, tile_rows),
+        out_shape=jax.ShapeDtypeStruct((frames, extended, columns), movie.dtype),
+        in_specs=[VMEM],
+        out_specs=VMEM,
+        name="pieces",
+    )(movie)
     strip_movie = lax.all_to_all(pieces, "tile", split_axis=0, concat_axis=0, tiled=True)
 
     traces_rows = traces.T
-    fitted, edge_a, edge_b, coupling, turned, table, sides = pl.pallas_call(
+    fitted, edge_a, edge_b, coupling, table, sides = pl.pallas_call(
         kernel_components,
         out_shape=[
             jax.ShapeDtypeStruct((frames, tile_rows, columns), jnp.float32),
             jax.ShapeDtypeStruct((frames, HALO, columns), jnp.bfloat16),
             jax.ShapeDtypeStruct((frames, HALO, columns), jnp.bfloat16),
             jax.ShapeDtypeStruct((components, components), jnp.float32),
-            jax.ShapeDtypeStruct((components, pixels), jnp.bfloat16),
             jax.ShapeDtypeStruct((2 * columns, columns), jnp.bfloat16),
             jax.ShapeDtypeStruct((2 * tile_rows, LANES), jnp.bfloat16),
         ],
-        in_specs=[VMEM, VMEM, VMEM, SMEM],
-        out_specs=[VMEM] * 7,
-        scratch_shapes=[pltpu.VMEM((halves, frames * tile_rows, LANES), jnp.float32)],
-        compiler_params=pltpu.CompilerParams(vmem_limit_bytes=12 << 20),
+        in_specs=[ANY] * 4,
+        out_specs=[VMEM] * 6,
+        scratch_shapes=[
+            pltpu.VMEM(footprints.shape, footprints.dtype),
+            pltpu.VMEM(support.shape, support.dtype),
+            pltpu.VMEM(traces_rows.shape, traces.dtype),
+            pltpu.VMEM(border_offsets.shape[::-1], border_offsets.dtype),
+            lined,
+            pltpu.SemaphoreType.DMA((tile_rows // BR,)),
+            pltpu.SemaphoreType.DMA((3,)),
+        ],
+        compiler_params=pltpu.CompilerParams(vmem_limit_bytes=40 << 20),
         cost_estimate=pl.CostEstimate(
             flops=2 * pixels * components * components,
             bytes_accessed=4 * pixels * components,
@@ -333,10 +413,16 @@
             jax.ShapeDtypeStruct((frames, components), jnp.bfloat16),
             jax.ShapeDtypeStruct((frames, tile_rows, columns), jnp.bfloat16),
         ],
-        in_specs=[VMEM] * 14,
+        in_specs=[VMEM] * 4 + [ANY] + [VMEM] * 8,
         out_specs=[VMEM] * 3,
-        scratch_shapes=[pltpu.VMEM((halves, frames * tile_rows, LANES), jnp.float32)] * 2,
-        compiler_params=pltpu.CompilerParams(vmem_limit_bytes=16 << 20),
+        scratch_shapes=[
+            lined,
+            lined,
+            pltpu.VMEM(footprints.shape, footprints.dtype),
+            pltpu.VMEM((components, pixels), jnp.bfloat16),
+            pltpu.SemaphoreType.DMA((tile_rows // BR,)),
+        ],
+        compiler_params=pltpu.CompilerParams(vmem_limit_bytes=48 << 20),
         cost_estimate=pl.CostEstimate(
             flops=8 * frames * pixels * components,
             bytes_accessed=4 * pixels * components,
@@ -353,23 +439,29 @@
         traces_rows,
         border_weight,
         coupling,
-        turned,
         table,
         sides,
         row_filter,
         col_filter,
     )
 
+    frame_count = lax.axis_size("frame")
+    all_traces = [rounded] + [
+        lax.ppermute(rounded, "frame", pairs(frame_count, turn)) for turn in range(1, frame_count)
+    ]
     remainder = lax.all_to_all(leftover, "tile", split_axis=0, concat_axis=0, tiled=True)
     remainder = (
         remainder.reshape(tile_count, own_frames, tile_rows, columns)
         .transpose(1, 0, 2, 3)
         .reshape(own_frames, tile_count * tile_rows, columns)
     )
-    all_traces = lax.all_gather(rounded, "frame", axis=0, tiled=True)
-    trace_gram = lax.dot_general(
-        all_traces, all_traces, (((0,), (0,)), ((), ())), preferred_element_type=jnp.float32
-    )
+    trace_gram = pl.pallas_call(
+        kernel_gram,
+        out_shape=jax.ShapeDtypeStruct((components, components), jnp.float32),
+        in_specs=[VMEM] * len(all_traces),
+        out_specs=VMEM,
+        name="gram",
+    )(*all_traces)
     return (new_traces.T, trace_gram, remainder)
 
 

time: 77.7 us -> 59.2 us (0.76)
  local copies, waits for them, and re-layouts: 32.6 us -> 8.56 us
  Pallas kernels: 14 us -> 22.9 us
  blocking collectives: 5.18 us -> 0 us
  starting transfers between devices: 19.5 us -> 21.4 us
  waiting for transfers between devices: 3.73 us -> 5.11 us
  matrix products: 1.07 us -> 0 us
    unnamed x32 -> x27, local copies, waits for them, and re-layouts: 31.2 us -> 8.56 us
    all_gather x1 -> x0, blocking collectives: 5.18 us -> none  [per_device(): all_traces = lax.all_gather(rounded, 'frame', axis=0, tiled=True)]
    pallas_call x0 -> x2, Pallas kernels: none -> 3.61 us  [the longest x1 1.82 us: per_device(): pl.pallas_call(kernel_gram, out_shape=jax.ShapeDtypeStruct((components, c...]
    pallas_call x1, Pallas kernels: 6.41 us -> 9.96 us  [per_device(): pl.pallas_call(functools.partial(kernel_frames, tile_count), out_shape=[j...]
    ppermute x0 -> x3, starting transfers between devices: none -> 1.86 us  [per_device(): lax.ppermute(rounded, 'frame', pairs(frame_count, turn))]
    ppermute x0 -> x3, waiting for transfers between devices: none -> 1.84 us  [per_device(): lax.ppermute(rounded, 'frame', pairs(frame_count, turn))]
    pallas_call x1, Pallas kernels: 7.59 us -> 9.31 us  [per_device(): pl.pallas_call(kernel_components, out_shape=[jax.ShapeDtypeStruct((frames...]
    concatenate x1 -> x0, local copies, waits for them, and re-layouts: 1.41 us -> none  [per_device(): jnp.concatenate([lax.slice_in_dim(padded, t * tile_rows, t * tile_rows +...]
  transfers between devices with their start and end apart: 4 -> 7, of which waited for: 2 -> 4; matrix products, arithmetic and copies ran while one was open for 1% -> 0% of each run, Pallas kernels for 10% -> 19%
where the time goes in v2:
time: 59.2 us; the launch traced here: 58.7 us
  Pallas kernels  22.9 us (39%)
  starting transfers between devices  21.4 us (36%)
  local copies, waits for them, and re-layouts  8.56 us (14%)
  waiting for transfers between devices  5.11 us (9%)
  between operations  0.77 us (1%)
    pallas_call x1, Pallas kernels, per_device(): pl.pallas_call(functools.partial(kernel_frames, tile_count), out_shape=[j...  9.96 us
    all_to_all x1, starting transfers between devices, per_device(): lax.all_to_all(leftover, 'tile', split_axis=0, concat_axis=0, tiled=True)  9.34 us
    pallas_call x1, Pallas kernels, per_device(): pl.pallas_call(kernel_components, out_shape=[jax.ShapeDtypeStruct((frames...  9.31 us
    unnamed x27, local copies, waits for them, and re-layouts  8.56 us
    all_to_all x1, starting transfers between devices, per_device(): lax.all_to_all(pieces, 'tile', split_axis=0, concat_axis=0, tiled=True)  7.28 us
    ppermute x1, starting transfers between devices, per_device(): edge_a = lax.ppermute(edge_a, 'tile', evens + [(j, i) for i, j in evens])  2.09 us
    ppermute x3, starting transfers between devices, per_device(): lax.ppermute(rounded, 'frame', pairs(frame_count, turn))  1.86 us
    ppermute x3, waiting for transfers between devices, per_device(): lax.ppermute(rounded, 'frame', pairs(frame_count, turn))  1.84 us
  transfers between devices with their start and end apart: 7, of which 4 were waited for; matrix products, arithmetic and copies ran while one was open for 0% of the time, Pallas kernels for 19%

profile of v2, /device:TPU:0, one launch (start us, length us, event | category | flops | bytes accessed | tf_op | source)
XLA Modules:
  0.0 58.7 jit_solution(17140919339345148696)
XLA Ops:
  0.6 0.0 copy-start.1
  0.6 0.0 copy-start.3
  0.7 0.0 copy-start.5
  0.7 1.8 %pieces.1 = bf16[8,112,256]{2,1,0:T(8,128)(2,1)} custom-call(bf16[1,512,256]{2,1,0:T(8,128)(2,1)} %movie_ref.1), custom_call_target="tpu_custom_call" | custom-call | tf_op jit(solution)/shard_map/pieces/pallas_call | solution.py:363
  2.5 7.3 %all-to-all-start = ((bf16[8,112,256]{2,1,0:T(8,128)(2,1)}), bf16[8,112,256]{2,1,0:T(8,128)(2,1)S(1)}, u32[]{:S(2)}, u32[]{:S(2)}) async-start(bf16[8,112,256]{2,1,0:T(8,128)(2,1)} %pieces.1), calls=%async_computation | async-start | bytes 917504 | tf_op jit(solution)/shard_map/all_to_all | solution.py:370
  9.8 4.6 %copy-done = bf16[64,256,384]{2,1,0:T(8,128)(2,1)S(1)} copy-done((bf16[64,256,384]{2,1,0:T(8,128)(2,1)S(1)}, bf16[64,256,384]{2,1,0:T(8,128)(2,1)}, u32[]{:S(2)}) %copy-start) | copy-done | bytes 12582936
  14.3 0.7 %copy-done.4 = s32[8,384]{1,0:T(8,128)S(1)} copy-done((s32[8,384]{1,0:T(8,128)S(1)}, s32[8,384]{1,0:T(8,128)}, u32[]{:S(2)}) %copy-start.4) | copy-done | bytes 12312
  15.0 0.7 %copy-done.6 = bf16[384,8]{0,1:T(8,128)(2,1)S(1)} copy-done((bf16[384,8]{0,1:T(8,128)(2,1)S(1)}, bf16[384,8]{0,1:T(8,128)(2,1)}, u32[]{:S(2)}) %copy-start.6) | copy-done | bytes 6168
  15.7 0.7 %copy-done.9 = s32[64,2]{0,1:T(2,128)S(1)} copy-done((s32[64,2]{0,1:T(2,128)S(1)}, s32[64,2]{0,1:T(2,128)}, u32[]{:S(2)}) %copy-start.9) | copy-done | bytes 536
  16.4 9.3 %components.1 = (f32[8,64,256]{2,1,0:T(8,128)S(1)}, bf16[8,24,256]{2,1,0:T(8,128)(2,1)S(1)}, bf16[8,24,256]{2,1,0:T(8,128)(2,1)S(1)}, f32[384,384]{1,0:T(8,128)S...) custom-call(bf16[64,256,384]{2,1,0:T(8,128)(2,1)S(1)} %copy-done, s32[8,384]{1,0:T(8,128)S(1)} %copy-done.4, ...), custom_call_target="tpu_custom_call" | custom-call | flops 4831838208 | bytes 25165824 | tf_op jit(solution)/shard_map/components/pallas_call | solution.py:373
  25.7 2.1 %collective-permute-start = (bf16[8,24,256]{2,1,0:T(8,128)(2,1)S(1)}, bf16[8,24,256]{2,1,0:T(8,128)(2,1)S(1)}, u32[]{:S(2)}, u32[]{:S(2)}) collective-permute-start(bf16[8,24,256]{2,1,0:T(8,128)(2,1)S(1)} %get-tuple-element.13), channel_id=1, source_target_pairs={{0,4},{8,12},{16,20},{24,28},{4,0},{12,8},{20,16},{28,24},{1,5},{9... | collective-permute-start | bytes 294920 | tf_op jit(solution)/shard_map/ppermute | solution.py:405
  27.8 0.8 %collective-permute-start.1 = (bf16[8,24,256]{2,1,0:T(8,128)(2,1)S(1)}, bf16[8,24,256]{2,1,0:T(8,128)(2,1)S(1)}, u32[]{:S(2)}, u32[]{:S(2)}) collective-permute-start(bf16[8,24,256]{2,1,0:T(8,128)(2,1)S(1)} %get-tuple-element.14), channel_id=1, source_target_pairs={{4,8},{12,16},{20,24},{8,4},{16,12},{24,20},{5,9},{13,17},{21,25},... | collective-permute-start | bytes 294920 | tf_op jit(solution)/shard_map/ppermute | solution.py:406
  28.7 1.8 %collective-permute-done.edge_a_ref = bf16[8,24,256]{2,1,0:T(8,128)(2,1)S(1)} collective-permute-done((bf16[8,24,256]{2,1,0:T(8,128)(2,1)S(1)}, bf16[8,24,256]{2,1,0:T(8,128)(2,1)S(1)}, u32[]{:S(2)}, u32[]{:S(2)}) %collective-permute-start) | collective-permute-done | bytes 98336 | tf_op jit(solution)/shard_map/ppermute | solution.py:405
  30.5 10.0 %frames.1 = (f32[8,384]{1,0:T(8,128)}, bf16[8,384]{1,0:T(8,128)(2,1)S(1)}, bf16[8,64,256]{2,1,0:T(8,128)(2,1)}) custom-call(bf16[8,112,256]{2,1,0:T(8,128)(2,1)S(1)} %all-to-all-done.movie_ref, f32[8,64,256]{2,1,0:T(8,128)S(1)} %get-tuple-element.12.fitted_ref, bf16[8,24,256]{2,1,0:T(8,128)(2,1)S(1)} %collective-permute-done.edge_a_ref, ...), custom_call_target="tpu_custom_call" | custom-call | flops 402653184 | bytes 25165824 | tf_op jit(solution)/shard_map/frames/pallas_call | solution.py:409
  40.5 9.3 %all-to-all-start.1 = ((bf16[8,64,256]{2,1,0:T(8,128)(2,1)}), bf16[8,64,256]{2,1,0:T(8,128)(2,1)S(1)}, u32[]{:S(2)}, u32[]{:S(2)}) async-start(bf16[8,64,256]{2,1,0:T(8,128)(2,1)} %get-tuple-element.20), calls=%async_computation.1 | async-start | bytes 524288 | tf_op jit(solution)/shard_map/all_to_all | solution.py:452
  49.8 1.6 %collective-permute-start.3 = (bf16[8,384]{1,0:T(8,128)(2,1)S(1)}, bf16[8,384]{1,0:T(8,128)(2,1)S(1)}, u32[]{:S(2)}, u32[]{:S(2)}) collective-permute-start(bf16[8,384]{1,0:T(8,128)(2,1)S(1)} %get-tuple-element.19.refs_0_), channel_id=1, source_target_pairs={{0,2},{1,3},{2,0},{3,1},{4,6},{5,7},{6,4},{7,5},{8,10},{9,11},{10,... | collective-permute-start | bytes 18440 | tf_op jit(solution)/shard_map/ppermute | solution.py:450
  51.4 0.3 collective-permute-start.2
  51.7 1.2 %collective-permute-done.4.refs_3_ = bf16[8,384]{1,0:T(8,128)(2,1)S(1)} collective-permute-done((bf16[8,384]{1,0:T(8,128)(2,1)S(1)}, bf16[8,384]{1,0:T(8,128)(2,1)S(1)}, u32[]{:S(2)}, u32[]{:S(2)}) %collective-permute-start.4) | collective-permute-done | bytes 6176 | tf_op jit(solution)/shard_map/ppermute | solution.py:450
  52.9 0.6 %collective-permute-done.3.refs_2_ = bf16[8,384]{1,0:T(8,128)(2,1)S(1)} collective-permute-done((bf16[8,384]{1,0:T(8,128)(2,1)S(1)}, bf16[8,384]{1,0:T(8,128)(2,1)S(1)}, u32[]{:S(2)}, u32[]{:S(2)}) %collective-permute-start.3) | collective-permute-done | bytes 6176 | tf_op jit(solution)/shard_map/ppermute | solution.py:450
  53.5 0.6 copy-done.11
  54.1 0.6 copy-done.12
  54.7 1.8 %gram.1 = f32[384,384]{1,0:T(8,128)} custom-call(bf16[8,384]{1,0:T(8,128)(2,1)} %copy-done.8, bf16[8,384]{1,0:T(8,128)(2,1)} %copy-done.12, bf16[8,384]{1,0:T(8,128)(2,1)} %copy-done.11, bf16[8,384]{1,0:T(8,128)(2,1)} %copy-done.10), custom_call_target="tpu_custom_call" | custom-call | tf_op jit(solution)/shard_map/gram/pallas_call | solution.py:458
  56.5 1.5 %all-to-all-done.1 = bf16[8,64,256]{2,1,0:T(8,128)(2,1)S(1)} async-done(((bf16[8,64,256]{2,1,0:T(8,128)(2,1)}), bf16[8,64,256]{2,1,0:T(8,128)(2,1)S(1)}, u32[]{:S(2)}, u32[]{:S(2)}) %all-to-all-start.1) | async-done | bytes 262176 | tf_op jit(solution)/shard_map/all_to_all | solution.py:452
  58.0 0.7 %copy.12 = bf16[1,512,256]{2,1,0:T(8,128)(2,1)} copy(bf16[1,512,256]{2,1,0:T(8,128)(2,1)S(1)} %bitcast.7) | data formatting | bytes 524288
  (21 shorter events, 0.0 us)
Async XLA Ops:
  0.6 29.8 %copy-start.1 = (bf16[768,256]{1,0:T(8,128)(2,1)S(1)}, bf16[768,256]{1,0:T(8,128)(2,1)}, u32[]{:S(2)}) copy-start(bf16[768,256]{1,0:T(8,128)(2,1)} %constant.5.clone.col_filter_ref) | copy-start | bytes 1179652
  0.6 29.8 %copy-start.3 = (bf16[96,224]{1,0:T(8,128)(2,1)S(1)}, bf16[96,224]{1,0:T(8,128)(2,1)}, u32[]{:S(2)}) copy-start(bf16[96,224]{1,0:T(8,128)(2,1)} %constant.4.clone.row_filter_ref) | copy-start | bytes 129028
  0.7 29.8 %copy-start.5 = (s32[8,384]{1,0:T(8,128)S(1)}, s32[8,384]{1,0:T(8,128)}, u32[]{:S(2)}) copy-start(s32[8,384]{1,0:T(8,128)} %support_ref.1) | copy-start | bytes 36868
  0.7 29.8 %copy-start.7 = (bf16[384,8]{0,1:T(8,128)(2,1)S(1)}, bf16[384,8]{0,1:T(8,128)(2,1)}, u32[]{:S(2)}) copy-start(bf16[384,8]{0,1:T(8,128)(2,1)} %param.11) | copy-start | bytes 18436
  0.7 29.8 %copy-start.2 = (f32[64,256]{1,0:T(8,128)S(1)}, f32[64,256]{1,0:T(8,128)}, u32[]{:S(2)}) copy-start(f32[64,256]{1,0:T(8,128)} %weight_ref.1) | copy-start | bytes 196612
  2.5 27.9 %all-to-all-start = ((bf16[8,112,256]{2,1,0:T(8,128)(2,1)}), bf16[8,112,256]{2,1,0:T(8,128)(2,1)S(1)}, u32[]{:S(2)}, u32[]{:S(2)}) async-start(bf16[8,112,256]{2,1,0:T(8,128)(2,1)} %pieces.1), calls=%async_computation | async-start | bytes 917504 | tf_op jit(solution)/shard_map/all_to_all | solution.py:370
  9.8 4.6 %copy-start = (bf16[64,256,384]{2,1,0:T(8,128)(2,1)S(1)}, bf16[64,256,384]{2,1,0:T(8,128)(2,1)}, u32[]{:S(2)}) copy-start(bf16[64,256,384]{2,1,0:T(8,128)(2,1)} %footprints_hbm.3) | copy-start | bytes 37748740
  14.3 0.7 %copy-start.4 = (s32[8,384]{1,0:T(8,128)S(1)}, s32[8,384]{1,0:T(8,128)}, u32[]{:S(2)}) copy-start(s32[8,384]{1,0:T(8,128)} %support_ref.1) | copy-start | bytes 36868
  15.0 0.7 %copy-start.6 = (bf16[384,8]{0,1:T(8,128)(2,1)S(1)}, bf16[384,8]{0,1:T(8,128)(2,1)}, u32[]{:S(2)}) copy-start(bf16[384,8]{0,1:T(8,128)(2,1)} %param.11) | copy-start | bytes 18436
  15.7 0.7 %copy-start.9 = (s32[64,2]{0,1:T(2,128)S(1)}, s32[64,2]{0,1:T(2,128)}, u32[]{:S(2)}) copy-start(s32[64,2]{0,1:T(2,128)} %param.13) | copy-start | bytes 1540
  25.7 4.7 %collective-permute-start = (bf16[8,24,256]{2,1,0:T(8,128)(2,1)S(1)}, bf16[8,24,256]{2,1,0:T(8,128)(2,1)S(1)}, u32[]{:S(2)}, u32[]{:S(2)}) collective-permute-start(bf16[8,24,256]{2,1,0:T(8,128)(2,1)S(1)} %get-tuple-element.13), channel_id=1, source_target_pairs={{0,4},{8,12},{16,20},{24,28},{4,0},{12,8},{20,16},{28,24},{1,5},{9... | collective-permute-start | bytes 294920 | tf_op jit(solution)/shard_map/ppermute | solution.py:405
  27.8 2.6 %collective-permute-start.1 = (bf16[8,24,256]{2,1,0:T(8,128)(2,1)S(1)}, bf16[8,24,256]{2,1,0:T(8,128)(2,1)S(1)}, u32[]{:S(2)}, u32[]{:S(2)}) collective-permute-start(bf16[8,24,256]{2,1,0:T(8,128)(2,1)S(1)} %get-tuple-element.14), channel_id=1, source_target_pairs={{4,8},{12,16},{20,24},{8,4},{16,12},{24,20},{5,9},{13,17},{21,25},... | collective-permute-start | bytes 294920 | tf_op jit(solution)/shard_map/ppermute | solution.py:406
  40.4 13.1 %copy-start.8 = (bf16[8,384]{1,0:T(8,128)(2,1)}, bf16[8,384]{1,0:T(8,128)(2,1)S(1)}, u32[]{:S(2)}) copy-start(bf16[8,384]{1,0:T(8,128)(2,1)S(1)} %get-tuple-element.19.refs_0_) | copy-start | bytes 18436
  40.5 17.6 %all-to-all-start.1 = ((bf16[8,64,256]{2,1,0:T(8,128)(2,1)}), bf16[8,64,256]{2,1,0:T(8,128)(2,1)S(1)}, u32[]{:S(2)}, u32[]{:S(2)}) async-start(bf16[8,64,256]{2,1,0:T(8,128)(2,1)} %get-tuple-element.20), calls=%async_computation.1 | async-start | bytes 524288 | tf_op jit(solution)/shard_map/all_to_all | solution.py:452
  49.8 3.1 %collective-permute-start.4 = (bf16[8,384]{1,0:T(8,128)(2,1)S(1)}, bf16[8,384]{1,0:T(8,128)(2,1)S(1)}, u32[]{:S(2)}, u32[]{:S(2)}) collective-permute-start(bf16[8,384]{1,0:T(8,128)(2,1)S(1)} %get-tuple-element.19.refs_0_), channel_id=1, source_target_pairs={{0,3},{1,2},{2,1},{3,0},{4,7},{5,6},{6,5},{7,4},{8,11},{9,10},{10,... | collective-permute-start | bytes 18440 | tf_op jit(solution)/shard_map/ppermute | solution.py:450
  49.8 3.7 %collective-permute-start.3 = (bf16[8,384]{1,0:T(8,128)(2,1)S(1)}, bf16[8,384]{1,0:T(8,128)(2,1)S(1)}, u32[]{:S(2)}, u32[]{:S(2)}) collective-permute-start(bf16[8,384]{1,0:T(8,128)(2,1)S(1)} %get-tuple-element.19.refs_0_), channel_id=1, source_target_pairs={{0,2},{1,3},{2,0},{3,1},{4,6},{5,7},{6,4},{7,5},{8,10},{9,11},{10,... | collective-permute-start | bytes 18440 | tf_op jit(solution)/shard_map/ppermute | solution.py:450
  51.4 2.1 %collective-permute-start.2 = (bf16[8,384]{1,0:T(8,128)(2,1)S(1)}, bf16[8,384]{1,0:T(8,128)(2,1)S(1)}, u32[]{:S(2)}, u32[]{:S(2)}) collective-permute-start(bf16[8,384]{1,0:T(8,128)(2,1)S(1)} %get-tuple-element.19.refs_0_), channel_id=1, source_target_pairs={{0,1},{1,0},{2,3},{3,2},{4,5},{5,4},{6,7},{7,6},{8,9},{9,8},{10,11... | collective-permute-start | bytes 18440 | tf_op jit(solution)/shard_map/ppermute | solution.py:450
  52.9 0.6 %copy-start.10 = (bf16[8,384]{1,0:T(8,128)(2,1)}, bf16[8,384]{1,0:T(8,128)(2,1)S(1)}, u32[]{:S(2)}) copy-start(bf16[8,384]{1,0:T(8,128)(2,1)S(1)} %collective-permute-done.4.refs_3_) | copy-start | bytes 18436
  53.5 0.6 %copy-start.11 = (bf16[8,384]{1,0:T(8,128)(2,1)}, bf16[8,384]{1,0:T(8,128)(2,1)S(1)}, u32[]{:S(2)}) copy-start(bf16[8,384]{1,0:T(8,128)(2,1)S(1)} %collective-permute-done.3.refs_2_) | copy-start | bytes 18436
  54.1 0.6 copy-start.12

commit v3 on v2

--- a/solution.py
+++ b/solution.py
@@ -16,8 +16,9 @@
 NR = 64
 HALO = 24
 LANES = 128
+AHEAD = 3
 VMEM = pl.BlockSpec(memory_space=pltpu.VMEM)
-ANY = pl.BlockSpec(memory_space=pl.ANY)
+HBM = pl.BlockSpec(memory_space=pltpu.HBM)
 
 
 def split_high_low(values):
@@ -87,42 +88,29 @@
         )
 
 
-def kernel_pieces(tile_rows, movie_ref, pieces_ref):
-    frames, image_rows, columns = movie_ref.shape
-    count = image_rows // tile_rows
-    for tile in range(count):
-        for frame in range(frames):
-            start = max(tile * tile_rows - HALO, 0)
-            stop = min((tile + 1) * tile_rows + HALO, image_rows)
-            rows = movie_ref[frame, start:stop, :]
-            blank = jnp.zeros((tile_rows + 2 * HALO - (stop - start), columns), movie_ref.dtype)
-            if tile == 0:
-                rows = jnp.concatenate([blank, rows], axis=0)
-            elif tile == count - 1:
-                rows = jnp.concatenate([rows, blank], axis=0)
-            pieces_ref[tile * frames + frame] = rows
-
-
-def start_footprints(footprints_hbm, footprints_ref, arrived):
-    copies = []
-    for b in range(footprints_ref.shape[0] // BR):
-        rows = pl.ds(b * BR, BR)
-        copies.append(
-            pltpu.make_async_copy(footprints_hbm.at[rows], footprints_ref.at[rows], arrived.at[b])
-        )
-        copies[-1].start()
-    return copies
-
-
-def kernel_components(
+class Footprints:
+    def __init__(self, source, target, arrived):
+        self.copies = []
+        for b in range(target.shape[0] // BR):
+            rows = pl.ds(b * BR, BR)
+            self.copies.append(
+                pltpu.make_async_copy(source.at[rows], target.at[rows], arrived.at[b])
+            )
+        for copy in self.copies[:AHEAD]:
+            copy.start()
+
+    def wait(self, b):
+        self.copies[b].wait()
+        if b + AHEAD < len(self.copies):
+            self.copies[b + AHEAD].start()
+
+
+def kernel_fitted(
     footprints_hbm,
     support_hbm,
     traces_hbm,
     offsets_hbm,
     fitted_ref,
-    edge_a_ref,
-    edge_b_ref,
-    coupling_ref,
     table_ref,
     sides_ref,
     footprints_ref,
@@ -145,28 +133,45 @@
     ]
     for copy in small:
         copy.start()
-    copies = start_footprints(footprints_hbm, footprints_ref, arrived)
+    blocks = Footprints(footprints_hbm, footprints_ref, arrived)
     tile_rows, columns, components = footprints_ref.shape
     frames = traces_ref.shape[0]
     halves = columns // LANES
     block = BR * columns
-    split = components // 256 * 256
     for copy in small:
         copy.wait()
     border_tables(offsets_ref[...], table_ref, sides_ref)
     traces = traces_ref[...]
     for b in range(tile_rows // BR):
-        copies[b].wait()
-        mask = support_ref[b : b + 1, :].astype(jnp.bfloat16)
-        shaped = footprints_ref[b * BR : (b + 1) * BR].reshape(block, components) * mask
-        turned = shaped.T
-        fitted = jnp.dot(traces, turned, preferred_element_type=jnp.float32)
+        blocks.wait(b)
+        fitted = lax.dot_general(
+            traces * support_ref[b : b + 1, :].astype(jnp.bfloat16),
+            footprints_ref[b * BR : (b + 1) * BR].reshape(block, components),
+            (((1,), (1,)), ((), ())),
+            preferred_element_type=jnp.float32,
+        )
         for row in range(BR):
             for half in range(halves):
                 start = row * columns + half * LANES
                 lined_ref[half, pl.ds(b * BR + row, frames, stride=tile_rows), :] = fitted[
                     :, start : start + LANES
                 ]
+    for half in range(halves):
+        for frame in range(frames):
+            fitted_ref[frame, :, half * LANES : (half + 1) * LANES] = lined_ref[
+                half, frame * tile_rows : (frame + 1) * tile_rows, :
+            ]
+
+
+def kernel_coupling(footprints_ref, support_ref, turned_ref, coupling_ref):
+    tile_rows, columns, components = footprints_ref.shape
+    block = BR * columns
+    split = components // 256 * 256
+    for b in range(tile_rows // BR):
+        mask = support_ref[b : b + 1, :].astype(jnp.bfloat16)
+        shaped = footprints_ref[b * BR : (b + 1) * BR].reshape(block, components) * mask
+        turned = shaped.T
+        turned_ref[:, b * block : (b + 1) * block] = turned
         left = jnp.dot(turned, shaped[:, :split], preferred_element_type=jnp.float32)
         right = jnp.dot(turned[split:], shaped[:, split:], preferred_element_type=jnp.float32)
         if b == 0:
@@ -176,25 +181,15 @@
             coupling_ref[:, :split] += left
             coupling_ref[split:, split:] += right
     coupling_ref[:split, split:] = coupling_ref[split:, :split].T
-    odd = lax.axis_index("tile") % 2 == 1
-    for half in range(halves):
-        lanes = slice(half * LANES, (half + 1) * LANES)
-        for frame in range(frames):
-            lines = lined_ref[half, frame * tile_rows : (frame + 1) * tile_rows, :]
-            fitted_ref[frame, :, lanes] = lines
-            top = lines[:HALO]
-            bottom = lines[tile_rows - HALO :]
-            edge_a_ref[frame, :, lanes] = jnp.where(odd, top, bottom).astype(jnp.bfloat16)
-            edge_b_ref[frame, :, lanes] = jnp.where(odd, bottom, top).astype(jnp.bfloat16)
-
-
-def kernel_frames(
+
+
+def kernel_traces(
     tile_count,
     movie_ref,
-    fitted_ref,
+    first_ref,
     edge_a_ref,
     edge_b_ref,
-    footprints_hbm,
+    footprints_ref,
     support_ref,
     traces_ref,
     weight_ref,
@@ -205,14 +200,8 @@
     col_filter_ref,
     new_traces_ref,
     rounded_ref,
-    remainder_ref,
     cleaned_ref,
-    refit_ref,
-    footprints_ref,
-    turned_ref,
-    arrived,
 ):
-    copies = start_footprints(footprints_hbm, footprints_ref, arrived)
     tile_rows, columns, components = footprints_ref.shape
     frames = traces_ref.shape[0]
     halves = columns // LANES
@@ -229,15 +218,14 @@
     for frame in range(frames):
         edge_a = edge_a_ref[frame].astype(jnp.float32)
         edge_b = edge_b_ref[frame].astype(jnp.float32)
-        fitted = jnp.concatenate(
+        first = jnp.concatenate(
             [
                 jnp.where(odd, edge_a, edge_b),
-                fitted_ref[frame],
+                first_ref[frame].astype(jnp.float32),
                 jnp.where(odd, edge_b, edge_a),
             ],
             axis=0,
-        )
-        first = (movie_ref[frame].astype(jnp.float32) - fitted).astype(jnp.bfloat16)
+        ).astype(jnp.bfloat16)
         tall.append(
             jnp.dot(
                 row_filter,
@@ -264,22 +252,15 @@
         summed = summed + jnp.where(lane >= RR, west, 0.0)
         summed = summed + jnp.where(lane < columns - RR, east, 0.0)
         background = weight * summed * (1.0 / math.sqrt(NR))
-        movie = movie_ref[frame, HALO : HALO + tile_rows, :].astype(jnp.float32)
+        movie = movie_ref[frame].astype(jnp.float32)
         cleaned = (movie - background).astype(jnp.bfloat16).astype(jnp.float32)
         for half in range(halves):
             cleaned_ref[half, frame * tile_rows : (frame + 1) * tile_rows, :] = cleaned[
                 :, half * LANES : (half + 1) * LANES
             ]
 
-    block = BR * columns
     projected = jnp.zeros((frames, components), jnp.float32)
     for b in range(tile_rows // BR):
-        copies[b].wait()
-        mask = support_ref[b : b + 1, :]
-        shaped = footprints_ref[b * BR : (b + 1) * BR].reshape(
-            block, components
-        ) * mask.astype(jnp.bfloat16)
-        turned_ref[:, b * block : (b + 1) * block] = shaped.T
         part = jnp.zeros((frames, components), jnp.float32)
         for row in range(b * BR, (b + 1) * BR):
             pixels = jnp.concatenate(
@@ -292,7 +273,7 @@
             part = part + jnp.dot(
                 pixels, footprints_ref[row], preferred_element_type=jnp.float32
             )
-        projected = projected + part * mask.astype(jnp.float32)
+        projected = projected + part * support_ref[b : b + 1, :].astype(jnp.float32)
 
     coupling = coupling_ref[...]
     diagonal = lax.broadcasted_iota(jnp.int32, coupling.shape, 0) == lax.broadcasted_iota(
@@ -317,6 +298,12 @@
     new_traces_ref[...] = state
     rounded_ref[...] = rounded
 
+
+def kernel_refit(rounded_ref, turned_ref, cleaned_ref, remainder_ref, refit_ref):
+    frames, tile_rows, columns = remainder_ref.shape
+    halves = columns // LANES
+    block = BR * columns
+    rounded = rounded_ref[...]
     for b in range(tile_rows // BR):
         refit = jnp.dot(
             rounded,
@@ -357,81 +344,99 @@
     frames = own_frames * tile_count
     pixels = tile_rows * columns
     halves = columns // LANES
-    extended = tile_rows + 2 * HALO
     lined = pltpu.VMEM((halves, frames * tile_rows, LANES), jnp.float32)
-
-    pieces = pl.pallas_call(
-        functools.partial(kernel_pieces, tile_rows),
-        out_shape=jax.ShapeDtypeStruct((frames, extended, columns), movie.dtype),
-        in_specs=[VMEM],
-        out_specs=VMEM,
-        name="pieces",
-    )(movie)
+    lined_shape = jax.ShapeDtypeStruct(lined.shape, lined.dtype)
+    blocks = tile_rows // BR
+
+    pieces = (
+        movie.reshape(own_frames, tile_count, tile_rows, columns)
+        .transpose(1, 0, 2, 3)
+        .reshape(frames, tile_rows, columns)
+    )
     strip_movie = lax.all_to_all(pieces, "tile", split_axis=0, concat_axis=0, tiled=True)
 
     traces_rows = traces.T
-    fitted, edge_a, edge_b, coupling, table, sides = pl.pallas_call(
-        kernel_components,
+    pinned = [
+        pltpu.with_memory_space_constraint(array, pltpu.HBM)
+        for array in (footprints, support, traces_rows, border_offsets.T)
+    ]
+    fitted, table, sides = pl.pallas_call(
+        kernel_fitted,
         out_shape=[
             jax.ShapeDtypeStruct((frames, tile_rows, columns), jnp.float32),
-            jax.ShapeDtypeStruct((frames, HALO, columns), jnp.bfloat16),
-            jax.ShapeDtypeStruct((frames, HALO, columns), jnp.bfloat16),
-            jax.ShapeDtypeStruct((components, components), jnp.float32),
             jax.ShapeDtypeStruct((2 * columns, columns), jnp.bfloat16),
             jax.ShapeDtypeStruct((2 * tile_rows, LANES), jnp.bfloat16),
         ],
-        in_specs=[ANY] * 4,
-        out_specs=[VMEM] * 6,
+        in_specs=[HBM] * 4,
+        out_specs=[VMEM] * 3,
         scratch_shapes=[
             pltpu.VMEM(footprints.shape, footprints.dtype),
             pltpu.VMEM(support.shape, support.dtype),
             pltpu.VMEM(traces_rows.shape, traces.dtype),
             pltpu.VMEM(border_offsets.shape[::-1], border_offsets.dtype),
             lined,
-            pltpu.SemaphoreType.DMA((tile_rows // BR,)),
+            pltpu.SemaphoreType.DMA((blocks,)),
             pltpu.SemaphoreType.DMA((3,)),
         ],
-        compiler_params=pltpu.CompilerParams(vmem_limit_bytes=40 << 20),
+        compiler_params=pltpu.CompilerParams(vmem_limit_bytes=24 << 20),
+        cost_estimate=pl.CostEstimate(
+            flops=2 * frames * pixels * components,
+            bytes_accessed=2 * pixels * components,
+            transcendentals=0,
+        ),
+        name="fitted",
+    )(*pinned)
+
+    first = (strip_movie.astype(jnp.float32) - fitted).astype(jnp.bfloat16)
+    odd = lax.axis_index("tile") % 2 == 1
+    top = first[:, :HALO]
+    bottom = first[:, tile_rows - HALO :]
+    evens = [(i, i + 1) for i in range(0, tile_count - 1, 2)]
+    odds = [(i, i + 1) for i in range(1, tile_count - 1, 2)]
+    edge_a = lax.ppermute(
+        jnp.where(odd, top, bottom), "tile", evens + [(j, i) for i, j in evens]
+    )
+    edge_b = lax.ppermute(
+        jnp.where(odd, bottom, top), "tile", odds + [(j, i) for i, j in odds]
+    )
+
+    turned, coupling = pl.pallas_call(
+        kernel_coupling,
+        out_shape=[
+            jax.ShapeDtypeStruct((components, pixels), jnp.bfloat16),
+            jax.ShapeDtypeStruct((components, components), jnp.float32),
+        ],
+        in_specs=[VMEM] * 2,
+        out_specs=[VMEM] * 2,
+        compiler_params=pltpu.CompilerParams(vmem_limit_bytes=24 << 20),
         cost_estimate=pl.CostEstimate(
             flops=2 * pixels * components * components,
             bytes_accessed=4 * pixels * components,
             transcendentals=0,
         ),
-        name="components",
-    )(footprints, support, traces_rows, border_offsets.T)
-
-    evens = [(i, i + 1) for i in range(0, tile_count - 1, 2)]
-    odds = [(i, i + 1) for i in range(1, tile_count - 1, 2)]
-    edge_a = lax.ppermute(edge_a, "tile", evens + [(j, i) for i, j in evens])
-    edge_b = lax.ppermute(edge_b, "tile", odds + [(j, i) for i, j in odds])
+        name="coupling",
+    )(footprints, support)
 
     row_filter, col_filter = filter_bands(tile_rows, columns)
-    new_traces, rounded, leftover = pl.pallas_call(
-        functools.partial(kernel_frames, tile_count),
+    new_traces, rounded, cleaned = pl.pallas_call(
+        functools.partial(kernel_traces, tile_count),
         out_shape=[
             jax.ShapeDtypeStruct((frames, components), jnp.float32),
             jax.ShapeDtypeStruct((frames, components), jnp.bfloat16),
-            jax.ShapeDtypeStruct((frames, tile_rows, columns), jnp.bfloat16),
+            lined_shape,
         ],
-        in_specs=[VMEM] * 4 + [ANY] + [VMEM] * 8,
+        in_specs=[VMEM] * 13,
         out_specs=[VMEM] * 3,
-        scratch_shapes=[
-            lined,
-            lined,
-            pltpu.VMEM(footprints.shape, footprints.dtype),
-            pltpu.VMEM((components, pixels), jnp.bfloat16),
-            pltpu.SemaphoreType.DMA((tile_rows // BR,)),
-        ],
-        compiler_params=pltpu.CompilerParams(vmem_limit_bytes=48 << 20),
+        compiler_params=pltpu.CompilerParams(vmem_limit_bytes=20 << 20),
         cost_estimate=pl.CostEstimate(
-            flops=8 * frames * pixels * components,
-            bytes_accessed=4 * pixels * components,
+            flops=4 * frames * pixels * components,
+            bytes_accessed=2 * pixels * components,
             transcendentals=0,
         ),
-        name="frames",
+        name="traces",
     )(
         strip_movie,
-        fitted,
+        first,
         edge_a,
         edge_b,
         footprints,
@@ -444,6 +449,20 @@
         row_filter,
         col_filter,
     )
+    leftover = pl.pallas_call(
+        kernel_refit,
+        out_shape=jax.ShapeDtypeStruct((frames, tile_rows, columns), jnp.bfloat16),
+        in_specs=[VMEM] * 3,
+        out_specs=VMEM,
+        scratch_shapes=[lined],
+        compiler_params=pltpu.CompilerParams(vmem_limit_bytes=20 << 20),
+        cost_estimate=pl.CostEstimate(
+            flops=2 * frames * pixels * components,
+            bytes_accessed=2 * pixels * components,
+            transcendentals=0,
+        ),
+        name="refit",
+    )(rounded, turned, cleaned)
 
     frame_count = lax.axis_size("frame")
     all_traces = [rounded] + [

time: 59.2 us -> 50.9 us (0.86)
  starting transfers between devices: 21.4 us -> 17.3 us
  Pallas kernels: 22.9 us -> 20.1 us
  local copies, waits for them, and re-layouts: 8.56 us -> 6.49 us
    all_to_all x1, starting transfers between devices: 9.34 us -> 3.41 us  [per_device(): lax.all_to_all(leftover, 'tile', split_axis=0, concat_axis=0, tiled=True)]
    pallas_call x3 -> x4, Pallas kernels: 21.1 us -> 18.3 us  [the longest x1 6.44 us: per_device(): pl.pallas_call(kernel_fitted, out_shape=[jax.ShapeDtypeStruct((frames, ti...]
    all_to_all x1, waiting for transfers between devices: 0.01 us -> 2.42 us  [per_device(): lax.all_to_all(pieces, 'tile', split_axis=0, concat_axis=0, tiled=True)]
    unnamed x27 -> x23, local copies, waits for them, and re-layouts: 8.56 us -> 6.49 us
    ppermute x2, starting transfers between devices: 2.92 us -> 4.68 us  [the longest x1 3.83 us: per_device(): lax.ppermute(jnp.where(odd, top, bottom), 'tile', evens + [(j, i) for i,...]
    ppermute x2, waiting for transfers between devices: 1.76 us -> 0.01 us  [the longest x1 0.01 us: per_device(): lax.ppermute(jnp.where(odd, bottom, top), 'tile', odds + [(j, i) for i, j...]
  transfers between devices with their start and end apart: 7 -> 7, of which waited for: 4 -> 4; matrix products, arithmetic and copies ran while one was open for 0% -> 0% of each run, Pallas kernels for 19% -> 26%
where the time goes in v3:
time: 50.9 us; the launch traced here: 50.4 us
  Pallas kernels  20.1 us (39%)
  starting transfers between devices  17.3 us (34%)
  local copies, waits for them, and re-layouts  6.49 us (13%)
  waiting for transfers between devices  5.65 us (11%)
  between operations  0.79 us (2%)
    all_to_all x1, starting transfers between devices, per_device(): lax.all_to_all(pieces, 'tile', split_axis=0, concat_axis=0, tiled=True)  7.29 us
    unnamed x23, local copies, waits for them, and re-layouts  6.49 us
    pallas_call x1, Pallas kernels, per_device(): pl.pallas_call(kernel_fitted, out_shape=[jax.ShapeDtypeStruct((frames, ti...  6.44 us
    pallas_call x1, Pallas kernels, per_device(): pl.pallas_call(kernel_coupling, out_shape=[jax.ShapeDtypeStruct((componen...  4.67 us
    pallas_call x1, Pallas kernels, per_device(): pl.pallas_call(functools.partial(kernel_traces, tile_count), out_shape=[j...  4.53 us
    ppermute x1, starting transfers between devices, per_device(): lax.ppermute(jnp.where(odd, top, bottom), 'tile', evens + [(j, i) for i,...  3.83 us
    all_to_all x1, starting transfers between devices, per_device(): lax.all_to_all(leftover, 'tile', split_axis=0, concat_axis=0, tiled=True)  3.41 us
    pallas_call x1, Pallas kernels, per_device(): pl.pallas_call(kernel_refit, out_shape=jax.ShapeDtypeStruct((frames, tile...  2.62 us
  transfers between devices with their start and end apart: 7, of which 4 were waited for; matrix products, arithmetic and copies ran while one was open for 0% of the time, Pallas kernels for 26%

profile of v3, /device:TPU:0, one launch (start us, length us, event | category | flops | bytes accessed | tf_op | source)
XLA Modules:
  0.0 50.4 jit_solution(510990936231824691)
XLA Ops:
  0.6 7.3 %all-to-all-start = ((bf16[8,64,256]{2,1,0:T(8,128)(2,1)}), bf16[8,64,256]{2,1,0:T(8,128)(2,1)S(1)}, u32[]{:S(2)}, u32[]{:S(2)}) async-start(bf16[8,64,256]{2,1,0:T(8,128)(2,1)} %bitcast.8), calls=%async_computation | async-start | bytes 524288 | tf_op jit(solution)/shard_map/all_to_all | solution.py:356
  7.9 6.4 %fitted.1 = (f32[8,64,256]{2,1,0:T(8,128)S(1)}, bf16[512,256]{1,0:T(8,128)(2,1)S(1)}, bf16[128,128]{1,0:T(8,128)(2,1)S(1)}) custom-call(bf16[64,256,384]{2,1,0:T(8,128)(2,1)} %footprints_ref.3, s32[8,384]{1,0:T(8,128)} %support_ref.3, bf16[8,384]{1,0:T(8,128)(2,1)} %bitcast.5, s32[2,64]{1,0:T(2,128)} %bitcast.9), custom_call_target="tpu_custom_call" | custom-call | flops 100663296 | bytes 12582912 | tf_op jit(solution)/shard_map/fitted/pallas_call | solution.py:363
  14.4 0.0 copy-start.2
  14.4 0.0 copy-start.3
  14.4 0.0 copy-start.4
  14.4 2.4 %all-to-all-done.movie_ref = bf16[8,64,256]{2,1,0:T(8,128)(2,1)S(1)} async-done(((bf16[8,64,256]{2,1,0:T(8,128)(2,1)}), bf16[8,64,256]{2,1,0:T(8,128)(2,1)S(1)}, u32[]{:S(2)}, u32[]{:S(2)}) %all-to-all-start) | async-done | bytes 262176 | tf_op jit(solution)/shard_map/all_to_all | solution.py:356
  16.9 0.1 subtract_convert_fusion.first_ref
  16.9 0.8 %collective-permute-start.1 = (bf16[8,24,256]{2,1,0:T(8,128)(2,1)S(1)}, bf16[8,24,256]{2,1,0:T(8,128)(2,1)S(1)}, u32[]{:S(2)}, u32[]{:S(2)}) collective-permute-start(bf16[8,24,256]{2,1,0:T(8,128)(2,1)S(1)} %get-tuple-element.19), channel_id=1, source_target_pairs={{4,8},{12,16},{20,24},{8,4},{16,12},{24,20},{5,9},{13,17},{21,25},... | collective-permute-start | bytes 294920 | tf_op jit(solution)/shard_map/ppermute | solution.py:399
  17.8 3.8 %collective-permute-start = (bf16[8,24,256]{2,1,0:T(8,128)(2,1)S(1)}, bf16[8,24,256]{2,1,0:T(8,128)(2,1)S(1)}, u32[]{:S(2)}, u32[]{:S(2)}) collective-permute-start(bf16[8,24,256]{2,1,0:T(8,128)(2,1)S(1)} %get-tuple-element.20), channel_id=1, source_target_pairs={{0,4},{8,12},{16,20},{24,28},{4,0},{12,8},{20,16},{28,24},{1,5},{9... | collective-permute-start | bytes 294920 | tf_op jit(solution)/shard_map/ppermute | solution.py:396
  21.6 4.6 %copy-done = bf16[64,256,384]{2,1,0:T(8,128)(2,1)S(1)} copy-done((bf16[64,256,384]{2,1,0:T(8,128)(2,1)S(1)}, bf16[64,256,384]{2,1,0:T(8,128)(2,1)}, u32[]{:S(2)}) %copy-start) | copy-done | bytes 12582936
  26.2 4.7 %coupling.1 = (bf16[384,16384]{1,0:T(8,128)(2,1)S(1)}, f32[384,384]{1,0:T(8,128)S(1)}) custom-call(bf16[64,256,384]{2,1,0:T(8,128)(2,1)S(1)} %copy-done, s32[8,384]{1,0:T(8,128)S(1)} %copy-done.5), custom_call_target="tpu_custom_call" | custom-call | flops 4831838208 | bytes 25165824 | tf_op jit(solution)/shard_map/coupling/pallas_call | solution.py:403
  31.0 4.5 %traces.1 = (f32[8,384]{1,0:T(8,128)}, bf16[8,384]{1,0:T(8,128)(2,1)S(1)}, f32[2,512,128]{2,1,0:T(8,128)S(1)}) custom-call(bf16[8,64,256]{2,1,0:T(8,128)(2,1)S(1)} %all-to-all-done.movie_ref, bf16[8,64,256]{2,1,0:T(8,128)(2,1)S(1)} %subtract_convert_fusion.first_ref, bf16[8,24,256]{2,1,0:T(8,128)(2,1)S(1)} %collective-permute-done.edge_a_ref, ...), custom_call_target="tpu_custom_call" | custom-call | flops 201326592 | bytes 12582912 | tf_op jit(solution)/shard_map/traces/pallas_call | solution.py:421
  35.5 2.6 %refit.1 = bf16[8,64,256]{2,1,0:T(8,128)(2,1)} custom-call(bf16[8,384]{1,0:T(8,128)(2,1)S(1)} %get-tuple-element.16.refs_0_.rounded_ref, bf16[384,16384]{1,0:T(8,128)(2,1)S(1)} %get-tuple-element.17.turned_ref, f32[2,512,128]{2,1,0:T(8,128)S(1)} %get-tuple-element.18.cleaned_ref), custom_call_target="tpu_custom_call" | custom-call | flops 100663296 | bytes 12582912 | tf_op jit(solution)/shard_map/refit/pallas_call | solution.py:452
  38.1 3.4 %all-to-all-start.1 = ((bf16[8,64,256]{2,1,0:T(8,128)(2,1)}), bf16[8,64,256]{2,1,0:T(8,128)(2,1)S(1)}, u32[]{:S(2)}, u32[]{:S(2)}) async-start(bf16[8,64,256]{2,1,0:T(8,128)(2,1)} %refit.1), calls=%async_computation.1 | async-start | bytes 524288 | tf_op jit(solution)/shard_map/all_to_all | solution.py:471
  41.5 0.1 collective-permute-start.4
  41.6 1.6 %collective-permute-start.3 = (bf16[8,384]{1,0:T(8,128)(2,1)S(1)}, bf16[8,384]{1,0:T(8,128)(2,1)S(1)}, u32[]{:S(2)}, u32[]{:S(2)}) collective-permute-start(bf16[8,384]{1,0:T(8,128)(2,1)S(1)} %get-tuple-element.16.refs_0_.rounded_ref), channel_id=1, source_target_pairs={{0,2},{1,3},{2,0},{3,1},{4,6},{5,7},{6,4},{7,5},{8,10},{9,11},{10,... | collective-permute-start | bytes 18440 | tf_op jit(solution)/shard_map/ppermute | solution.py:469
  43.2 0.3 collective-permute-start.2
  43.5 1.2 %collective-permute-done.4.refs_3_ = bf16[8,384]{1,0:T(8,128)(2,1)S(1)} collective-permute-done((bf16[8,384]{1,0:T(8,128)(2,1)S(1)}, bf16[8,384]{1,0:T(8,128)(2,1)S(1)}, u32[]{:S(2)}, u32[]{:S(2)}) %collective-permute-start.4) | collective-permute-done | bytes 6176 | tf_op jit(solution)/shard_map/ppermute | solution.py:469
  44.7 0.6 %collective-permute-done.3.refs_2_ = bf16[8,384]{1,0:T(8,128)(2,1)S(1)} collective-permute-done((bf16[8,384]{1,0:T(8,128)(2,1)S(1)}, bf16[8,384]{1,0:T(8,128)(2,1)S(1)}, u32[]{:S(2)}, u32[]{:S(2)}) %collective-permute-start.3) | collective-permute-done | bytes 6176 | tf_op jit(solution)/shard_map/ppermute | solution.py:469
  45.3 0.6 %copy-done.9 = bf16[8,384]{1,0:T(8,128)(2,1)} copy-done((bf16[8,384]{1,0:T(8,128)(2,1)}, bf16[8,384]{1,0:T(8,128)(2,1)S(1)}, u32[]{:S(2)}) %copy-start.9) | copy-done | bytes 6168
  45.9 0.6 %copy-done.10 = bf16[8,384]{1,0:T(8,128)(2,1)} copy-done((bf16[8,384]{1,0:T(8,128)(2,1)}, bf16[8,384]{1,0:T(8,128)(2,1)S(1)}, u32[]{:S(2)}) %copy-start.10) | copy-done | bytes 6168
  46.5 1.8 %gram.1 = f32[384,384]{1,0:T(8,128)} custom-call(bf16[8,384]{1,0:T(8,128)(2,1)} %copy-done.7, bf16[8,384]{1,0:T(8,128)(2,1)} %copy-done.10, bf16[8,384]{1,0:T(8,128)(2,1)} %copy-done.9, bf16[8,384]{1,0:T(8,128)(2,1)} %copy-done.8), custom_call_target="tpu_custom_call" | custom-call | tf_op jit(solution)/shard_map/gram/pallas_call | solution.py:477
  48.3 1.4 %all-to-all-done.1 = bf16[8,64,256]{2,1,0:T(8,128)(2,1)S(1)} async-done(((bf16[8,64,256]{2,1,0:T(8,128)(2,1)}), bf16[8,64,256]{2,1,0:T(8,128)(2,1)S(1)}, u32[]{:S(2)}, u32[]{:S(2)}) %all-to-all-start.1) | async-done | bytes 262176 | tf_op jit(solution)/shard_map/all_to_all | solution.py:471
  49.7 0.7 %copy.12 = bf16[1,512,256]{2,1,0:T(8,128)(2,1)} copy(bf16[1,512,256]{2,1,0:T(8,128)(2,1)S(1)} %bitcast.7) | data formatting | bytes 524288
  (20 shorter events, 0.1 us)
Async XLA Ops:
  0.6 21.0 %copy-start.5 = (s32[8,384]{1,0:T(8,128)S(1)}, s32[8,384]{1,0:T(8,128)}, u32[]{:S(2)}) copy-start(s32[8,384]{1,0:T(8,128)} %support_ref.3) | copy-start | bytes 36868
  0.6 16.2 %all-to-all-start = ((bf16[8,64,256]{2,1,0:T(8,128)(2,1)}), bf16[8,64,256]{2,1,0:T(8,128)(2,1)S(1)}, u32[]{:S(2)}, u32[]{:S(2)}) async-start(bf16[8,64,256]{2,1,0:T(8,128)(2,1)} %bitcast.8), calls=%async_computation | async-start | bytes 524288 | tf_op jit(solution)/shard_map/all_to_all | solution.py:356
  14.4 16.5 %copy-start.2 = (bf16[768,256]{1,0:T(8,128)(2,1)S(1)}, bf16[768,256]{1,0:T(8,128)(2,1)}, u32[]{:S(2)}) copy-start(bf16[768,256]{1,0:T(8,128)(2,1)} %constant.25.clone.col_filter_ref) | copy-start | bytes 1179652
  14.4 16.5 %copy-start.3 = (f32[64,256]{1,0:T(8,128)S(1)}, f32[64,256]{1,0:T(8,128)}, u32[]{:S(2)}) copy-start(f32[64,256]{1,0:T(8,128)} %weight_ref.1) | copy-start | bytes 196612
  14.4 16.5 %copy-start.4 = (bf16[96,224]{1,0:T(8,128)(2,1)S(1)}, bf16[96,224]{1,0:T(8,128)(2,1)}, u32[]{:S(2)}) copy-start(bf16[96,224]{1,0:T(8,128)(2,1)} %constant.24.clone.row_filter_ref) | copy-start | bytes 129028
  14.4 16.5 %copy-start.6 = (bf16[384,8]{0,1:T(8,128)(2,1)S(1)}, bf16[384,8]{0,1:T(8,128)(2,1)}, u32[]{:S(2)}) copy-start(bf16[384,8]{0,1:T(8,128)(2,1)} %param.11) | copy-start | bytes 18436
  16.9 13.9 %collective-permute-start.1 = (bf16[8,24,256]{2,1,0:T(8,128)(2,1)S(1)}, bf16[8,24,256]{2,1,0:T(8,128)(2,1)S(1)}, u32[]{:S(2)}, u32[]{:S(2)}) collective-permute-start(bf16[8,24,256]{2,1,0:T(8,128)(2,1)S(1)} %get-tuple-element.19), channel_id=1, source_target_pairs={{4,8},{12,16},{20,24},{8,4},{16,12},{24,20},{5,9},{13,17},{21,25},... | collective-permute-start | bytes 294920 | tf_op jit(solution)/shard_map/ppermute | solution.py:399
  17.8 13.1 %collective-permute-start = (bf16[8,24,256]{2,1,0:T(8,128)(2,1)S(1)}, bf16[8,24,256]{2,1,0:T(8,128)(2,1)S(1)}, u32[]{:S(2)}, u32[]{:S(2)}) collective-permute-start(bf16[8,24,256]{2,1,0:T(8,128)(2,1)S(1)} %get-tuple-element.20), channel_id=1, source_target_pairs={{0,4},{8,12},{16,20},{24,28},{4,0},{12,8},{20,16},{28,24},{1,5},{9... | collective-permute-start | bytes 294920 | tf_op jit(solution)/shard_map/ppermute | solution.py:396
  21.6 4.6 %copy-start = (bf16[64,256,384]{2,1,0:T(8,128)(2,1)S(1)}, bf16[64,256,384]{2,1,0:T(8,128)(2,1)}, u32[]{:S(2)}) copy-start(bf16[64,256,384]{2,1,0:T(8,128)(2,1)} %footprints_ref.3) | copy-start | bytes 37748740
  26.2 4.7 %copy-start.1 = (bf16[64,256,384]{2,1,0:T(8,128)(2,1)S(1)}, bf16[64,256,384]{2,1,0:T(8,128)(2,1)}, u32[]{:S(2)}) copy-start(bf16[64,256,384]{2,1,0:T(8,128)(2,1)} %footprints_ref.3) | copy-start | bytes 37748740
  35.5 9.8 %copy-start.7 = (bf16[8,384]{1,0:T(8,128)(2,1)}, bf16[8,384]{1,0:T(8,128)(2,1)S(1)}, u32[]{:S(2)}) copy-start(bf16[8,384]{1,0:T(8,128)(2,1)S(1)} %get-tuple-element.16.refs_0_.rounded_ref) | copy-start | bytes 18436
  38.1 11.6 %all-to-all-start.1 = ((bf16[8,64,256]{2,1,0:T(8,128)(2,1)}), bf16[8,64,256]{2,1,0:T(8,128)(2,1)S(1)}, u32[]{:S(2)}, u32[]{:S(2)}) async-start(bf16[8,64,256]{2,1,0:T(8,128)(2,1)} %refit.1), calls=%async_computation.1 | async-start | bytes 524288 | tf_op jit(solution)/shard_map/all_to_all | solution.py:471
  41.5 3.1 %collective-permute-start.4 = (bf16[8,384]{1,0:T(8,128)(2,1)S(1)}, bf16[8,384]{1,0:T(8,128)(2,1)S(1)}, u32[]{:S(2)}, u32[]{:S(2)}) collective-permute-start(bf16[8,384]{1,0:T(8,128)(2,1)S(1)} %get-tuple-element.16.refs_0_.rounded_ref), channel_id=1, source_target_pairs={{0,3},{1,2},{2,1},{3,0},{4,7},{5,6},{6,5},{7,4},{8,11},{9,10},{10,... | collective-permute-start | bytes 18440 | tf_op jit(solution)/shard_map/ppermute | solution.py:469
  41.6 3.7 %collective-permute-start.3 = (bf16[8,384]{1,0:T(8,128)(2,1)S(1)}, bf16[8,384]{1,0:T(8,128)(2,1)S(1)}, u32[]{:S(2)}, u32[]{:S(2)}) collective-permute-start(bf16[8,384]{1,0:T(8,128)(2,1)S(1)} %get-tuple-element.16.refs_0_.rounded_ref), channel_id=1, source_target_pairs={{0,2},{1,3},{2,0},{3,1},{4,6},{5,7},{6,4},{7,5},{8,10},{9,11},{10,... | collective-permute-start | bytes 18440 | tf_op jit(solution)/shard_map/ppermute | solution.py:469
  43.2 2.1 %collective-permute-start.2 = (bf16[8,384]{1,0:T(8,128)(2,1)S(1)}, bf16[8,384]{1,0:T(8,128)(2,1)S(1)}, u32[]{:S(2)}, u32[]{:S(2)}) collective-permute-start(bf16[8,384]{1,0:T(8,128)(2,1)S(1)} %get-tuple-element.16.refs_0_.rounded_ref), channel_id=1, source_target_pairs={{0,1},{1,0},{2,3},{3,2},{4,5},{5,4},{6,7},{7,6},{8,9},{9,8},{10,11... | collective-permute-start | bytes 18440 | tf_op jit(solution)/shard_map/ppermute | solution.py:469
  44.7 0.7 %copy-start.8 = (bf16[8,384]{1,0:T(8,128)(2,1)}, bf16[8,384]{1,0:T(8,128)(2,1)S(1)}, u32[]{:S(2)}) copy-start(bf16[8,384]{1,0:T(8,128)(2,1)S(1)} %collective-permute-done.4.refs_3_) | copy-start | bytes 18436
  45.3 0.6 %copy-start.9 = (bf16[8,384]{1,0:T(8,128)(2,1)}, bf16[8,384]{1,0:T(8,128)(2,1)S(1)}, u32[]{:S(2)}) copy-start(bf16[8,384]{1,0:T(8,128)(2,1)S(1)} %collective-permute-done.3.refs_2_) | copy-start | bytes 18436
  45.9 0.6 %copy-start.10 = (bf16[8,384]{1,0:T(8,128)(2,1)}, bf16[8,384]{1,0:T(8,128)(2,1)S(1)}, u32[]{:S(2)}) copy-start(bf16[8,384]{1,0:T(8,128)(2,1)S(1)} %collective-permute-done.2.refs_1_) | copy-start | bytes 18436

commit v4 on v3

--- a/solution.py
+++ b/solution.py
@@ -17,6 +17,7 @@
 HALO = 24
 LANES = 128
 AHEAD = 3
+EARLY = 7
 VMEM = pl.BlockSpec(memory_space=pltpu.VMEM)
 HBM = pl.BlockSpec(memory_space=pltpu.HBM)
 
@@ -88,35 +89,23 @@
         )
 
 
-class Footprints:
-    def __init__(self, source, target, arrived):
-        self.copies = []
-        for b in range(target.shape[0] // BR):
-            rows = pl.ds(b * BR, BR)
-            self.copies.append(
-                pltpu.make_async_copy(source.at[rows], target.at[rows], arrived.at[b])
-            )
-        for copy in self.copies[:AHEAD]:
-            copy.start()
-
-    def wait(self, b):
-        self.copies[b].wait()
-        if b + AHEAD < len(self.copies):
-            self.copies[b + AHEAD].start()
+def block_copies(source, target, arrived, first=0):
+    return [
+        pltpu.make_async_copy(
+            source.at[pl.ds((first + b) * BR, BR)], target.at[pl.ds(b * BR, BR)], arrived.at[b]
+        )
+        for b in range(target.shape[0] // BR)
+    ]
 
 
 def kernel_fitted(
     footprints_hbm,
     support_hbm,
     traces_hbm,
-    offsets_hbm,
     fitted_ref,
-    table_ref,
-    sides_ref,
     footprints_ref,
     support_ref,
     traces_ref,
-    offsets_ref,
     lined_ref,
     arrived,
     arrived_small,
@@ -125,7 +114,6 @@
         pltpu.make_async_copy(source, target, arrived_small.at[i])
         for i, (source, target) in enumerate(
             [
-                (offsets_hbm, offsets_ref),
                 (support_hbm, support_ref),
                 (traces_hbm, traces_ref),
             ]
@@ -133,17 +121,20 @@
     ]
     for copy in small:
         copy.start()
-    blocks = Footprints(footprints_hbm, footprints_ref, arrived)
+    copies = block_copies(footprints_hbm, footprints_ref, arrived)
+    for copy in copies[:AHEAD]:
+        copy.start()
     tile_rows, columns, components = footprints_ref.shape
     frames = traces_ref.shape[0]
     halves = columns // LANES
     block = BR * columns
     for copy in small:
         copy.wait()
-    border_tables(offsets_ref[...], table_ref, sides_ref)
     traces = traces_ref[...]
     for b in range(tile_rows // BR):
-        blocks.wait(b)
+        copies[b].wait()
+        if b + AHEAD < len(copies):
+            copies[b + AHEAD].start()
         fitted = lax.dot_general(
             traces * support_ref[b : b + 1, :].astype(jnp.bfloat16),
             footprints_ref[b * BR : (b + 1) * BR].reshape(block, components),
@@ -163,47 +154,38 @@
             ]
 
 
-def kernel_coupling(footprints_ref, support_ref, turned_ref, coupling_ref):
-    tile_rows, columns, components = footprints_ref.shape
-    block = BR * columns
-    split = components // 256 * 256
-    for b in range(tile_rows // BR):
-        mask = support_ref[b : b + 1, :].astype(jnp.bfloat16)
-        shaped = footprints_ref[b * BR : (b + 1) * BR].reshape(block, components) * mask
-        turned = shaped.T
-        turned_ref[:, b * block : (b + 1) * block] = turned
-        left = jnp.dot(turned, shaped[:, :split], preferred_element_type=jnp.float32)
-        right = jnp.dot(turned[split:], shaped[:, split:], preferred_element_type=jnp.float32)
-        if b == 0:
-            coupling_ref[:, :split] = left
-            coupling_ref[split:, split:] = right
-        else:
-            coupling_ref[:, :split] += left
-            coupling_ref[split:, split:] += right
-    coupling_ref[:split, split:] = coupling_ref[split:, :split].T
-
-
-def kernel_traces(
+def kernel_early(footprints_hbm, offsets_ref, early_ref, table_ref, sides_ref, arrived):
+    copies = block_copies(footprints_hbm, early_ref, arrived)
+    for copy in copies:
+        copy.start()
+    border_tables(offsets_ref[...], table_ref, sides_ref)
+    for copy in copies:
+        copy.wait()
+
+
+def kernel_background(
     tile_count,
     movie_ref,
     first_ref,
     edge_a_ref,
     edge_b_ref,
-    footprints_ref,
-    support_ref,
-    traces_ref,
+    footprints_hbm,
     weight_ref,
-    coupling_ref,
     table_ref,
     sides_ref,
     row_filter_ref,
     col_filter_ref,
-    new_traces_ref,
-    rounded_ref,
     cleaned_ref,
+    late_ref,
+    arrived,
 ):
-    tile_rows, columns, components = footprints_ref.shape
-    frames = traces_ref.shape[0]
+    tile_rows, columns, components = footprints_hbm.shape
+    copies = block_copies(
+        footprints_hbm, late_ref, arrived, (tile_rows - late_ref.shape[0]) // BR
+    )
+    for copy in copies:
+        copy.start()
+    frames = movie_ref.shape[0]
     halves = columns // LANES
     span = tile_rows + 2 * RR
     tile = lax.axis_index("tile")
@@ -259,22 +241,88 @@
                 :, half * LANES : (half + 1) * LANES
             ]
 
-    projected = jnp.zeros((frames, components), jnp.float32)
+    for copy in copies:
+        copy.wait()
+
+
+def kernel_coupling(
+    frames,
+    early_ref,
+    late_ref,
+    cleaned_ref,
+    support_ref,
+    stacked_ref,
+    coupling_ref,
+    projected_ref,
+    left_ref,
+    right_ref,
+):
+    columns, components = early_ref.shape[1:]
+    early = early_ref.shape[0] // BR
+    tile_rows = early_ref.shape[0] + late_ref.shape[0]
+    halves = columns // LANES
+    block = BR * columns
+    split = components // 256 * 256
+    spare = stacked_ref.shape[0] - components - frames
     for b in range(tile_rows // BR):
-        part = jnp.zeros((frames, components), jnp.float32)
-        for row in range(b * BR, (b + 1) * BR):
-            pixels = jnp.concatenate(
-                [
-                    cleaned_ref[half, pl.ds(row, frames, stride=tile_rows), :]
-                    for half in range(halves)
-                ],
-                axis=1,
-            ).astype(jnp.bfloat16)
-            part = part + jnp.dot(
-                pixels, footprints_ref[row], preferred_element_type=jnp.float32
-            )
-        projected = projected + part * support_ref[b : b + 1, :].astype(jnp.float32)
-
+        if b < early:
+            raw = early_ref[b * BR : (b + 1) * BR]
+        else:
+            raw = late_ref[(b - early) * BR : (b - early + 1) * BR]
+        shaped = raw.reshape(block, components) * support_ref[b : b + 1, :].astype(jnp.bfloat16)
+        pixels = slice(b * block, (b + 1) * block)
+        stacked_ref[:components, pixels] = shaped.T
+        cleaned = jnp.concatenate(
+            [
+                cleaned_ref[half, pl.ds(row, frames, stride=tile_rows), :]
+                for row in range(b * BR, (b + 1) * BR)
+                for half in range(halves)
+            ],
+            axis=1,
+        )
+        if spare:
+            cleaned = jnp.concatenate([cleaned, jnp.zeros((spare, block), jnp.float32)], axis=0)
+        stacked_ref[components:, pixels] = cleaned.astype(jnp.bfloat16)
+        left = jnp.dot(
+            stacked_ref[:, pixels], shaped[:, :split], preferred_element_type=jnp.float32
+        )
+        right = jnp.dot(
+            stacked_ref[split:, pixels], shaped[:, split:], preferred_element_type=jnp.float32
+        )
+        if b == 0:
+            left_ref[...] = left
+            right_ref[...] = right
+        else:
+            left_ref[...] += left
+            right_ref[...] += right
+    coupling_ref[:, :split] = left_ref[:components]
+    coupling_ref[split:, split:] = right_ref[: components - split]
+    coupling_ref[:split, split:] = left_ref[split:components].T
+    projected_ref[...] = jnp.concatenate(
+        [
+            left_ref[components : components + frames],
+            right_ref[components - split : components - split + frames],
+        ],
+        axis=1,
+    )
+
+
+def kernel_traces(
+    stacked_ref,
+    coupling_ref,
+    projected_ref,
+    traces_ref,
+    cleaned_ref,
+    new_traces_ref,
+    rounded_ref,
+    remainder_ref,
+    refit_ref,
+):
+    frames, tile_rows, columns = remainder_ref.shape
+    components = coupling_ref.shape[0]
+    halves = columns // LANES
+    block = BR * columns
+    projected = projected_ref[...]
     coupling = coupling_ref[...]
     diagonal = lax.broadcasted_iota(jnp.int32, coupling.shape, 0) == lax.broadcasted_iota(
         jnp.int32, coupling.shape, 1
@@ -298,16 +346,10 @@
     new_traces_ref[...] = state
     rounded_ref[...] = rounded
 
-
-def kernel_refit(rounded_ref, turned_ref, cleaned_ref, remainder_ref, refit_ref):
-    frames, tile_rows, columns = remainder_ref.shape
-    halves = columns // LANES
-    block = BR * columns
-    rounded = rounded_ref[...]
     for b in range(tile_rows // BR):
         refit = jnp.dot(
             rounded,
-            turned_ref[:, b * block : (b + 1) * block],
+            stacked_ref[:components, b * block : (b + 1) * block],
             preferred_element_type=jnp.float32,
         )
         for row in range(BR):
@@ -345,7 +387,6 @@
     pixels = tile_rows * columns
     halves = columns // LANES
     lined = pltpu.VMEM((halves, frames * tile_rows, LANES), jnp.float32)
-    lined_shape = jax.ShapeDtypeStruct(lined.shape, lined.dtype)
     blocks = tile_rows // BR
 
     pieces = (
@@ -358,25 +399,20 @@
     traces_rows = traces.T
     pinned = [
         pltpu.with_memory_space_constraint(array, pltpu.HBM)
-        for array in (footprints, support, traces_rows, border_offsets.T)
+        for array in (footprints, support, traces_rows)
     ]
-    fitted, table, sides = pl.pallas_call(
+    fitted = pl.pallas_call(
         kernel_fitted,
-        out_shape=[
-            jax.ShapeDtypeStruct((frames, tile_rows, columns), jnp.float32),
-            jax.ShapeDtypeStruct((2 * columns, columns), jnp.bfloat16),
-            jax.ShapeDtypeStruct((2 * tile_rows, LANES), jnp.bfloat16),
-        ],
-        in_specs=[HBM] * 4,
-        out_specs=[VMEM] * 3,
+        out_shape=jax.ShapeDtypeStruct((frames, tile_rows, columns), jnp.float32),
+        in_specs=[HBM] * 3,
+        out_specs=VMEM,
         scratch_shapes=[
             pltpu.VMEM(footprints.shape, footprints.dtype),
             pltpu.VMEM(support.shape, support.dtype),
             pltpu.VMEM(traces_rows.shape, traces.dtype),
-            pltpu.VMEM(border_offsets.shape[::-1], border_offsets.dtype),
             lined,
             pltpu.SemaphoreType.DMA((blocks,)),
-            pltpu.SemaphoreType.DMA((3,)),
+            pltpu.SemaphoreType.DMA((2,)),
         ],
         compiler_params=pltpu.CompilerParams(vmem_limit_bytes=24 << 20),
         cost_estimate=pl.CostEstimate(
@@ -400,69 +436,79 @@
         jnp.where(odd, bottom, top), "tile", odds + [(j, i) for i, j in odds]
     )
 
-    turned, coupling = pl.pallas_call(
-        kernel_coupling,
+    early = blocks * EARLY // 8
+    early_footprints, table, sides = pl.pallas_call(
+        kernel_early,
         out_shape=[
-            jax.ShapeDtypeStruct((components, pixels), jnp.bfloat16),
-            jax.ShapeDtypeStruct((components, components), jnp.float32),
-        ],
-        in_specs=[VMEM] * 2,
-        out_specs=[VMEM] * 2,
+            jax.ShapeDtypeStruct((early * BR, columns, components), footprints.dtype),
+            jax.ShapeDtypeStruct((2 * columns, columns), jnp.bfloat16),
+            jax.ShapeDtypeStruct((2 * tile_rows, LANES), jnp.bfloat16),
+        ],
+        in_specs=[HBM, VMEM],
+        out_specs=[VMEM] * 3,
+        scratch_shapes=[pltpu.SemaphoreType.DMA((early,))],
         compiler_params=pltpu.CompilerParams(vmem_limit_bytes=24 << 20),
         cost_estimate=pl.CostEstimate(
-            flops=2 * pixels * components * components,
-            bytes_accessed=4 * pixels * components,
-            transcendentals=0,
+            flops=0, bytes_accessed=4 * early * BR * columns * components, transcendentals=0
         ),
-        name="coupling",
-    )(footprints, support)
+        name="early",
+    )(pinned[0], border_offsets.T)
 
     row_filter, col_filter = filter_bands(tile_rows, columns)
-    new_traces, rounded, cleaned = pl.pallas_call(
-        functools.partial(kernel_traces, tile_count),
+    cleaned, late_footprints = pl.pallas_call(
+        functools.partial(kernel_background, tile_count),
         out_shape=[
-            jax.ShapeDtypeStruct((frames, components), jnp.float32),
-            jax.ShapeDtypeStruct((frames, components), jnp.bfloat16),
-            lined_shape,
-        ],
-        in_specs=[VMEM] * 13,
-        out_specs=[VMEM] * 3,
+            jax.ShapeDtypeStruct(lined.shape, lined.dtype),
+            jax.ShapeDtypeStruct((tile_rows - early * BR, columns, components), footprints.dtype),
+        ],
+        in_specs=[VMEM] * 4 + [HBM] + [VMEM] * 5,
+        out_specs=[VMEM] * 2,
+        scratch_shapes=[pltpu.SemaphoreType.DMA((blocks - early,))],
         compiler_params=pltpu.CompilerParams(vmem_limit_bytes=20 << 20),
-        cost_estimate=pl.CostEstimate(
-            flops=4 * frames * pixels * components,
-            bytes_accessed=2 * pixels * components,
-            transcendentals=0,
-        ),
-        name="traces",
+        name="background",
     )(
         strip_movie,
         first,
         edge_a,
         edge_b,
-        footprints,
-        support,
-        traces_rows,
+        pinned[0],
         border_weight,
-        coupling,
         table,
         sides,
         row_filter,
         col_filter,
     )
-    leftover = pl.pallas_call(
-        kernel_refit,
-        out_shape=jax.ShapeDtypeStruct((frames, tile_rows, columns), jnp.bfloat16),
-        in_specs=[VMEM] * 3,
-        out_specs=VMEM,
+    split = components // 256 * 256
+    height = -(-(components + frames) // 16) * 16
+    stacked, coupling, projected = pl.pallas_call(
+        functools.partial(kernel_coupling, frames),
+        out_shape=[
+            jax.ShapeDtypeStruct((height, pixels), jnp.bfloat16),
+            jax.ShapeDtypeStruct((components, components), jnp.float32),
+            jax.ShapeDtypeStruct((frames, components), jnp.float32),
+        ],
+        in_specs=[VMEM] * 4,
+        out_specs=[VMEM] * 3,
+        scratch_shapes=[
+            pltpu.VMEM((height, split), jnp.float32),
+            pltpu.VMEM((height - split, components - split), jnp.float32),
+        ],
+        compiler_params=pltpu.CompilerParams(vmem_limit_bytes=24 << 20),
+        name="coupling",
+    )(early_footprints, late_footprints, cleaned, support)
+    new_traces, rounded, leftover = pl.pallas_call(
+        kernel_traces,
+        out_shape=[
+            jax.ShapeDtypeStruct((frames, components), jnp.float32),
+            jax.ShapeDtypeStruct((frames, components), jnp.bfloat16),
+            jax.ShapeDtypeStruct((frames, tile_rows, columns), jnp.bfloat16),
+        ],
+        in_specs=[VMEM] * 5,
+        out_specs=[VMEM] * 3,
         scratch_shapes=[lined],
         compiler_params=pltpu.CompilerParams(vmem_limit_bytes=20 << 20),
-        cost_estimate=pl.CostEstimate(
-            flops=2 * frames * pixels * components,
-            bytes_accessed=2 * pixels * components,
-            transcendentals=0,
-        ),
-        name="refit",
-    )(rounded, turned, cleaned)
+        name="traces",
+    )(stacked, coupling, projected, traces_rows, cleaned)
 
     frame_count = lax.axis_size("frame")
     all_traces = [rounded] + [

time: 50.9 us -> 48.4 us (0.951)
  local copies, waits for them, and re-layouts: 6.49 us -> 1.91 us
  Pallas kernels: 20.1 us -> 22.2 us
    unnamed x23 -> x21, local copies, waits for them, and re-layouts: 6.49 us -> 1.91 us
    pallas_call x4 -> x5, Pallas kernels: 18.3 us -> 20.3 us  [the longest x1 6.15 us: per_device(): pl.pallas_call(kernel_fitted, out_shape=jax.ShapeDtypeStruct((frames, til...]
where the time goes in v4:
time: 48.4 us; the launch traced here: 48 us
  Pallas kernels  22.2 us (46%)
  starting transfers between devices  17.1 us (35%)
  waiting for transfers between devices  5.95 us (12%)
  local copies, waits for them, and re-layouts  1.91 us (4%)
  between operations  0.8 us (2%)
    all_to_all x1, starting transfers between devices, per_device(): lax.all_to_all(pieces, 'tile', split_axis=0, concat_axis=0, tiled=True)  7.29 us
    pallas_call x1, Pallas kernels, per_device(): pl.pallas_call(kernel_fitted, out_shape=jax.ShapeDtypeStruct((frames, til...  6.15 us
    pallas_call x1, Pallas kernels, per_device(): pl.pallas_call(functools.partial(kernel_coupling, frames), out_shape=[jax...  5.1 us
    pallas_call x1, Pallas kernels, per_device(): pl.pallas_call(kernel_early, out_shape=[jax.ShapeDtypeStruct((early * BR,...  4.3 us
    ppermute x1, starting transfers between devices, per_device(): lax.ppermute(jnp.where(odd, top, bottom), 'tile', evens + [(j, i) for i,...  3.83 us
    all_to_all x1, starting transfers between devices, per_device(): lax.all_to_all(leftover, 'tile', split_axis=0, concat_axis=0, tiled=True)  3.41 us
    pallas_call x1, Pallas kernels, per_device(): pl.pallas_call(kernel_traces, out_shape=[jax.ShapeDtypeStruct((frames, co...  3.18 us
    all_to_all x1, waiting for transfers between devices, per_device(): lax.all_to_all(pieces, 'tile', split_axis=0, concat_axis=0, tiled=True)  2.73 us
  transfers between devices with their start and end apart: 7, of which 4 were waited for; matrix products, arithmetic and copies ran while one was open for 0% of the time, Pallas kernels for 26%

profile of v4, /device:TPU:0, one launch (start us, length us, event | category | flops | bytes accessed | tf_op | source)
XLA Modules:
  0.0 48.0 jit_solution(7733448606367056045)
XLA Ops:
  0.6 7.3 %all-to-all-start = ((bf16[8,64,256]{2,1,0:T(8,128)(2,1)}), bf16[8,64,256]{2,1,0:T(8,128)(2,1)S(1)}, u32[]{:S(2)}, u32[]{:S(2)}) async-start(bf16[8,64,256]{2,1,0:T(8,128)(2,1)} %bitcast.9), calls=%async_computation | async-start | bytes 524288 | tf_op jit(solution)/shard_map/all_to_all | solution.py:397
  7.9 0.0 copy-start.1
  8.0 0.0 copy-start.2
  8.0 6.2 %fitted.1 = f32[8,64,256]{2,1,0:T(8,128)S(1)} custom-call(bf16[64,256,384]{2,1,0:T(8,128)(2,1)} %footprints_hbm.5, s32[8,384]{1,0:T(8,128)} %support_ref.1, bf16[8,384]{1,0:T(8,128)(2,1)} %bitcast.5), custom_call_target="tpu_custom_call" | custom-call | flops 100663296 | bytes 12582912 | tf_op jit(solution)/shard_map/fitted/pallas_call | solution.py:404
  14.1 2.7 %all-to-all-done.movie_ref = bf16[8,64,256]{2,1,0:T(8,128)(2,1)S(1)} async-done(((bf16[8,64,256]{2,1,0:T(8,128)(2,1)}), bf16[8,64,256]{2,1,0:T(8,128)(2,1)S(1)}, u32[]{:S(2)}, u32[]{:S(2)}) %all-to-all-start) | async-done | bytes 262176 | tf_op jit(solution)/shard_map/all_to_all | solution.py:397
  16.9 0.1 subtract_convert_fusion.first_ref
  17.0 0.7 %collective-permute-start.1 = (bf16[8,24,256]{2,1,0:T(8,128)(2,1)S(1)}, bf16[8,24,256]{2,1,0:T(8,128)(2,1)S(1)}, u32[]{:S(2)}, u32[]{:S(2)}) collective-permute-start(bf16[8,24,256]{2,1,0:T(8,128)(2,1)S(1)} %get-tuple-element.25), channel_id=1, source_target_pairs={{4,8},{12,16},{20,24},{8,4},{16,12},{24,20},{5,9},{13,17},{21,25},... | collective-permute-start | bytes 294920 | tf_op jit(solution)/shard_map/ppermute | solution.py:435
  17.6 3.8 %collective-permute-start = (bf16[8,24,256]{2,1,0:T(8,128)(2,1)S(1)}, bf16[8,24,256]{2,1,0:T(8,128)(2,1)S(1)}, u32[]{:S(2)}, u32[]{:S(2)}) collective-permute-start(bf16[8,24,256]{2,1,0:T(8,128)(2,1)S(1)} %get-tuple-element.26), channel_id=1, source_target_pairs={{0,4},{8,12},{16,20},{24,28},{4,0},{12,8},{20,16},{28,24},{1,5},{9... | collective-permute-start | bytes 294920 | tf_op jit(solution)/shard_map/ppermute | solution.py:432
  21.5 4.3 %early.1 = (bf16[56,256,384]{2,1,0:T(8,128)(2,1)S(1)}, bf16[512,256]{1,0:T(8,128)(2,1)S(1)}, bf16[128,128]{1,0:T(8,128)(2,1)S(1)}) custom-call(bf16[64,256,384]{2,1,0:T(8,128)(2,1)} %footprints_hbm.5, s32[2,64]{1,0:T(2,128)S(1)} %bitcast.7), custom_call_target="tpu_custom_call" | custom-call | bytes 22020096 | tf_op jit(solution)/shard_map/early/pallas_call | solution.py:440
  25.8 0.0 copy-start.4
  25.8 1.6 %background.1 = (f32[2,512,128]{2,1,0:T(8,128)S(1)}, bf16[8,256,384]{2,1,0:T(8,128)(2,1)S(1)}) custom-call(bf16[8,64,256]{2,1,0:T(8,128)(2,1)S(1)} %all-to-all-done.movie_ref, bf16[8,64,256]{2,1,0:T(8,128)(2,1)S(1)} %subtract_convert_fusion.first_ref, bf16[8,24,256]{2,1,0:T(8,128)(2,1)S(1)} %collective-permute-done.edge_a_ref, ...), custom_call_target="tpu_custom_call" | custom-call | tf_op jit(solution)/shard_map/background/pallas_call | solution.py:458
  27.5 5.1 %coupling.1 = (bf16[400,16384]{1,0:T(8,128)(2,1)S(1)}, f32[384,384]{1,0:T(8,128)S(1)}, f32[8,384]{1,0:T(8,128)S(1)}) custom-call(bf16[56,256,384]{2,1,0:T(8,128)(2,1)S(1)} %get-tuple-element.14.early_ref, bf16[8,256,384]{2,1,0:T(8,128)(2,1)S(1)} %get-tuple-element.17.late_ref, f32[2,512,128]{2,1,0:T(8,128)S(1)} %get-tuple-element.18.cleaned_ref, ...), custom_call_target="tpu_custom_call" | custom-call | tf_op jit(solution)/shard_map/coupling/pallas_call | solution.py:483
  32.6 3.2 %traces.1 = (f32[8,384]{1,0:T(8,128)}, bf16[8,384]{1,0:T(8,128)(2,1)S(1)}, bf16[8,64,256]{2,1,0:T(8,128)(2,1)}) custom-call(bf16[400,16384]{1,0:T(8,128)(2,1)S(1)} %get-tuple-element.19.stacked_ref, f32[384,384]{1,0:T(8,128)S(1)} %get-tuple-element.20.coupling_ref, f32[8,384]{1,0:T(8,128)S(1)} %get-tuple-element.21.projected_ref, ...), custom_call_target="tpu_custom_call" | custom-call | tf_op jit(solution)/shard_map/traces/pallas_call | solution.py:499
  35.8 3.4 %all-to-all-start.1 = ((bf16[8,64,256]{2,1,0:T(8,128)(2,1)}), bf16[8,64,256]{2,1,0:T(8,128)(2,1)S(1)}, u32[]{:S(2)}, u32[]{:S(2)}) async-start(bf16[8,64,256]{2,1,0:T(8,128)(2,1)} %get-tuple-element.24), calls=%async_computation.1 | async-start | bytes 524288 | tf_op jit(solution)/shard_map/all_to_all | solution.py:517
  39.2 0.1 collective-permute-start.4
  39.3 1.6 %collective-permute-start.3 = (bf16[8,384]{1,0:T(8,128)(2,1)S(1)}, bf16[8,384]{1,0:T(8,128)(2,1)S(1)}, u32[]{:S(2)}, u32[]{:S(2)}) collective-permute-start(bf16[8,384]{1,0:T(8,128)(2,1)S(1)} %get-tuple-element.23.refs_0_), channel_id=1, source_target_pairs={{0,2},{1,3},{2,0},{3,1},{4,6},{5,7},{6,4},{7,5},{8,10},{9,11},{10,... | collective-permute-start | bytes 18440 | tf_op jit(solution)/shard_map/ppermute | solution.py:515
  40.8 0.3 collective-permute-start.2
  41.1 1.2 %collective-permute-done.4.refs_3_ = bf16[8,384]{1,0:T(8,128)(2,1)S(1)} collective-permute-done((bf16[8,384]{1,0:T(8,128)(2,1)S(1)}, bf16[8,384]{1,0:T(8,128)(2,1)S(1)}, u32[]{:S(2)}, u32[]{:S(2)}) %collective-permute-start.4) | collective-permute-done | bytes 6176 | tf_op jit(solution)/shard_map/ppermute | solution.py:515
  42.3 0.6 %collective-permute-done.3.refs_2_ = bf16[8,384]{1,0:T(8,128)(2,1)S(1)} collective-permute-done((bf16[8,384]{1,0:T(8,128)(2,1)S(1)}, bf16[8,384]{1,0:T(8,128)(2,1)S(1)}, u32[]{:S(2)}, u32[]{:S(2)}) %collective-permute-start.3) | collective-permute-done | bytes 6176 | tf_op jit(solution)/shard_map/ppermute | solution.py:515
  43.0 0.6 %copy-done.8 = bf16[8,384]{1,0:T(8,128)(2,1)} copy-done((bf16[8,384]{1,0:T(8,128)(2,1)}, bf16[8,384]{1,0:T(8,128)(2,1)S(1)}, u32[]{:S(2)}) %copy-start.8) | copy-done | bytes 6168
  43.6 0.6 %copy-done.9 = bf16[8,384]{1,0:T(8,128)(2,1)} copy-done((bf16[8,384]{1,0:T(8,128)(2,1)}, bf16[8,384]{1,0:T(8,128)(2,1)S(1)}, u32[]{:S(2)}) %copy-start.9) | copy-done | bytes 6168
  44.1 1.8 %gram.1 = f32[384,384]{1,0:T(8,128)} custom-call(bf16[8,384]{1,0:T(8,128)(2,1)} %copy-done.5, bf16[8,384]{1,0:T(8,128)(2,1)} %copy-done.9, bf16[8,384]{1,0:T(8,128)(2,1)} %copy-done.8, bf16[8,384]{1,0:T(8,128)(2,1)} %copy-done.7), custom_call_target="tpu_custom_call" | custom-call | tf_op jit(solution)/shard_map/gram/pallas_call | solution.py:523
  46.0 1.4 %all-to-all-done.1 = bf16[8,64,256]{2,1,0:T(8,128)(2,1)S(1)} async-done(((bf16[8,64,256]{2,1,0:T(8,128)(2,1)}), bf16[8,64,256]{2,1,0:T(8,128)(2,1)S(1)}, u32[]{:S(2)}, u32[]{:S(2)}) %all-to-all-start.1) | async-done | bytes 262176 | tf_op jit(solution)/shard_map/all_to_all | solution.py:517
  47.3 0.7 %copy.12 = bf16[1,512,256]{2,1,0:T(8,128)(2,1)} copy(bf16[1,512,256]{2,1,0:T(8,128)(2,1)S(1)} %bitcast.8) | data formatting | bytes 524288
  (19 shorter events, 0.1 us)
Async XLA Ops:
  0.6 20.8 %copy-start.6 = (s32[64,2]{0,1:T(2,128)S(1)}, s32[64,2]{0,1:T(2,128)}, u32[]{:S(2)}) copy-start(s32[64,2]{0,1:T(2,128)} %param.13) | copy-start | bytes 1540
  0.6 16.2 %all-to-all-start = ((bf16[8,64,256]{2,1,0:T(8,128)(2,1)}), bf16[8,64,256]{2,1,0:T(8,128)(2,1)S(1)}, u32[]{:S(2)}, u32[]{:S(2)}) async-start(bf16[8,64,256]{2,1,0:T(8,128)(2,1)} %bitcast.9), calls=%async_computation | async-start | bytes 524288 | tf_op jit(solution)/shard_map/all_to_all | solution.py:397
  7.9 17.9 %copy-start = (bf16[768,256]{1,0:T(8,128)(2,1)S(1)}, bf16[768,256]{1,0:T(8,128)(2,1)}, u32[]{:S(2)}) copy-start(bf16[768,256]{1,0:T(8,128)(2,1)} %constant.25.clone.col_filter_ref) | copy-start | bytes 1179652
  7.9 17.9 %copy-start.1 = (f32[64,256]{1,0:T(8,128)S(1)}, f32[64,256]{1,0:T(8,128)}, u32[]{:S(2)}) copy-start(f32[64,256]{1,0:T(8,128)} %weight_ref.1) | copy-start | bytes 196612
  8.0 17.9 %copy-start.2 = (bf16[96,224]{1,0:T(8,128)(2,1)S(1)}, bf16[96,224]{1,0:T(8,128)(2,1)}, u32[]{:S(2)}) copy-start(bf16[96,224]{1,0:T(8,128)(2,1)} %constant.24.clone.row_filter_ref) | copy-start | bytes 129028
  17.0 8.8 %collective-permute-start.1 = (bf16[8,24,256]{2,1,0:T(8,128)(2,1)S(1)}, bf16[8,24,256]{2,1,0:T(8,128)(2,1)S(1)}, u32[]{:S(2)}, u32[]{:S(2)}) collective-permute-start(bf16[8,24,256]{2,1,0:T(8,128)(2,1)S(1)} %get-tuple-element.25), channel_id=1, source_target_pairs={{4,8},{12,16},{20,24},{8,4},{16,12},{24,20},{5,9},{13,17},{21,25},... | collective-permute-start | bytes 294920 | tf_op jit(solution)/shard_map/ppermute | solution.py:435
  17.6 8.2 %collective-permute-start = (bf16[8,24,256]{2,1,0:T(8,128)(2,1)S(1)}, bf16[8,24,256]{2,1,0:T(8,128)(2,1)S(1)}, u32[]{:S(2)}, u32[]{:S(2)}) collective-permute-start(bf16[8,24,256]{2,1,0:T(8,128)(2,1)S(1)} %get-tuple-element.26), channel_id=1, source_target_pairs={{0,4},{8,12},{16,20},{24,28},{4,0},{12,8},{20,16},{28,24},{1,5},{9... | collective-permute-start | bytes 294920 | tf_op jit(solution)/shard_map/ppermute | solution.py:432
  21.5 6.0 %copy-start.3 = (s32[8,384]{1,0:T(8,128)S(1)}, s32[8,384]{1,0:T(8,128)}, u32[]{:S(2)}) copy-start(s32[8,384]{1,0:T(8,128)} %support_ref.1) | copy-start | bytes 36868
  25.8 6.7 %copy-start.4 = (bf16[384,8]{0,1:T(8,128)(2,1)S(1)}, bf16[384,8]{0,1:T(8,128)(2,1)}, u32[]{:S(2)}) copy-start(bf16[384,8]{0,1:T(8,128)(2,1)} %param.11) | copy-start | bytes 18436
  35.8 7.2 %copy-start.5 = (bf16[8,384]{1,0:T(8,128)(2,1)}, bf16[8,384]{1,0:T(8,128)(2,1)S(1)}, u32[]{:S(2)}) copy-start(bf16[8,384]{1,0:T(8,128)(2,1)S(1)} %get-tuple-element.23.refs_0_) | copy-start | bytes 18436
  35.8 11.6 %all-to-all-start.1 = ((bf16[8,64,256]{2,1,0:T(8,128)(2,1)}), bf16[8,64,256]{2,1,0:T(8,128)(2,1)S(1)}, u32[]{:S(2)}, u32[]{:S(2)}) async-start(bf16[8,64,256]{2,1,0:T(8,128)(2,1)} %get-tuple-element.24), calls=%async_computation.1 | async-start | bytes 524288 | tf_op jit(solution)/shard_map/all_to_all | solution.py:517
  39.2 3.1 %collective-permute-start.4 = (bf16[8,384]{1,0:T(8,128)(2,1)S(1)}, bf16[8,384]{1,0:T(8,128)(2,1)S(1)}, u32[]{:S(2)}, u32[]{:S(2)}) collective-permute-start(bf16[8,384]{1,0:T(8,128)(2,1)S(1)} %get-tuple-element.23.refs_0_), channel_id=1, source_target_pairs={{0,3},{1,2},{2,1},{3,0},{4,7},{5,6},{6,5},{7,4},{8,11},{9,10},{10,... | collective-permute-start | bytes 18440 | tf_op jit(solution)/shard_map/ppermute | solution.py:515
  39.3 3.7 %collective-permute-start.3 = (bf16[8,384]{1,0:T(8,128)(2,1)S(1)}, bf16[8,384]{1,0:T(8,128)(2,1)S(1)}, u32[]{:S(2)}, u32[]{:S(2)}) collective-permute-start(bf16[8,384]{1,0:T(8,128)(2,1)S(1)} %get-tuple-element.23.refs_0_), channel_id=1, source_target_pairs={{0,2},{1,3},{2,0},{3,1},{4,6},{5,7},{6,4},{7,5},{8,10},{9,11},{10,... | collective-permute-start | bytes 18440 | tf_op jit(solution)/shard_map/ppermute | solution.py:515
  40.8 2.1 %collective-permute-start.2 = (bf16[8,384]{1,0:T(8,128)(2,1)S(1)}, bf16[8,384]{1,0:T(8,128)(2,1)S(1)}, u32[]{:S(2)}, u32[]{:S(2)}) collective-permute-start(bf16[8,384]{1,0:T(8,128)(2,1)S(1)} %get-tuple-element.23.refs_0_), channel_id=1, source_target_pairs={{0,1},{1,0},{2,3},{3,2},{4,5},{5,4},{6,7},{7,6},{8,9},{9,8},{10,11... | collective-permute-start | bytes 18440 | tf_op jit(solution)/shard_map/ppermute | solution.py:515
  42.3 0.7 %copy-start.7 = (bf16[8,384]{1,0:T(8,128)(2,1)}, bf16[8,384]{1,0:T(8,128)(2,1)S(1)}, u32[]{:S(2)}) copy-start(bf16[8,384]{1,0:T(8,128)(2,1)S(1)} %collective-permute-done.4.refs_3_) | copy-start | bytes 18436
  43.0 0.6 %copy-start.8 = (bf16[8,384]{1,0:T(8,128)(2,1)}, bf16[8,384]{1,0:T(8,128)(2,1)S(1)}, u32[]{:S(2)}) copy-start(bf16[8,384]{1,0:T(8,128)(2,1)S(1)} %collective-permute-done.3.refs_2_) | copy-start | bytes 18436
  43.6 0.6 %copy-start.9 = (bf16[8,384]{1,0:T(8,128)(2,1)}, bf16[8,384]{1,0:T(8,128)(2,1)S(1)}, u32[]{:S(2)}) copy-start(bf16[8,384]{1,0:T(8,128)(2,1)S(1)} %collective-permute-done.2.refs_1_) | copy-start | bytes 18436

commit v5 on v4

--- a/solution.py
+++ b/solution.py
@@ -17,7 +17,7 @@
 HALO = 24
 LANES = 128
 AHEAD = 3
-EARLY = 7
+LATE = 1
 VMEM = pl.BlockSpec(memory_space=pltpu.VMEM)
 HBM = pl.BlockSpec(memory_space=pltpu.HBM)
 
@@ -103,7 +103,8 @@
     support_hbm,
     traces_hbm,
     fitted_ref,
-    footprints_ref,
+    kept_ref,
+    others_ref,
     support_ref,
     traces_ref,
     lined_ref,
@@ -121,10 +122,16 @@
     ]
     for copy in small:
         copy.start()
-    copies = block_copies(footprints_hbm, footprints_ref, arrived)
+    tile_rows, columns, components = footprints_hbm.shape
+    others = others_ref.shape[0]
+    copies = block_copies(footprints_hbm, others_ref, arrived)
+    copies.append(
+        pltpu.make_async_copy(
+            footprints_hbm.at[pl.ds(others, BR)], kept_ref, arrived.at[len(copies)]
+        )
+    )
     for copy in copies[:AHEAD]:
         copy.start()
-    tile_rows, columns, components = footprints_ref.shape
     frames = traces_ref.shape[0]
     halves = columns // LANES
     block = BR * columns
@@ -135,9 +142,10 @@
         copies[b].wait()
         if b + AHEAD < len(copies):
             copies[b + AHEAD].start()
+        raw = kept_ref[...] if b * BR == others else others_ref[b * BR : (b + 1) * BR]
         fitted = lax.dot_general(
             traces * support_ref[b : b + 1, :].astype(jnp.bfloat16),
-            footprints_ref[b * BR : (b + 1) * BR].reshape(block, components),
+            raw.reshape(block, components),
             (((1,), (1,)), ((), ())),
             preferred_element_type=jnp.float32,
         )
@@ -179,13 +187,11 @@
     late_ref,
     arrived,
 ):
-    tile_rows, columns, components = footprints_hbm.shape
-    copies = block_copies(
-        footprints_hbm, late_ref, arrived, (tile_rows - late_ref.shape[0]) // BR
-    )
+    frames, tile_rows, columns = movie_ref.shape
+    late = tile_rows // BR - 1 - late_ref.shape[0] // BR
+    copies = block_copies(footprints_hbm, late_ref, arrived, late)
     for copy in copies:
         copy.start()
-    frames = movie_ref.shape[0]
     halves = columns // LANES
     span = tile_rows + 2 * RR
     tile = lax.axis_index("tile")
@@ -249,6 +255,7 @@
     frames,
     early_ref,
     late_ref,
+    kept_ref,
     cleaned_ref,
     support_ref,
     stacked_ref,
@@ -258,17 +265,15 @@
     right_ref,
 ):
     columns, components = early_ref.shape[1:]
-    early = early_ref.shape[0] // BR
-    tile_rows = early_ref.shape[0] + late_ref.shape[0]
+    parts = [(part, b) for part in (early_ref, late_ref, kept_ref) for b in range(part.shape[0] // BR)]
+    tile_rows = len(parts) * BR
     halves = columns // LANES
     block = BR * columns
     split = components // 256 * 256
     spare = stacked_ref.shape[0] - components - frames
     for b in range(tile_rows // BR):
-        if b < early:
-            raw = early_ref[b * BR : (b + 1) * BR]
-        else:
-            raw = late_ref[(b - early) * BR : (b - early + 1) * BR]
+        part, at = parts[b]
+        raw = part[at * BR : (at + 1) * BR]
         shaped = raw.reshape(block, components) * support_ref[b : b + 1, :].astype(jnp.bfloat16)
         pixels = slice(b * block, (b + 1) * block)
         stacked_ref[:components, pixels] = shaped.T
@@ -401,13 +406,16 @@
         pltpu.with_memory_space_constraint(array, pltpu.HBM)
         for array in (footprints, support, traces_rows)
     ]
-    fitted = pl.pallas_call(
+    fitted, kept_footprints = pl.pallas_call(
         kernel_fitted,
-        out_shape=jax.ShapeDtypeStruct((frames, tile_rows, columns), jnp.float32),
+        out_shape=[
+            jax.ShapeDtypeStruct((frames, tile_rows, columns), jnp.float32),
+            jax.ShapeDtypeStruct((BR, columns, components), footprints.dtype),
+        ],
         in_specs=[HBM] * 3,
-        out_specs=VMEM,
+        out_specs=[VMEM] * 2,
         scratch_shapes=[
-            pltpu.VMEM(footprints.shape, footprints.dtype),
+            pltpu.VMEM((tile_rows - BR, columns, components), footprints.dtype),
             pltpu.VMEM(support.shape, support.dtype),
             pltpu.VMEM(traces_rows.shape, traces.dtype),
             lined,
@@ -436,20 +444,21 @@
         jnp.where(odd, bottom, top), "tile", odds + [(j, i) for i, j in odds]
     )
 
-    early = blocks * EARLY // 8
+    late_rows = BR * LATE
+    early_rows = tile_rows - BR - late_rows
     early_footprints, table, sides = pl.pallas_call(
         kernel_early,
         out_shape=[
-            jax.ShapeDtypeStruct((early * BR, columns, components), footprints.dtype),
+            jax.ShapeDtypeStruct((early_rows, columns, components), footprints.dtype),
             jax.ShapeDtypeStruct((2 * columns, columns), jnp.bfloat16),
             jax.ShapeDtypeStruct((2 * tile_rows, LANES), jnp.bfloat16),
         ],
         in_specs=[HBM, VMEM],
         out_specs=[VMEM] * 3,
-        scratch_shapes=[pltpu.SemaphoreType.DMA((early,))],
+        scratch_shapes=[pltpu.SemaphoreType.DMA((early_rows // BR,))],
         compiler_params=pltpu.CompilerParams(vmem_limit_bytes=24 << 20),
         cost_estimate=pl.CostEstimate(
-            flops=0, bytes_accessed=4 * early * BR * columns * components, transcendentals=0
+            flops=0, bytes_accessed=4 * early_rows * columns * components, transcendentals=0
         ),
         name="early",
     )(pinned[0], border_offsets.T)
@@ -459,11 +468,11 @@
         functools.partial(kernel_background, tile_count),
         out_shape=[
             jax.ShapeDtypeStruct(lined.shape, lined.dtype),
-            jax.ShapeDtypeStruct((tile_rows - early * BR, columns, components), footprints.dtype),
+            jax.ShapeDtypeStruct((late_rows, columns, components), footprints.dtype),
         ],
         in_specs=[VMEM] * 4 + [HBM] + [VMEM] * 5,
         out_specs=[VMEM] * 2,
-        scratch_shapes=[pltpu.SemaphoreType.DMA((blocks - early,))],
+        scratch_shapes=[pltpu.SemaphoreType.DMA((LATE,))],
         compiler_params=pltpu.CompilerParams(vmem_limit_bytes=20 << 20),
         name="background",
     )(
@@ -487,7 +496,7 @@
             jax.ShapeDtypeStruct((components, components), jnp.float32),
             jax.ShapeDtypeStruct((frames, components), jnp.float32),
         ],
-        in_specs=[VMEM] * 4,
+        in_specs=[VMEM] * 5,
         out_specs=[VMEM] * 3,
         scratch_shapes=[
             pltpu.VMEM((height, split), jnp.float32),
@@ -495,7 +504,7 @@
         ],
         compiler_params=pltpu.CompilerParams(vmem_limit_bytes=24 << 20),
         name="coupling",
-    )(early_footprints, late_footprints, cleaned, support)
+    )(early_footprints, late_footprints, kept_footprints, cleaned, support)
     new_traces, rounded, leftover = pl.pallas_call(
         kernel_traces,
         out_shape=[

time: 48.4 us -> 47.9 us (0.990)
  Pallas kernels: 22.2 us -> 21.6 us
  transfers between devices with their start and end apart: 7 -> 7, of which waited for: 4 -> 4; matrix products, arithmetic and copies ran while one was open for 0% -> 0% of each run, Pallas kernels for 26% -> 25%
where the time goes in v5:
time: 47.9 us; the launch traced here: 47.5 us
  Pallas kernels  21.6 us (45%)
  starting transfers between devices  17.1 us (36%)
  waiting for transfers between devices  5.94 us (12%)
  local copies, waits for them, and re-layouts  1.92 us (4%)
  between operations  0.82 us (2%)
    all_to_all x1, starting transfers between devices, per_device(): lax.all_to_all(pieces, 'tile', split_axis=0, concat_axis=0, tiled=True)  7.29 us
    pallas_call x1, Pallas kernels, per_device(): pl.pallas_call(kernel_fitted, out_shape=[jax.ShapeDtypeStruct((frames, ti...  6.15 us
    pallas_call x1, Pallas kernels, per_device(): pl.pallas_call(functools.partial(kernel_coupling, frames), out_shape=[jax...  5.02 us
    pallas_call x1, Pallas kernels, per_device(): pl.pallas_call(kernel_early, out_shape=[jax.ShapeDtypeStruct((early_rows,...  3.84 us
    ppermute x1, starting transfers between devices, per_device(): lax.ppermute(jnp.where(odd, top, bottom), 'tile', evens + [(j, i) for i,...  3.83 us
    all_to_all x1, starting transfers between devices, per_device(): lax.all_to_all(leftover, 'tile', split_axis=0, concat_axis=0, tiled=True)  3.41 us
    pallas_call x1, Pallas kernels, per_device(): pl.pallas_call(kernel_traces, out_shape=[jax.ShapeDtypeStruct((frames, co...  3.19 us
    all_to_all x1, waiting for transfers between devices, per_device(): lax.all_to_all(pieces, 'tile', split_axis=0, concat_axis=0, tiled=True)  2.72 us
  transfers between devices with their start and end apart: 7, of which 4 were waited for; matrix products, arithmetic and copies ran while one was open for 0% of the time, Pallas kernels for 25%

profile of v5, /device:TPU:0, one launch (start us, length us, event | category | flops | bytes accessed | tf_op | source)
XLA Modules:
  0.0 47.5 jit_solution(1448707735945819581)
XLA Ops:
  0.6 7.3 %all-to-all-start = ((bf16[8,64,256]{2,1,0:T(8,128)(2,1)}), bf16[8,64,256]{2,1,0:T(8,128)(2,1)S(1)}, u32[]{:S(2)}, u32[]{:S(2)}) async-start(bf16[8,64,256]{2,1,0:T(8,128)(2,1)} %bitcast.9), calls=%async_computation | async-start | bytes 524288 | tf_op jit(solution)/shard_map/all_to_all | solution.py:402
  7.9 6.2 %fitted.1 = (f32[8,64,256]{2,1,0:T(8,128)S(1)}, bf16[8,256,384]{2,1,0:T(8,128)(2,1)S(1)}) custom-call(bf16[64,256,384]{2,1,0:T(8,128)(2,1)} %footprints_hbm.5, s32[8,384]{1,0:T(8,128)} %support_ref.1, bf16[8,384]{1,0:T(8,128)(2,1)} %bitcast.5), custom_call_target="tpu_custom_call" | custom-call | flops 100663296 | bytes 12582912 | tf_op jit(solution)/shard_map/fitted/pallas_call | solution.py:409
  14.1 0.0 copy-start
  14.1 0.0 copy-start.2
  14.1 2.7 %all-to-all-done.movie_ref = bf16[8,64,256]{2,1,0:T(8,128)(2,1)S(1)} async-done(((bf16[8,64,256]{2,1,0:T(8,128)(2,1)}), bf16[8,64,256]{2,1,0:T(8,128)(2,1)S(1)}, u32[]{:S(2)}, u32[]{:S(2)}) %all-to-all-start) | async-done | bytes 262176 | tf_op jit(solution)/shard_map/all_to_all | solution.py:402
  16.9 0.1 subtract_convert_fusion.first_ref
  17.0 0.7 %collective-permute-start.1 = (bf16[8,24,256]{2,1,0:T(8,128)(2,1)S(1)}, bf16[8,24,256]{2,1,0:T(8,128)(2,1)S(1)}, u32[]{:S(2)}, u32[]{:S(2)}) collective-permute-start(bf16[8,24,256]{2,1,0:T(8,128)(2,1)S(1)} %get-tuple-element.29), channel_id=1, source_target_pairs={{4,8},{12,16},{20,24},{8,4},{16,12},{24,20},{5,9},{13,17},{21,25},... | collective-permute-start | bytes 294920 | tf_op jit(solution)/shard_map/ppermute | solution.py:443
  17.6 3.8 %collective-permute-start = (bf16[8,24,256]{2,1,0:T(8,128)(2,1)S(1)}, bf16[8,24,256]{2,1,0:T(8,128)(2,1)S(1)}, u32[]{:S(2)}, u32[]{:S(2)}) collective-permute-start(bf16[8,24,256]{2,1,0:T(8,128)(2,1)S(1)} %get-tuple-element.30), channel_id=1, source_target_pairs={{0,4},{8,12},{16,20},{24,28},{4,0},{12,8},{20,16},{28,24},{1,5},{9... | collective-permute-start | bytes 294920 | tf_op jit(solution)/shard_map/ppermute | solution.py:440
  21.5 3.8 %early.1 = (bf16[48,256,384]{2,1,0:T(8,128)(2,1)S(1)}, bf16[512,256]{1,0:T(8,128)(2,1)S(1)}, bf16[128,128]{1,0:T(8,128)(2,1)S(1)}) custom-call(bf16[64,256,384]{2,1,0:T(8,128)(2,1)} %footprints_hbm.5, s32[2,64]{1,0:T(2,128)S(1)} %bitcast.7), custom_call_target="tpu_custom_call" | custom-call | bytes 18874368 | tf_op jit(solution)/shard_map/early/pallas_call | solution.py:449
  25.3 0.0 copy-start.3
  25.4 1.6 %background.1 = (f32[2,512,128]{2,1,0:T(8,128)S(1)}, bf16[8,256,384]{2,1,0:T(8,128)(2,1)S(1)}) custom-call(bf16[8,64,256]{2,1,0:T(8,128)(2,1)S(1)} %all-to-all-done.movie_ref, bf16[8,64,256]{2,1,0:T(8,128)(2,1)S(1)} %subtract_convert_fusion.first_ref, bf16[8,24,256]{2,1,0:T(8,128)(2,1)S(1)} %collective-permute-done.edge_a_ref, ...), custom_call_target="tpu_custom_call" | custom-call | tf_op jit(solution)/shard_map/background/pallas_call | solution.py:467
  27.0 5.0 %coupling.1 = (bf16[400,16384]{1,0:T(8,128)(2,1)S(1)}, f32[384,384]{1,0:T(8,128)S(1)}, f32[8,384]{1,0:T(8,128)S(1)}) custom-call(bf16[48,256,384]{2,1,0:T(8,128)(2,1)S(1)} %get-tuple-element.16.early_ref, bf16[8,256,384]{2,1,0:T(8,128)(2,1)S(1)} %get-tuple-element.20.late_ref, bf16[8,256,384]{2,1,0:T(8,128)(2,1)S(1)} %get-tuple-element.21.kept_ref, ...), custom_call_target="tpu_custom_call" | custom-call | tf_op jit(solution)/shard_map/coupling/pallas_call | solution.py:492
  32.1 3.2 %traces.1 = (f32[8,384]{1,0:T(8,128)}, bf16[8,384]{1,0:T(8,128)(2,1)S(1)}, bf16[8,64,256]{2,1,0:T(8,128)(2,1)}) custom-call(bf16[400,16384]{1,0:T(8,128)(2,1)S(1)} %get-tuple-element.23.stacked_ref, f32[384,384]{1,0:T(8,128)S(1)} %get-tuple-element.24.coupling_ref, f32[8,384]{1,0:T(8,128)S(1)} %get-tuple-element.25.projected_ref, ...), custom_call_target="tpu_custom_call" | custom-call | tf_op jit(solution)/shard_map/traces/pallas_call | solution.py:508
  35.2 3.4 %all-to-all-start.1 = ((bf16[8,64,256]{2,1,0:T(8,128)(2,1)}), bf16[8,64,256]{2,1,0:T(8,128)(2,1)S(1)}, u32[]{:S(2)}, u32[]{:S(2)}) async-start(bf16[8,64,256]{2,1,0:T(8,128)(2,1)} %get-tuple-element.28), calls=%async_computation.1 | async-start | bytes 524288 | tf_op jit(solution)/shard_map/all_to_all | solution.py:526
  38.7 0.1 collective-permute-start.4
  38.7 1.6 %collective-permute-start.3 = (bf16[8,384]{1,0:T(8,128)(2,1)S(1)}, bf16[8,384]{1,0:T(8,128)(2,1)S(1)}, u32[]{:S(2)}, u32[]{:S(2)}) collective-permute-start(bf16[8,384]{1,0:T(8,128)(2,1)S(1)} %get-tuple-element.27.refs_0_), channel_id=1, source_target_pairs={{0,2},{1,3},{2,0},{3,1},{4,6},{5,7},{6,4},{7,5},{8,10},{9,11},{10,... | collective-permute-start | bytes 18440 | tf_op jit(solution)/shard_map/ppermute | solution.py:524
  40.3 0.3 collective-permute-start.2
  40.6 1.2 %collective-permute-done.4.refs_3_ = bf16[8,384]{1,0:T(8,128)(2,1)S(1)} collective-permute-done((bf16[8,384]{1,0:T(8,128)(2,1)S(1)}, bf16[8,384]{1,0:T(8,128)(2,1)S(1)}, u32[]{:S(2)}, u32[]{:S(2)}) %collective-permute-start.4) | collective-permute-done | bytes 6176 | tf_op jit(solution)/shard_map/ppermute | solution.py:524
  41.8 0.6 %collective-permute-done.3.refs_2_ = bf16[8,384]{1,0:T(8,128)(2,1)S(1)} collective-permute-done((bf16[8,384]{1,0:T(8,128)(2,1)S(1)}, bf16[8,384]{1,0:T(8,128)(2,1)S(1)}, u32[]{:S(2)}, u32[]{:S(2)}) %collective-permute-start.3) | collective-permute-done | bytes 6176 | tf_op jit(solution)/shard_map/ppermute | solution.py:524
  42.5 0.6 %copy-done.8 = bf16[8,384]{1,0:T(8,128)(2,1)} copy-done((bf16[8,384]{1,0:T(8,128)(2,1)}, bf16[8,384]{1,0:T(8,128)(2,1)S(1)}, u32[]{:S(2)}) %copy-start.8) | copy-done | bytes 6168
  43.0 0.6 %copy-done.9 = bf16[8,384]{1,0:T(8,128)(2,1)} copy-done((bf16[8,384]{1,0:T(8,128)(2,1)}, bf16[8,384]{1,0:T(8,128)(2,1)S(1)}, u32[]{:S(2)}) %copy-start.9) | copy-done | bytes 6168
  43.6 1.8 %gram.1 = f32[384,384]{1,0:T(8,128)} custom-call(bf16[8,384]{1,0:T(8,128)(2,1)} %copy-done.5, bf16[8,384]{1,0:T(8,128)(2,1)} %copy-done.9, bf16[8,384]{1,0:T(8,128)(2,1)} %copy-done.8, bf16[8,384]{1,0:T(8,128)(2,1)} %copy-done.7), custom_call_target="tpu_custom_call" | custom-call | tf_op jit(solution)/shard_map/gram/pallas_call | solution.py:532
  45.5 1.4 %all-to-all-done.1 = bf16[8,64,256]{2,1,0:T(8,128)(2,1)S(1)} async-done(((bf16[8,64,256]{2,1,0:T(8,128)(2,1)}), bf16[8,64,256]{2,1,0:T(8,128)(2,1)S(1)}, u32[]{:S(2)}, u32[]{:S(2)}) %all-to-all-start.1) | async-done | bytes 262176 | tf_op jit(solution)/shard_map/all_to_all | solution.py:526
  46.8 0.7 %copy.12 = bf16[1,512,256]{2,1,0:T(8,128)(2,1)} copy(bf16[1,512,256]{2,1,0:T(8,128)(2,1)S(1)} %bitcast.8) | data formatting | bytes 524288
  (19 shorter events, 0.1 us)
Async XLA Ops:
  0.6 20.8 %copy-start.6 = (s32[64,2]{0,1:T(2,128)S(1)}, s32[64,2]{0,1:T(2,128)}, u32[]{:S(2)}) copy-start(s32[64,2]{0,1:T(2,128)} %param.13) | copy-start | bytes 1540
  0.6 16.2 %all-to-all-start = ((bf16[8,64,256]{2,1,0:T(8,128)(2,1)}), bf16[8,64,256]{2,1,0:T(8,128)(2,1)S(1)}, u32[]{:S(2)}, u32[]{:S(2)}) async-start(bf16[8,64,256]{2,1,0:T(8,128)(2,1)} %bitcast.9), calls=%async_computation | async-start | bytes 524288 | tf_op jit(solution)/shard_map/all_to_all | solution.py:402
  14.1 11.3 %copy-start = (bf16[768,256]{1,0:T(8,128)(2,1)S(1)}, bf16[768,256]{1,0:T(8,128)(2,1)}, u32[]{:S(2)}) copy-start(bf16[768,256]{1,0:T(8,128)(2,1)} %constant.25.clone.col_filter_ref) | copy-start | bytes 1179652
  14.1 11.3 %copy-start.1 = (f32[64,256]{1,0:T(8,128)S(1)}, f32[64,256]{1,0:T(8,128)}, u32[]{:S(2)}) copy-start(f32[64,256]{1,0:T(8,128)} %weight_ref.1) | copy-start | bytes 196612
  14.1 11.3 %copy-start.2 = (bf16[96,224]{1,0:T(8,128)(2,1)S(1)}, bf16[96,224]{1,0:T(8,128)(2,1)}, u32[]{:S(2)}) copy-start(bf16[96,224]{1,0:T(8,128)(2,1)} %constant.24.clone.row_filter_ref) | copy-start | bytes 129028
  17.0 8.4 %collective-permute-start.1 = (bf16[8,24,256]{2,1,0:T(8,128)(2,1)S(1)}, bf16[8,24,256]{2,1,0:T(8,128)(2,1)S(1)}, u32[]{:S(2)}, u32[]{:S(2)}) collective-permute-start(bf16[8,24,256]{2,1,0:T(8,128)(2,1)S(1)} %get-tuple-element.29), channel_id=1, source_target_pairs={{4,8},{12,16},{20,24},{8,4},{16,12},{24,20},{5,9},{13,17},{21,25},... | collective-permute-start | bytes 294920 | tf_op jit(solution)/shard_map/ppermute | solution.py:443
  17.6 7.7 %collective-permute-start = (bf16[8,24,256]{2,1,0:T(8,128)(2,1)S(1)}, bf16[8,24,256]{2,1,0:T(8,128)(2,1)S(1)}, u32[]{:S(2)}, u32[]{:S(2)}) collective-permute-start(bf16[8,24,256]{2,1,0:T(8,128)(2,1)S(1)} %get-tuple-element.30), channel_id=1, source_target_pairs={{0,4},{8,12},{16,20},{24,28},{4,0},{12,8},{20,16},{28,24},{1,5},{9... | collective-permute-start | bytes 294920 | tf_op jit(solution)/shard_map/ppermute | solution.py:440
  25.3 1.7 %copy-start.3 = (s32[8,384]{1,0:T(8,128)S(1)}, s32[8,384]{1,0:T(8,128)}, u32[]{:S(2)}) copy-start(s32[8,384]{1,0:T(8,128)} %support_ref.1) | copy-start | bytes 36868
  27.0 5.0 %copy-start.4 = (bf16[384,8]{0,1:T(8,128)(2,1)S(1)}, bf16[384,8]{0,1:T(8,128)(2,1)}, u32[]{:S(2)}) copy-start(bf16[384,8]{0,1:T(8,128)(2,1)} %param.11) | copy-start | bytes 18436
  35.2 7.2 %copy-start.5 = (bf16[8,384]{1,0:T(8,128)(2,1)}, bf16[8,384]{1,0:T(8,128)(2,1)S(1)}, u32[]{:S(2)}) copy-start(bf16[8,384]{1,0:T(8,128)(2,1)S(1)} %get-tuple-element.27.refs_0_) | copy-start | bytes 18436
  35.2 11.6 %all-to-all-start.1 = ((bf16[8,64,256]{2,1,0:T(8,128)(2,1)}), bf16[8,64,256]{2,1,0:T(8,128)(2,1)S(1)}, u32[]{:S(2)}, u32[]{:S(2)}) async-start(bf16[8,64,256]{2,1,0:T(8,128)(2,1)} %get-tuple-element.28), calls=%async_computation.1 | async-start | bytes 524288 | tf_op jit(solution)/shard_map/all_to_all | solution.py:526
  38.7 3.1 %collective-permute-start.4 = (bf16[8,384]{1,0:T(8,128)(2,1)S(1)}, bf16[8,384]{1,0:T(8,128)(2,1)S(1)}, u32[]{:S(2)}, u32[]{:S(2)}) collective-permute-start(bf16[8,384]{1,0:T(8,128)(2,1)S(1)} %get-tuple-element.27.refs_0_), channel_id=1, source_target_pairs={{0,3},{1,2},{2,1},{3,0},{4,7},{5,6},{6,5},{7,4},{8,11},{9,10},{10,... | collective-permute-start | bytes 18440 | tf_op jit(solution)/shard_map/ppermute | solution.py:524
  38.7 3.7 %collective-permute-start.3 = (bf16[8,384]{1,0:T(8,128)(2,1)S(1)}, bf16[8,384]{1,0:T(8,128)(2,1)S(1)}, u32[]{:S(2)}, u32[]{:S(2)}) collective-permute-start(bf16[8,384]{1,0:T(8,128)(2,1)S(1)} %get-tuple-element.27.refs_0_), channel_id=1, source_target_pairs={{0,2},{1,3},{2,0},{3,1},{4,6},{5,7},{6,4},{7,5},{8,10},{9,11},{10,... | collective-permute-start | bytes 18440 | tf_op jit(solution)/shard_map/ppermute | solution.py:524
  40.3 2.1 %collective-permute-start.2 = (bf16[8,384]{1,0:T(8,128)(2,1)S(1)}, bf16[8,384]{1,0:T(8,128)(2,1)S(1)}, u32[]{:S(2)}, u32[]{:S(2)}) collective-permute-start(bf16[8,384]{1,0:T(8,128)(2,1)S(1)} %get-tuple-element.27.refs_0_), channel_id=1, source_target_pairs={{0,1},{1,0},{2,3},{3,2},{4,5},{5,4},{6,7},{7,6},{8,9},{9,8},{10,11... | collective-permute-start | bytes 18440 | tf_op jit(solution)/shard_map/ppermute | solution.py:524
  41.8 0.7 %copy-start.7 = (bf16[8,384]{1,0:T(8,128)(2,1)}, bf16[8,384]{1,0:T(8,128)(2,1)S(1)}, u32[]{:S(2)}) copy-start(bf16[8,384]{1,0:T(8,128)(2,1)S(1)} %collective-permute-done.4.refs_3_) | copy-start | bytes 18436
  42.4 0.6 %copy-start.8 = (bf16[8,384]{1,0:T(8,128)(2,1)}, bf16[8,384]{1,0:T(8,128)(2,1)S(1)}, u32[]{:S(2)}) copy-start(bf16[8,384]{1,0:T(8,128)(2,1)S(1)} %collective-permute-done.3.refs_2_) | copy-start | bytes 18436
  43.0 0.6 %copy-start.9 = (bf16[8,384]{1,0:T(8,128)(2,1)}, bf16[8,384]{1,0:T(8,128)(2,1)S(1)}, u32[]{:S(2)}) copy-start(bf16[8,384]{1,0:T(8,128)(2,1)S(1)} %collective-permute-done.2.refs_1_) | copy-start | bytes 18436

commit v6 on v5

--- a/solution.py
+++ b/solution.py
@@ -175,8 +175,8 @@
     tile_count,
     movie_ref,
     first_ref,
+    edge_b_ref,
     edge_a_ref,
-    edge_b_ref,
     footprints_hbm,
     weight_ref,
     table_ref,
@@ -437,11 +437,11 @@
     bottom = first[:, tile_rows - HALO :]
     evens = [(i, i + 1) for i in range(0, tile_count - 1, 2)]
     odds = [(i, i + 1) for i in range(1, tile_count - 1, 2)]
+    edge_b = lax.ppermute(
+        jnp.where(odd, bottom, top), "tile", odds + [(j, i) for i, j in odds]
+    )
     edge_a = lax.ppermute(
         jnp.where(odd, top, bottom), "tile", evens + [(j, i) for i, j in evens]
-    )
-    edge_b = lax.ppermute(
-        jnp.where(odd, bottom, top), "tile", odds + [(j, i) for i, j in odds]
     )
 
     late_rows = BR * LATE
@@ -478,8 +478,8 @@
     )(
         strip_movie,
         first,
+        edge_b,
         edge_a,
-        edge_b,
         pinned[0],
         border_weight,
         table,

time: 47.9 us -> 47.8 us (level)
    ppermute x1, starting transfers between devices: 3.83 us -> 1.48 us  [per_device(): lax.ppermute(jnp.where(odd, top, bottom), 'tile', evens + [(j, i) for i,...]
    all_to_all x1, starting transfers between devices: 3.41 us -> 5.56 us  [per_device(): lax.all_to_all(leftover, 'tile', split_axis=0, concat_axis=0, tiled=True)]
where the time goes in v6:
time: 47.8 us; the launch traced here: 47.4 us
  Pallas kernels  21.6 us (45%)
  starting transfers between devices  16.8 us (35%)
  waiting for transfers between devices  6.06 us (13%)
  local copies, waits for them, and re-layouts  1.92 us (4%)
  between operations  0.81 us (2%)
    all_to_all x1, starting transfers between devices, per_device(): lax.all_to_all(pieces, 'tile', split_axis=0, concat_axis=0, tiled=True)  7.29 us
    pallas_call x1, Pallas kernels, per_device(): pl.pallas_call(kernel_fitted, out_shape=[jax.ShapeDtypeStruct((frames, ti...  6.15 us
    all_to_all x1, starting transfers between devices, per_device(): lax.all_to_all(leftover, 'tile', split_axis=0, concat_axis=0, tiled=True)  5.56 us
    pallas_call x1, Pallas kernels, per_device(): pl.pallas_call(functools.partial(kernel_coupling, frames), out_shape=[jax...  5.02 us
    pallas_call x1, Pallas kernels, per_device(): pl.pallas_call(kernel_early, out_shape=[jax.ShapeDtypeStruct((early_rows,...  3.84 us
    pallas_call x1, Pallas kernels, per_device(): pl.pallas_call(kernel_traces, out_shape=[jax.ShapeDtypeStruct((frames, co...  3.19 us
    all_to_all x1, waiting for transfers between devices, per_device(): lax.all_to_all(pieces, 'tile', split_axis=0, concat_axis=0, tiled=True)  2.72 us
    unnamed x21, local copies, waits for them, and re-layouts  1.92 us
  transfers between devices with their start and end apart: 7, of which 4 were waited for; matrix products, arithmetic and copies ran while one was open for 0% of the time, Pallas kernels for 25%

profile of v6, /device:TPU:0, one launch (start us, length us, event | category | flops | bytes accessed | tf_op | source)
XLA Modules:
  0.0 47.4 jit_solution(16542641976795889235)
XLA Ops:
  0.6 7.3 %all-to-all-start = ((bf16[8,64,256]{2,1,0:T(8,128)(2,1)}), bf16[8,64,256]{2,1,0:T(8,128)(2,1)S(1)}, u32[]{:S(2)}, u32[]{:S(2)}) async-start(bf16[8,64,256]{2,1,0:T(8,128)(2,1)} %bitcast.9), calls=%async_computation | async-start | bytes 524288 | tf_op jit(solution)/shard_map/all_to_all | solution.py:402
  7.9 6.2 %fitted.1 = (f32[8,64,256]{2,1,0:T(8,128)S(1)}, bf16[8,256,384]{2,1,0:T(8,128)(2,1)S(1)}) custom-call(bf16[64,256,384]{2,1,0:T(8,128)(2,1)} %footprints_hbm.5, s32[8,384]{1,0:T(8,128)} %support_ref.1, bf16[8,384]{1,0:T(8,128)(2,1)} %bitcast.5), custom_call_target="tpu_custom_call" | custom-call | flops 100663296 | bytes 12582912 | tf_op jit(solution)/shard_map/fitted/pallas_call | solution.py:409
  14.1 0.0 copy-start
  14.1 0.0 copy-start.1
  14.1 0.0 copy-start.2
  14.1 2.7 %all-to-all-done.movie_ref = bf16[8,64,256]{2,1,0:T(8,128)(2,1)S(1)} async-done(((bf16[8,64,256]{2,1,0:T(8,128)(2,1)}), bf16[8,64,256]{2,1,0:T(8,128)(2,1)S(1)}, u32[]{:S(2)}, u32[]{:S(2)}) %all-to-all-start) | async-done | bytes 262176 | tf_op jit(solution)/shard_map/all_to_all | solution.py:402
  16.9 0.1 subtract_convert_fusion.first_ref
  17.0 1.5 %collective-permute-start.1 = (bf16[8,24,256]{2,1,0:T(8,128)(2,1)S(1)}, bf16[8,24,256]{2,1,0:T(8,128)(2,1)S(1)}, u32[]{:S(2)}, u32[]{:S(2)}) collective-permute-start(bf16[8,24,256]{2,1,0:T(8,128)(2,1)S(1)} %get-tuple-element.29), channel_id=1, source_target_pairs={{0,4},{8,12},{16,20},{24,28},{4,0},{12,8},{20,16},{28,24},{1,5},{9... | collective-permute-start | bytes 294920 | tf_op jit(solution)/shard_map/ppermute | solution.py:443
  18.4 0.7 %collective-permute-start = (bf16[8,24,256]{2,1,0:T(8,128)(2,1)S(1)}, bf16[8,24,256]{2,1,0:T(8,128)(2,1)S(1)}, u32[]{:S(2)}, u32[]{:S(2)}) collective-permute-start(bf16[8,24,256]{2,1,0:T(8,128)(2,1)S(1)} %get-tuple-element.30), channel_id=1, source_target_pairs={{4,8},{12,16},{20,24},{8,4},{16,12},{24,20},{5,9},{13,17},{21,25},... | collective-permute-start | bytes 294920 | tf_op jit(solution)/shard_map/ppermute | solution.py:440
  19.1 3.8 %early.1 = (bf16[48,256,384]{2,1,0:T(8,128)(2,1)S(1)}, bf16[512,256]{1,0:T(8,128)(2,1)S(1)}, bf16[128,128]{1,0:T(8,128)(2,1)S(1)}) custom-call(bf16[64,256,384]{2,1,0:T(8,128)(2,1)} %footprints_hbm.5, s32[2,64]{1,0:T(2,128)S(1)} %bitcast.7), custom_call_target="tpu_custom_call" | custom-call | bytes 18874368 | tf_op jit(solution)/shard_map/early/pallas_call | solution.py:449
  23.0 0.0 copy-start.3
  23.0 1.6 %background.1 = (f32[2,512,128]{2,1,0:T(8,128)S(1)}, bf16[8,256,384]{2,1,0:T(8,128)(2,1)S(1)}) custom-call(bf16[8,64,256]{2,1,0:T(8,128)(2,1)S(1)} %all-to-all-done.movie_ref, bf16[8,64,256]{2,1,0:T(8,128)(2,1)S(1)} %subtract_convert_fusion.first_ref, bf16[8,24,256]{2,1,0:T(8,128)(2,1)S(1)} %collective-permute-done.edge_b_ref, ...), custom_call_target="tpu_custom_call" | custom-call | tf_op jit(solution)/shard_map/background/pallas_call | solution.py:467
  24.7 5.0 %coupling.1 = (bf16[400,16384]{1,0:T(8,128)(2,1)S(1)}, f32[384,384]{1,0:T(8,128)S(1)}, f32[8,384]{1,0:T(8,128)S(1)}) custom-call(bf16[48,256,384]{2,1,0:T(8,128)(2,1)S(1)} %get-tuple-element.16.early_ref, bf16[8,256,384]{2,1,0:T(8,128)(2,1)S(1)} %get-tuple-element.20.late_ref, bf16[8,256,384]{2,1,0:T(8,128)(2,1)S(1)} %get-tuple-element.21.kept_ref, ...), custom_call_target="tpu_custom_call" | custom-call | tf_op jit(solution)/shard_map/coupling/pallas_call | solution.py:492
  29.7 3.2 %traces.1 = (f32[8,384]{1,0:T(8,128)}, bf16[8,384]{1,0:T(8,128)(2,1)S(1)}, bf16[8,64,256]{2,1,0:T(8,128)(2,1)}) custom-call(bf16[400,16384]{1,0:T(8,128)(2,1)S(1)} %get-tuple-element.23.stacked_ref, f32[384,384]{1,0:T(8,128)S(1)} %get-tuple-element.24.coupling_ref, f32[8,384]{1,0:T(8,128)S(1)} %get-tuple-element.25.projected_ref, ...), custom_call_target="tpu_custom_call" | custom-call | tf_op jit(solution)/shard_map/traces/pallas_call | solution.py:508
  32.9 5.6 %all-to-all-start.1 = ((bf16[8,64,256]{2,1,0:T(8,128)(2,1)}), bf16[8,64,256]{2,1,0:T(8,128)(2,1)S(1)}, u32[]{:S(2)}, u32[]{:S(2)}) async-start(bf16[8,64,256]{2,1,0:T(8,128)(2,1)} %get-tuple-element.28), calls=%async_computation.1 | async-start | bytes 524288 | tf_op jit(solution)/shard_map/all_to_all | solution.py:526
  38.5 1.6 %collective-permute-start.3 = (bf16[8,384]{1,0:T(8,128)(2,1)S(1)}, bf16[8,384]{1,0:T(8,128)(2,1)S(1)}, u32[]{:S(2)}, u32[]{:S(2)}) collective-permute-start(bf16[8,384]{1,0:T(8,128)(2,1)S(1)} %get-tuple-element.27.refs_0_), channel_id=1, source_target_pairs={{0,2},{1,3},{2,0},{3,1},{4,6},{5,7},{6,4},{7,5},{8,10},{9,11},{10,... | collective-permute-start | bytes 18440 | tf_op jit(solution)/shard_map/ppermute | solution.py:524
  40.0 0.3 collective-permute-start.2
  40.3 1.2 %collective-permute-done.4.refs_3_ = bf16[8,384]{1,0:T(8,128)(2,1)S(1)} collective-permute-done((bf16[8,384]{1,0:T(8,128)(2,1)S(1)}, bf16[8,384]{1,0:T(8,128)(2,1)S(1)}, u32[]{:S(2)}, u32[]{:S(2)}) %collective-permute-start.4) | collective-permute-done | bytes 6176 | tf_op jit(solution)/shard_map/ppermute | solution.py:524
  41.5 0.6 %collective-permute-done.3.refs_2_ = bf16[8,384]{1,0:T(8,128)(2,1)S(1)} collective-permute-done((bf16[8,384]{1,0:T(8,128)(2,1)S(1)}, bf16[8,384]{1,0:T(8,128)(2,1)S(1)}, u32[]{:S(2)}, u32[]{:S(2)}) %collective-permute-start.3) | collective-permute-done | bytes 6176 | tf_op jit(solution)/shard_map/ppermute | solution.py:524
  42.2 0.6 %copy-done.8 = bf16[8,384]{1,0:T(8,128)(2,1)} copy-done((bf16[8,384]{1,0:T(8,128)(2,1)}, bf16[8,384]{1,0:T(8,128)(2,1)S(1)}, u32[]{:S(2)}) %copy-start.8) | copy-done | bytes 6168
  42.7 0.6 %copy-done.9 = bf16[8,384]{1,0:T(8,128)(2,1)} copy-done((bf16[8,384]{1,0:T(8,128)(2,1)}, bf16[8,384]{1,0:T(8,128)(2,1)S(1)}, u32[]{:S(2)}) %copy-start.9) | copy-done | bytes 6168
  43.3 1.8 %gram.1 = f32[384,384]{1,0:T(8,128)} custom-call(bf16[8,384]{1,0:T(8,128)(2,1)} %copy-done.5, bf16[8,384]{1,0:T(8,128)(2,1)} %copy-done.9, bf16[8,384]{1,0:T(8,128)(2,1)} %copy-done.8, bf16[8,384]{1,0:T(8,128)(2,1)} %copy-done.7), custom_call_target="tpu_custom_call" | custom-call | tf_op jit(solution)/shard_map/gram/pallas_call | solution.py:532
  45.2 1.5 %all-to-all-done.1 = bf16[8,64,256]{2,1,0:T(8,128)(2,1)S(1)} async-done(((bf16[8,64,256]{2,1,0:T(8,128)(2,1)}), bf16[8,64,256]{2,1,0:T(8,128)(2,1)S(1)}, u32[]{:S(2)}, u32[]{:S(2)}) %all-to-all-start.1) | async-done | bytes 262176 | tf_op jit(solution)/shard_map/all_to_all | solution.py:526
  46.7 0.7 %copy.12 = bf16[1,512,256]{2,1,0:T(8,128)(2,1)} copy(bf16[1,512,256]{2,1,0:T(8,128)(2,1)S(1)} %bitcast.8) | data formatting | bytes 524288
  (19 shorter events, 0.1 us)
Async XLA Ops:
  0.6 18.5 %copy-start.6 = (s32[64,2]{0,1:T(2,128)S(1)}, s32[64,2]{0,1:T(2,128)}, u32[]{:S(2)}) copy-start(s32[64,2]{0,1:T(2,128)} %param.13) | copy-start | bytes 1540
  0.6 16.2 %all-to-all-start = ((bf16[8,64,256]{2,1,0:T(8,128)(2,1)}), bf16[8,64,256]{2,1,0:T(8,128)(2,1)S(1)}, u32[]{:S(2)}, u32[]{:S(2)}) async-start(bf16[8,64,256]{2,1,0:T(8,128)(2,1)} %bitcast.9), calls=%async_computation | async-start | bytes 524288 | tf_op jit(solution)/shard_map/all_to_all | solution.py:402
  14.1 8.9 %copy-start = (bf16[768,256]{1,0:T(8,128)(2,1)S(1)}, bf16[768,256]{1,0:T(8,128)(2,1)}, u32[]{:S(2)}) copy-start(bf16[768,256]{1,0:T(8,128)(2,1)} %constant.25.clone.col_filter_ref) | copy-start | bytes 1179652
  14.1 8.9 %copy-start.1 = (f32[64,256]{1,0:T(8,128)S(1)}, f32[64,256]{1,0:T(8,128)}, u32[]{:S(2)}) copy-start(f32[64,256]{1,0:T(8,128)} %weight_ref.1) | copy-start | bytes 196612
  14.1 8.9 %copy-start.2 = (bf16[96,224]{1,0:T(8,128)(2,1)S(1)}, bf16[96,224]{1,0:T(8,128)(2,1)}, u32[]{:S(2)}) copy-start(bf16[96,224]{1,0:T(8,128)(2,1)} %constant.24.clone.row_filter_ref) | copy-start | bytes 129028
  17.0 6.0 %collective-permute-start.1 = (bf16[8,24,256]{2,1,0:T(8,128)(2,1)S(1)}, bf16[8,24,256]{2,1,0:T(8,128)(2,1)S(1)}, u32[]{:S(2)}, u32[]{:S(2)}) collective-permute-start(bf16[8,24,256]{2,1,0:T(8,128)(2,1)S(1)} %get-tuple-element.29), channel_id=1, source_target_pairs={{0,4},{8,12},{16,20},{24,28},{4,0},{12,8},{20,16},{28,24},{1,5},{9... | collective-permute-start | bytes 294920 | tf_op jit(solution)/shard_map/ppermute | solution.py:443
  18.4 4.5 %collective-permute-start = (bf16[8,24,256]{2,1,0:T(8,128)(2,1)S(1)}, bf16[8,24,256]{2,1,0:T(8,128)(2,1)S(1)}, u32[]{:S(2)}, u32[]{:S(2)}) collective-permute-start(bf16[8,24,256]{2,1,0:T(8,128)(2,1)S(1)} %get-tuple-element.30), channel_id=1, source_target_pairs={{4,8},{12,16},{20,24},{8,4},{16,12},{24,20},{5,9},{13,17},{21,25},... | collective-permute-start | bytes 294920 | tf_op jit(solution)/shard_map/ppermute | solution.py:440
  23.0 1.7 %copy-start.3 = (s32[8,384]{1,0:T(8,128)S(1)}, s32[8,384]{1,0:T(8,128)}, u32[]{:S(2)}) copy-start(s32[8,384]{1,0:T(8,128)} %support_ref.1) | copy-start | bytes 36868
  24.6 5.0 %copy-start.4 = (bf16[384,8]{0,1:T(8,128)(2,1)S(1)}, bf16[384,8]{0,1:T(8,128)(2,1)}, u32[]{:S(2)}) copy-start(bf16[384,8]{0,1:T(8,128)(2,1)} %param.11) | copy-start | bytes 18436
  32.9 9.3 %copy-start.5 = (bf16[8,384]{1,0:T(8,128)(2,1)}, bf16[8,384]{1,0:T(8,128)(2,1)S(1)}, u32[]{:S(2)}) copy-start(bf16[8,384]{1,0:T(8,128)(2,1)S(1)} %get-tuple-element.27.refs_0_) | copy-start | bytes 18436
  32.9 13.8 %all-to-all-start.1 = ((bf16[8,64,256]{2,1,0:T(8,128)(2,1)}), bf16[8,64,256]{2,1,0:T(8,128)(2,1)S(1)}, u32[]{:S(2)}, u32[]{:S(2)}) async-start(bf16[8,64,256]{2,1,0:T(8,128)(2,1)} %get-tuple-element.28), calls=%async_computation.1 | async-start | bytes 524288 | tf_op jit(solution)/shard_map/all_to_all | solution.py:526
  38.4 3.1 %collective-permute-start.4 = (bf16[8,384]{1,0:T(8,128)(2,1)S(1)}, bf16[8,384]{1,0:T(8,128)(2,1)S(1)}, u32[]{:S(2)}, u32[]{:S(2)}) collective-permute-start(bf16[8,384]{1,0:T(8,128)(2,1)S(1)} %get-tuple-element.27.refs_0_), channel_id=1, source_target_pairs={{0,3},{1,2},{2,1},{3,0},{4,7},{5,6},{6,5},{7,4},{8,11},{9,10},{10,... | collective-permute-start | bytes 18440 | tf_op jit(solution)/shard_map/ppermute | solution.py:524
  38.5 3.7 %collective-permute-start.3 = (bf16[8,384]{1,0:T(8,128)(2,1)S(1)}, bf16[8,384]{1,0:T(8,128)(2,1)S(1)}, u32[]{:S(2)}, u32[]{:S(2)}) collective-permute-start(bf16[8,384]{1,0:T(8,128)(2,1)S(1)} %get-tuple-element.27.refs_0_), channel_id=1, source_target_pairs={{0,2},{1,3},{2,0},{3,1},{4,6},{5,7},{6,4},{7,5},{8,10},{9,11},{10,... | collective-permute-start | bytes 18440 | tf_op jit(solution)/shard_map/ppermute | solution.py:524
  40.0 2.1 %collective-permute-start.2 = (bf16[8,384]{1,0:T(8,128)(2,1)S(1)}, bf16[8,384]{1,0:T(8,128)(2,1)S(1)}, u32[]{:S(2)}, u32[]{:S(2)}) collective-permute-start(bf16[8,384]{1,0:T(8,128)(2,1)S(1)} %get-tuple-element.27.refs_0_), channel_id=1, source_target_pairs={{0,1},{1,0},{2,3},{3,2},{4,5},{5,4},{6,7},{7,6},{8,9},{9,8},{10,11... | collective-permute-start | bytes 18440 | tf_op jit(solution)/shard_map/ppermute | solution.py:524
  41.5 0.6 %copy-start.7 = (bf16[8,384]{1,0:T(8,128)(2,1)}, bf16[8,384]{1,0:T(8,128)(2,1)S(1)}, u32[]{:S(2)}) copy-start(bf16[8,384]{1,0:T(8,128)(2,1)S(1)} %collective-permute-done.4.refs_3_) | copy-start | bytes 18436
  42.1 0.6 %copy-start.8 = (bf16[8,384]{1,0:T(8,128)(2,1)}, bf16[8,384]{1,0:T(8,128)(2,1)S(1)}, u32[]{:S(2)}) copy-start(bf16[8,384]{1,0:T(8,128)(2,1)S(1)} %collective-permute-done.3.refs_2_) | copy-start | bytes 18436
  42.7 0.6 %copy-start.9 = (bf16[8,384]{1,0:T(8,128)(2,1)}, bf16[8,384]{1,0:T(8,128)(2,1)S(1)}, u32[]{:S(2)}) copy-start(bf16[8,384]{1,0:T(8,128)(2,1)S(1)} %collective-permute-done.2.refs_1_) | copy-start | bytes 18436

commit v7 on v6

--- a/solution.py
+++ b/solution.py
@@ -47,7 +47,7 @@
     cols_high, cols_low = parts(band(columns, columns, 0))
     return (
         jnp.asarray(np.concatenate([rows_high, rows_low], axis=1)),
-        jnp.asarray(np.concatenate([cols_high, cols_high, cols_low], axis=0)),
+        jnp.asarray(np.concatenate([cols_high, cols_low], axis=0)),
     )
 
 
@@ -221,9 +221,9 @@
                 preferred_element_type=jnp.float32,
             )
         )
-    high, low = split_high_low(jnp.concatenate(tall, axis=0))
+    high = jnp.concatenate(tall, axis=0).astype(jnp.bfloat16)
     smooth = jnp.dot(
-        jnp.concatenate([high, low, high], axis=1),
+        jnp.concatenate([high, high], axis=1),
         col_filter_ref[...],
         preferred_element_type=jnp.float32,
     ).astype(jnp.bfloat16)

time: 47.8 us -> 47.6 us (level)
  no operation moved by 1% of the time
where the time goes in v7:
time: 47.6 us; the launch traced here: 47.2 us
  Pallas kernels  21.5 us (45%)
  starting transfers between devices  16.8 us (35%)
  waiting for transfers between devices  6.07 us (13%)
  local copies, waits for them, and re-layouts  1.92 us (4%)
  between operations  0.81 us (2%)
    all_to_all x1, starting transfers between devices, per_device(): lax.all_to_all(pieces, 'tile', split_axis=0, concat_axis=0, tiled=True)  7.29 us
    pallas_call x1, Pallas kernels, per_device(): pl.pallas_call(kernel_fitted, out_shape=[jax.ShapeDtypeStruct((frames, ti...  6.15 us
    all_to_all x1, starting transfers between devices, per_device(): lax.all_to_all(leftover, 'tile', split_axis=0, concat_axis=0, tiled=True)  5.56 us
    pallas_call x1, Pallas kernels, per_device(): pl.pallas_call(functools.partial(kernel_coupling, frames), out_shape=[jax...  5.02 us
    pallas_call x1, Pallas kernels, per_device(): pl.pallas_call(kernel_early, out_shape=[jax.ShapeDtypeStruct((early_rows,...  3.84 us
    pallas_call x1, Pallas kernels, per_device(): pl.pallas_call(kernel_traces, out_shape=[jax.ShapeDtypeStruct((frames, co...  3.19 us
    all_to_all x1, waiting for transfers between devices, per_device(): lax.all_to_all(pieces, 'tile', split_axis=0, concat_axis=0, tiled=True)  2.72 us
    unnamed x21, local copies, waits for them, and re-layouts  1.92 us
  transfers between devices with their start and end apart: 7, of which 4 were waited for; matrix products, arithmetic and copies ran while one was open for 0% of the time, Pallas kernels for 25%

profile of v7, /device:TPU:0, one launch (start us, length us, event | category | flops | bytes accessed | tf_op | source)
XLA Modules:
  0.0 47.2 jit_solution(14511998678831395675)
XLA Ops:
  0.6 7.3 %all-to-all-start = ((bf16[8,64,256]{2,1,0:T(8,128)(2,1)}), bf16[8,64,256]{2,1,0:T(8,128)(2,1)S(1)}, u32[]{:S(2)}, u32[]{:S(2)}) async-start(bf16[8,64,256]{2,1,0:T(8,128)(2,1)} %bitcast.9), calls=%async_computation | async-start | bytes 524288 | tf_op jit(solution)/shard_map/all_to_all | solution.py:402
  7.9 6.2 %fitted.1 = (f32[8,64,256]{2,1,0:T(8,128)S(1)}, bf16[8,256,384]{2,1,0:T(8,128)(2,1)S(1)}) custom-call(bf16[64,256,384]{2,1,0:T(8,128)(2,1)} %footprints_hbm.5, s32[8,384]{1,0:T(8,128)} %support_ref.1, bf16[8,384]{1,0:T(8,128)(2,1)} %bitcast.5), custom_call_target="tpu_custom_call" | custom-call | flops 100663296 | bytes 12582912 | tf_op jit(solution)/shard_map/fitted/pallas_call | solution.py:409
  14.1 0.0 copy-start
  14.1 0.0 copy-start.1
  14.1 0.0 copy-start.2
  14.1 2.7 %all-to-all-done.movie_ref = bf16[8,64,256]{2,1,0:T(8,128)(2,1)S(1)} async-done(((bf16[8,64,256]{2,1,0:T(8,128)(2,1)}), bf16[8,64,256]{2,1,0:T(8,128)(2,1)S(1)}, u32[]{:S(2)}, u32[]{:S(2)}) %all-to-all-start) | async-done | bytes 262176 | tf_op jit(solution)/shard_map/all_to_all | solution.py:402
  16.9 0.1 subtract_convert_fusion.first_ref
  17.0 1.5 %collective-permute-start.1 = (bf16[8,24,256]{2,1,0:T(8,128)(2,1)S(1)}, bf16[8,24,256]{2,1,0:T(8,128)(2,1)S(1)}, u32[]{:S(2)}, u32[]{:S(2)}) collective-permute-start(bf16[8,24,256]{2,1,0:T(8,128)(2,1)S(1)} %get-tuple-element.29), channel_id=1, source_target_pairs={{0,4},{8,12},{16,20},{24,28},{4,0},{12,8},{20,16},{28,24},{1,5},{9... | collective-permute-start | bytes 294920 | tf_op jit(solution)/shard_map/ppermute | solution.py:443
  18.4 0.7 %collective-permute-start = (bf16[8,24,256]{2,1,0:T(8,128)(2,1)S(1)}, bf16[8,24,256]{2,1,0:T(8,128)(2,1)S(1)}, u32[]{:S(2)}, u32[]{:S(2)}) collective-permute-start(bf16[8,24,256]{2,1,0:T(8,128)(2,1)S(1)} %get-tuple-element.30), channel_id=1, source_target_pairs={{4,8},{12,16},{20,24},{8,4},{16,12},{24,20},{5,9},{13,17},{21,25},... | collective-permute-start | bytes 294920 | tf_op jit(solution)/shard_map/ppermute | solution.py:440
  19.1 3.8 %early.1 = (bf16[48,256,384]{2,1,0:T(8,128)(2,1)S(1)}, bf16[512,256]{1,0:T(8,128)(2,1)S(1)}, bf16[128,128]{1,0:T(8,128)(2,1)S(1)}) custom-call(bf16[64,256,384]{2,1,0:T(8,128)(2,1)} %footprints_hbm.5, s32[2,64]{1,0:T(2,128)S(1)} %bitcast.7), custom_call_target="tpu_custom_call" | custom-call | bytes 18874368 | tf_op jit(solution)/shard_map/early/pallas_call | solution.py:449
  23.0 1.4 %background.1 = (f32[2,512,128]{2,1,0:T(8,128)S(1)}, bf16[8,256,384]{2,1,0:T(8,128)(2,1)S(1)}) custom-call(bf16[8,64,256]{2,1,0:T(8,128)(2,1)S(1)} %all-to-all-done.movie_ref, bf16[8,64,256]{2,1,0:T(8,128)(2,1)S(1)} %subtract_convert_fusion.first_ref, bf16[8,24,256]{2,1,0:T(8,128)(2,1)S(1)} %collective-permute-done.edge_b_ref, ...), custom_call_target="tpu_custom_call" | custom-call | tf_op jit(solution)/shard_map/background/pallas_call | solution.py:467
  24.5 0.0 copy-start.4
  24.5 5.0 %coupling.1 = (bf16[400,16384]{1,0:T(8,128)(2,1)S(1)}, f32[384,384]{1,0:T(8,128)S(1)}, f32[8,384]{1,0:T(8,128)S(1)}) custom-call(bf16[48,256,384]{2,1,0:T(8,128)(2,1)S(1)} %get-tuple-element.16.early_ref, bf16[8,256,384]{2,1,0:T(8,128)(2,1)S(1)} %get-tuple-element.20.late_ref, bf16[8,256,384]{2,1,0:T(8,128)(2,1)S(1)} %get-tuple-element.21.kept_ref, ...), custom_call_target="tpu_custom_call" | custom-call | tf_op jit(solution)/shard_map/coupling/pallas_call | solution.py:492
  29.5 3.2 %traces.1 = (f32[8,384]{1,0:T(8,128)}, bf16[8,384]{1,0:T(8,128)(2,1)S(1)}, bf16[8,64,256]{2,1,0:T(8,128)(2,1)}) custom-call(bf16[400,16384]{1,0:T(8,128)(2,1)S(1)} %get-tuple-element.23.stacked_ref, f32[384,384]{1,0:T(8,128)S(1)} %get-tuple-element.24.coupling_ref, f32[8,384]{1,0:T(8,128)S(1)} %get-tuple-element.25.projected_ref, ...), custom_call_target="tpu_custom_call" | custom-call | tf_op jit(solution)/shard_map/traces/pallas_call | solution.py:508
  32.7 5.6 %all-to-all-start.1 = ((bf16[8,64,256]{2,1,0:T(8,128)(2,1)}), bf16[8,64,256]{2,1,0:T(8,128)(2,1)S(1)}, u32[]{:S(2)}, u32[]{:S(2)}) async-start(bf16[8,64,256]{2,1,0:T(8,128)(2,1)} %get-tuple-element.28), calls=%async_computation.1 | async-start | bytes 524288 | tf_op jit(solution)/shard_map/all_to_all | solution.py:526
  38.3 1.6 %collective-permute-start.3 = (bf16[8,384]{1,0:T(8,128)(2,1)S(1)}, bf16[8,384]{1,0:T(8,128)(2,1)S(1)}, u32[]{:S(2)}, u32[]{:S(2)}) collective-permute-start(bf16[8,384]{1,0:T(8,128)(2,1)S(1)} %get-tuple-element.27.refs_0_), channel_id=1, source_target_pairs={{0,2},{1,3},{2,0},{3,1},{4,6},{5,7},{6,4},{7,5},{8,10},{9,11},{10,... | collective-permute-start | bytes 18440 | tf_op jit(solution)/shard_map/ppermute | solution.py:524
  39.8 0.3 collective-permute-start.2
  40.1 1.2 %collective-permute-done.4.refs_3_ = bf16[8,384]{1,0:T(8,128)(2,1)S(1)} collective-permute-done((bf16[8,384]{1,0:T(8,128)(2,1)S(1)}, bf16[8,384]{1,0:T(8,128)(2,1)S(1)}, u32[]{:S(2)}, u32[]{:S(2)}) %collective-permute-start.4) | collective-permute-done | bytes 6176 | tf_op jit(solution)/shard_map/ppermute | solution.py:524
  41.3 0.6 %collective-permute-done.3.refs_2_ = bf16[8,384]{1,0:T(8,128)(2,1)S(1)} collective-permute-done((bf16[8,384]{1,0:T(8,128)(2,1)S(1)}, bf16[8,384]{1,0:T(8,128)(2,1)S(1)}, u32[]{:S(2)}, u32[]{:S(2)}) %collective-permute-start.3) | collective-permute-done | bytes 6176 | tf_op jit(solution)/shard_map/ppermute | solution.py:524
  42.0 0.6 %copy-done.8 = bf16[8,384]{1,0:T(8,128)(2,1)} copy-done((bf16[8,384]{1,0:T(8,128)(2,1)}, bf16[8,384]{1,0:T(8,128)(2,1)S(1)}, u32[]{:S(2)}) %copy-start.8) | copy-done | bytes 6168
  42.6 0.6 %copy-done.9 = bf16[8,384]{1,0:T(8,128)(2,1)} copy-done((bf16[8,384]{1,0:T(8,128)(2,1)}, bf16[8,384]{1,0:T(8,128)(2,1)S(1)}, u32[]{:S(2)}) %copy-start.9) | copy-done | bytes 6168
  43.2 1.8 %gram.1 = f32[384,384]{1,0:T(8,128)} custom-call(bf16[8,384]{1,0:T(8,128)(2,1)} %copy-done.5, bf16[8,384]{1,0:T(8,128)(2,1)} %copy-done.9, bf16[8,384]{1,0:T(8,128)(2,1)} %copy-done.8, bf16[8,384]{1,0:T(8,128)(2,1)} %copy-done.7), custom_call_target="tpu_custom_call" | custom-call | tf_op jit(solution)/shard_map/gram/pallas_call | solution.py:532
  45.0 1.5 %all-to-all-done.1 = bf16[8,64,256]{2,1,0:T(8,128)(2,1)S(1)} async-done(((bf16[8,64,256]{2,1,0:T(8,128)(2,1)}), bf16[8,64,256]{2,1,0:T(8,128)(2,1)S(1)}, u32[]{:S(2)}, u32[]{:S(2)}) %all-to-all-start.1) | async-done | bytes 262176 | tf_op jit(solution)/shard_map/all_to_all | solution.py:526
  46.5 0.7 %copy.12 = bf16[1,512,256]{2,1,0:T(8,128)(2,1)} copy(bf16[1,512,256]{2,1,0:T(8,128)(2,1)S(1)} %bitcast.8) | data formatting | bytes 524288
  (19 shorter events, 0.1 us)
Async XLA Ops:
  0.6 18.5 %copy-start.6 = (s32[64,2]{0,1:T(2,128)S(1)}, s32[64,2]{0,1:T(2,128)}, u32[]{:S(2)}) copy-start(s32[64,2]{0,1:T(2,128)} %param.13) | copy-start | bytes 1540
  0.6 16.2 %all-to-all-start = ((bf16[8,64,256]{2,1,0:T(8,128)(2,1)}), bf16[8,64,256]{2,1,0:T(8,128)(2,1)S(1)}, u32[]{:S(2)}, u32[]{:S(2)}) async-start(bf16[8,64,256]{2,1,0:T(8,128)(2,1)} %bitcast.9), calls=%async_computation | async-start | bytes 524288 | tf_op jit(solution)/shard_map/all_to_all | solution.py:402
  14.1 8.9 %copy-start = (bf16[512,256]{1,0:T(8,128)(2,1)S(1)}, bf16[512,256]{1,0:T(8,128)(2,1)}, u32[]{:S(2)}) copy-start(bf16[512,256]{1,0:T(8,128)(2,1)} %constant.25.clone.col_filter_ref) | copy-start | bytes 786436
  14.1 8.9 %copy-start.1 = (f32[64,256]{1,0:T(8,128)S(1)}, f32[64,256]{1,0:T(8,128)}, u32[]{:S(2)}) copy-start(f32[64,256]{1,0:T(8,128)} %weight_ref.1) | copy-start | bytes 196612
  14.1 8.9 %copy-start.2 = (bf16[96,224]{1,0:T(8,128)(2,1)S(1)}, bf16[96,224]{1,0:T(8,128)(2,1)}, u32[]{:S(2)}) copy-start(bf16[96,224]{1,0:T(8,128)(2,1)} %constant.24.clone.row_filter_ref) | copy-start | bytes 129028
  17.0 6.0 %collective-permute-start.1 = (bf16[8,24,256]{2,1,0:T(8,128)(2,1)S(1)}, bf16[8,24,256]{2,1,0:T(8,128)(2,1)S(1)}, u32[]{:S(2)}, u32[]{:S(2)}) collective-permute-start(bf16[8,24,256]{2,1,0:T(8,128)(2,1)S(1)} %get-tuple-element.29), channel_id=1, source_target_pairs={{0,4},{8,12},{16,20},{24,28},{4,0},{12,8},{20,16},{28,24},{1,5},{9... | collective-permute-start | bytes 294920 | tf_op jit(solution)/shard_map/ppermute | solution.py:443
  18.4 4.5 %collective-permute-start = (bf16[8,24,256]{2,1,0:T(8,128)(2,1)S(1)}, bf16[8,24,256]{2,1,0:T(8,128)(2,1)S(1)}, u32[]{:S(2)}, u32[]{:S(2)}) collective-permute-start(bf16[8,24,256]{2,1,0:T(8,128)(2,1)S(1)} %get-tuple-element.30), channel_id=1, source_target_pairs={{4,8},{12,16},{20,24},{8,4},{16,12},{24,20},{5,9},{13,17},{21,25},... | collective-permute-start | bytes 294920 | tf_op jit(solution)/shard_map/ppermute | solution.py:440
  23.0 1.5 %copy-start.3 = (s32[8,384]{1,0:T(8,128)S(1)}, s32[8,384]{1,0:T(8,128)}, u32[]{:S(2)}) copy-start(s32[8,384]{1,0:T(8,128)} %support_ref.1) | copy-start | bytes 36868
  24.5 5.1 %copy-start.4 = (bf16[384,8]{0,1:T(8,128)(2,1)S(1)}, bf16[384,8]{0,1:T(8,128)(2,1)}, u32[]{:S(2)}) copy-start(bf16[384,8]{0,1:T(8,128)(2,1)} %param.11) | copy-start | bytes 18436
  32.7 9.3 %copy-start.5 = (bf16[8,384]{1,0:T(8,128)(2,1)}, bf16[8,384]{1,0:T(8,128)(2,1)S(1)}, u32[]{:S(2)}) copy-start(bf16[8,384]{1,0:T(8,128)(2,1)S(1)} %get-tuple-element.27.refs_0_) | copy-start | bytes 18436
  32.7 13.8 %all-to-all-start.1 = ((bf16[8,64,256]{2,1,0:T(8,128)(2,1)}), bf16[8,64,256]{2,1,0:T(8,128)(2,1)S(1)}, u32[]{:S(2)}, u32[]{:S(2)}) async-start(bf16[8,64,256]{2,1,0:T(8,128)(2,1)} %get-tuple-element.28), calls=%async_computation.1 | async-start | bytes 524288 | tf_op jit(solution)/shard_map/all_to_all | solution.py:526
  38.3 3.1 %collective-permute-start.4 = (bf16[8,384]{1,0:T(8,128)(2,1)S(1)}, bf16[8,384]{1,0:T(8,128)(2,1)S(1)}, u32[]{:S(2)}, u32[]{:S(2)}) collective-permute-start(bf16[8,384]{1,0:T(8,128)(2,1)S(1)} %get-tuple-element.27.refs_0_), channel_id=1, source_target_pairs={{0,3},{1,2},{2,1},{3,0},{4,7},{5,6},{6,5},{7,4},{8,11},{9,10},{10,... | collective-permute-start | bytes 18440 | tf_op jit(solution)/shard_map/ppermute | solution.py:524
  38.3 3.7 %collective-permute-start.3 = (bf16[8,384]{1,0:T(8,128)(2,1)S(1)}, bf16[8,384]{1,0:T(8,128)(2,1)S(1)}, u32[]{:S(2)}, u32[]{:S(2)}) collective-permute-start(bf16[8,384]{1,0:T(8,128)(2,1)S(1)} %get-tuple-element.27.refs_0_), channel_id=1, source_target_pairs={{0,2},{1,3},{2,0},{3,1},{4,6},{5,7},{6,4},{7,5},{8,10},{9,11},{10,... | collective-permute-start | bytes 18440 | tf_op jit(solution)/shard_map/ppermute | solution.py:524
  39.8 2.1 %collective-permute-start.2 = (bf16[8,384]{1,0:T(8,128)(2,1)S(1)}, bf16[8,384]{1,0:T(8,128)(2,1)S(1)}, u32[]{:S(2)}, u32[]{:S(2)}) collective-permute-start(bf16[8,384]{1,0:T(8,128)(2,1)S(1)} %get-tuple-element.27.refs_0_), channel_id=1, source_target_pairs={{0,1},{1,0},{2,3},{3,2},{4,5},{5,4},{6,7},{7,6},{8,9},{9,8},{10,11... | collective-permute-start | bytes 18440 | tf_op jit(solution)/shard_map/ppermute | solution.py:524
  41.3 0.6 %copy-start.7 = (bf16[8,384]{1,0:T(8,128)(2,1)}, bf16[8,384]{1,0:T(8,128)(2,1)S(1)}, u32[]{:S(2)}) copy-start(bf16[8,384]{1,0:T(8,128)(2,1)S(1)} %collective-permute-done.4.refs_3_) | copy-start | bytes 18436
  42.0 0.6 %copy-start.8 = (bf16[8,384]{1,0:T(8,128)(2,1)}, bf16[8,384]{1,0:T(8,128)(2,1)S(1)}, u32[]{:S(2)}) copy-start(bf16[8,384]{1,0:T(8,128)(2,1)S(1)} %collective-permute-done.3.refs_2_) | copy-start | bytes 18436
  42.6 0.6 %copy-start.9 = (bf16[8,384]{1,0:T(8,128)(2,1)}, bf16[8,384]{1,0:T(8,128)(2,1)S(1)}, u32[]{:S(2)}) copy-start(bf16[8,384]{1,0:T(8,128)(2,1)S(1)} %collective-permute-done.2.refs_1_) | copy-start | bytes 18436

commit v8 on v6

--- a/solution.py
+++ b/solution.py
@@ -318,10 +318,13 @@
     projected_ref,
     traces_ref,
     cleaned_ref,
+    new_traces_hbm,
+    rounded_ref,
+    remainder_hbm,
+    refit_ref,
+    remainder_ref,
     new_traces_ref,
-    rounded_ref,
-    remainder_ref,
-    refit_ref,
+    left,
 ):
     frames, tile_rows, columns = remainder_ref.shape
     components = coupling_ref.shape[0]
@@ -350,7 +353,8 @@
     rounded = state.astype(jnp.bfloat16)
     new_traces_ref[...] = state
     rounded_ref[...] = rounded
-
+    copies = [pltpu.make_async_copy(new_traces_ref, new_traces_hbm, left.at[0])]
+    copies[0].start()
     for b in range(tile_rows // BR):
         refit = jnp.dot(
             rounded,
@@ -363,12 +367,24 @@
                 refit_ref[half, pl.ds(b * BR + row, frames, stride=tile_rows), :] = refit[
                     :, start : start + LANES
                 ]
-    for frame in range(frames):
-        rows = slice(frame * tile_rows, (frame + 1) * tile_rows)
-        for half in range(halves):
-            remainder_ref[frame, :, half * LANES : (half + 1) * LANES] = (
-                cleaned_ref[half, rows, :] - refit_ref[half, rows, :]
-            ).astype(jnp.bfloat16)
+        if b % 2 == 0:
+            continue
+        start = (b - 1) * BR
+        for frame in range(frames):
+            rows = slice(frame * tile_rows + start, frame * tile_rows + start + 2 * BR)
+            for half in range(halves):
+                remainder_ref[
+                    frame, start : start + 2 * BR, half * LANES : (half + 1) * LANES
+                ] = (cleaned_ref[half, rows, :] - refit_ref[half, rows, :]).astype(jnp.bfloat16)
+        part = pl.ds(start, 2 * BR)
+        copies.append(
+            pltpu.make_async_copy(
+                remainder_ref.at[:, part], remainder_hbm.at[:, part], left.at[len(copies)]
+            )
+        )
+        copies[-1].start()
+    for copy in copies:
+        copy.wait()
 
 
 def pairs(count, turn):
@@ -513,8 +529,13 @@
             jax.ShapeDtypeStruct((frames, tile_rows, columns), jnp.bfloat16),
         ],
         in_specs=[VMEM] * 5,
-        out_specs=[VMEM] * 3,
-        scratch_shapes=[lined],
+        out_specs=[HBM, VMEM, HBM],
+        scratch_shapes=[
+            lined,
+            pltpu.VMEM((frames, tile_rows, columns), jnp.bfloat16),
+            pltpu.VMEM((frames, components), jnp.float32),
+            pltpu.SemaphoreType.DMA((1 + tile_rows // (2 * BR),)),
+        ],
         compiler_params=pltpu.CompilerParams(vmem_limit_bytes=20 << 20),
         name="traces",
     )(stacked, coupling, projected, traces_rows, cleaned)

time: 47.8 us -> 47.8 us (level)
  no operation moved by 1% of the time
where the time goes in v8:
time: 47.8 us; the launch traced here: 47.4 us
  Pallas kernels  21.6 us (45%)
  starting transfers between devices  16.9 us (35%)
  waiting for transfers between devices  6.07 us (13%)
  local copies, waits for them, and re-layouts  1.92 us (4%)
  between operations  0.83 us (2%)
    all_to_all x1, starting transfers between devices, per_device(): lax.all_to_all(pieces, 'tile', split_axis=0, concat_axis=0, tiled=True)  7.29 us
    pallas_call x1, Pallas kernels, per_device(): pl.pallas_call(kernel_fitted, out_shape=[jax.ShapeDtypeStruct((frames, ti...  6.15 us
    all_to_all x1, starting transfers between devices, per_device(): lax.all_to_all(leftover, 'tile', split_axis=0, concat_axis=0, tiled=True)  5.57 us
    pallas_call x1, Pallas kernels, per_device(): pl.pallas_call(functools.partial(kernel_coupling, frames), out_shape=[jax...  5.02 us
    pallas_call x1, Pallas kernels, per_device(): pl.pallas_call(kernel_early, out_shape=[jax.ShapeDtypeStruct((early_rows,...  3.84 us
    pallas_call x1, Pallas kernels, per_device(): pl.pallas_call(kernel_traces, out_shape=[jax.ShapeDtypeStruct((frames, co...  3.15 us
    all_to_all x1, waiting for transfers between devices, per_device(): lax.all_to_all(pieces, 'tile', split_axis=0, concat_axis=0, tiled=True)  2.72 us
    unnamed x21, local copies, waits for them, and re-layouts  1.92 us
  transfers between devices with their start and end apart: 7, of which 4 were waited for; matrix products, arithmetic and copies ran while one was open for 0% of the time, Pallas kernels for 25%

profile of v8, /device:TPU:0, one launch (start us, length us, event | category | flops | bytes accessed | tf_op | source)
XLA Modules:
  0.0 47.4 jit_solution(11219853330319280597)
XLA Ops:
  0.6 7.3 %all-to-all-start = ((bf16[8,64,256]{2,1,0:T(8,128)(2,1)}), bf16[8,64,256]{2,1,0:T(8,128)(2,1)S(1)}, u32[]{:S(2)}, u32[]{:S(2)}) async-start(bf16[8,64,256]{2,1,0:T(8,128)(2,1)} %bitcast.9), calls=%async_computation | async-start | bytes 524288 | tf_op jit(solution)/shard_map/all_to_all | solution.py:418
  7.9 6.2 %fitted.1 = (f32[8,64,256]{2,1,0:T(8,128)S(1)}, bf16[8,256,384]{2,1,0:T(8,128)(2,1)S(1)}) custom-call(bf16[64,256,384]{2,1,0:T(8,128)(2,1)} %footprints_hbm.5, s32[8,384]{1,0:T(8,128)} %support_ref.1, bf16[8,384]{1,0:T(8,128)(2,1)} %bitcast.5), custom_call_target="tpu_custom_call" | custom-call | flops 100663296 | bytes 12582912 | tf_op jit(solution)/shard_map/fitted/pallas_call | solution.py:425
  14.1 0.0 copy-start
  14.1 0.0 copy-start.2
  14.1 2.7 %all-to-all-done.movie_ref = bf16[8,64,256]{2,1,0:T(8,128)(2,1)S(1)} async-done(((bf16[8,64,256]{2,1,0:T(8,128)(2,1)}), bf16[8,64,256]{2,1,0:T(8,128)(2,1)S(1)}, u32[]{:S(2)}, u32[]{:S(2)}) %all-to-all-start) | async-done | bytes 262176 | tf_op jit(solution)/shard_map/all_to_all | solution.py:418
  16.9 0.1 subtract_convert_fusion.first_ref
  17.0 1.5 %collective-permute-start.1 = (bf16[8,24,256]{2,1,0:T(8,128)(2,1)S(1)}, bf16[8,24,256]{2,1,0:T(8,128)(2,1)S(1)}, u32[]{:S(2)}, u32[]{:S(2)}) collective-permute-start(bf16[8,24,256]{2,1,0:T(8,128)(2,1)S(1)} %get-tuple-element.29), channel_id=1, source_target_pairs={{0,4},{8,12},{16,20},{24,28},{4,0},{12,8},{20,16},{28,24},{1,5},{9... | collective-permute-start | bytes 294920 | tf_op jit(solution)/shard_map/ppermute | solution.py:459
  18.4 0.7 %collective-permute-start = (bf16[8,24,256]{2,1,0:T(8,128)(2,1)S(1)}, bf16[8,24,256]{2,1,0:T(8,128)(2,1)S(1)}, u32[]{:S(2)}, u32[]{:S(2)}) collective-permute-start(bf16[8,24,256]{2,1,0:T(8,128)(2,1)S(1)} %get-tuple-element.30), channel_id=1, source_target_pairs={{4,8},{12,16},{20,24},{8,4},{16,12},{24,20},{5,9},{13,17},{21,25},... | collective-permute-start | bytes 294920 | tf_op jit(solution)/shard_map/ppermute | solution.py:456
  19.1 3.8 %early.1 = (bf16[48,256,384]{2,1,0:T(8,128)(2,1)S(1)}, bf16[512,256]{1,0:T(8,128)(2,1)S(1)}, bf16[128,128]{1,0:T(8,128)(2,1)S(1)}) custom-call(bf16[64,256,384]{2,1,0:T(8,128)(2,1)} %footprints_hbm.5, s32[2,64]{1,0:T(2,128)S(1)} %bitcast.7), custom_call_target="tpu_custom_call" | custom-call | bytes 18874368 | tf_op jit(solution)/shard_map/early/pallas_call | solution.py:465
  23.0 0.0 copy-start.3
  23.0 1.6 %background.1 = (f32[2,512,128]{2,1,0:T(8,128)S(1)}, bf16[8,256,384]{2,1,0:T(8,128)(2,1)S(1)}) custom-call(bf16[8,64,256]{2,1,0:T(8,128)(2,1)S(1)} %all-to-all-done.movie_ref, bf16[8,64,256]{2,1,0:T(8,128)(2,1)S(1)} %subtract_convert_fusion.first_ref, bf16[8,24,256]{2,1,0:T(8,128)(2,1)S(1)} %collective-permute-done.edge_b_ref, ...), custom_call_target="tpu_custom_call" | custom-call | tf_op jit(solution)/shard_map/background/pallas_call | solution.py:483
  24.6 0.0 copy-start.4
  24.7 5.0 %coupling.1 = (bf16[400,16384]{1,0:T(8,128)(2,1)S(1)}, f32[384,384]{1,0:T(8,128)S(1)}, f32[8,384]{1,0:T(8,128)S(1)}) custom-call(bf16[48,256,384]{2,1,0:T(8,128)(2,1)S(1)} %get-tuple-element.16.early_ref, bf16[8,256,384]{2,1,0:T(8,128)(2,1)S(1)} %get-tuple-element.20.late_ref, bf16[8,256,384]{2,1,0:T(8,128)(2,1)S(1)} %get-tuple-element.21.kept_ref, ...), custom_call_target="tpu_custom_call" | custom-call | tf_op jit(solution)/shard_map/coupling/pallas_call | solution.py:508
  29.7 3.2 %traces.1 = (f32[8,384]{1,0:T(8,128)}, bf16[8,384]{1,0:T(8,128)(2,1)S(1)}, bf16[8,64,256]{2,1,0:T(8,128)(2,1)}) custom-call(bf16[400,16384]{1,0:T(8,128)(2,1)S(1)} %get-tuple-element.23.stacked_ref, f32[384,384]{1,0:T(8,128)S(1)} %get-tuple-element.24.coupling_ref, f32[8,384]{1,0:T(8,128)S(1)} %get-tuple-element.25.projected_ref, ...), custom_call_target="tpu_custom_call" | custom-call | tf_op jit(solution)/shard_map/traces/pallas_call | solution.py:524
  32.9 5.6 %all-to-all-start.1 = ((bf16[8,64,256]{2,1,0:T(8,128)(2,1)}), bf16[8,64,256]{2,1,0:T(8,128)(2,1)S(1)}, u32[]{:S(2)}, u32[]{:S(2)}) async-start(bf16[8,64,256]{2,1,0:T(8,128)(2,1)} %get-tuple-element.28), calls=%async_computation.1 | async-start | bytes 524288 | tf_op jit(solution)/shard_map/all_to_all | solution.py:547
  38.4 1.6 %collective-permute-start.3 = (bf16[8,384]{1,0:T(8,128)(2,1)S(1)}, bf16[8,384]{1,0:T(8,128)(2,1)S(1)}, u32[]{:S(2)}, u32[]{:S(2)}) collective-permute-start(bf16[8,384]{1,0:T(8,128)(2,1)S(1)} %get-tuple-element.27.refs_0_), channel_id=1, source_target_pairs={{0,2},{1,3},{2,0},{3,1},{4,6},{5,7},{6,4},{7,5},{8,10},{9,11},{10,... | collective-permute-start | bytes 18440 | tf_op jit(solution)/shard_map/ppermute | solution.py:545
  40.0 0.3 collective-permute-start.2
  40.3 1.2 %collective-permute-done.4.refs_3_ = bf16[8,384]{1,0:T(8,128)(2,1)S(1)} collective-permute-done((bf16[8,384]{1,0:T(8,128)(2,1)S(1)}, bf16[8,384]{1,0:T(8,128)(2,1)S(1)}, u32[]{:S(2)}, u32[]{:S(2)}) %collective-permute-start.4) | collective-permute-done | bytes 6176 | tf_op jit(solution)/shard_map/ppermute | solution.py:545
  41.5 0.6 %collective-permute-done.3.refs_2_ = bf16[8,384]{1,0:T(8,128)(2,1)S(1)} collective-permute-done((bf16[8,384]{1,0:T(8,128)(2,1)S(1)}, bf16[8,384]{1,0:T(8,128)(2,1)S(1)}, u32[]{:S(2)}, u32[]{:S(2)}) %collective-permute-start.3) | collective-permute-done | bytes 6176 | tf_op jit(solution)/shard_map/ppermute | solution.py:545
  42.2 0.6 %copy-done.8 = bf16[8,384]{1,0:T(8,128)(2,1)} copy-done((bf16[8,384]{1,0:T(8,128)(2,1)}, bf16[8,384]{1,0:T(8,128)(2,1)S(1)}, u32[]{:S(2)}) %copy-start.8) | copy-done | bytes 6168
  42.7 0.6 %copy-done.9 = bf16[8,384]{1,0:T(8,128)(2,1)} copy-done((bf16[8,384]{1,0:T(8,128)(2,1)}, bf16[8,384]{1,0:T(8,128)(2,1)S(1)}, u32[]{:S(2)}) %copy-start.9) | copy-done | bytes 6168
  43.3 1.8 %gram.1 = f32[384,384]{1,0:T(8,128)} custom-call(bf16[8,384]{1,0:T(8,128)(2,1)} %copy-done.5, bf16[8,384]{1,0:T(8,128)(2,1)} %copy-done.9, bf16[8,384]{1,0:T(8,128)(2,1)} %copy-done.8, bf16[8,384]{1,0:T(8,128)(2,1)} %copy-done.7), custom_call_target="tpu_custom_call" | custom-call | tf_op jit(solution)/shard_map/gram/pallas_call | solution.py:553
  45.2 1.5 %all-to-all-done.1 = bf16[8,64,256]{2,1,0:T(8,128)(2,1)S(1)} async-done(((bf16[8,64,256]{2,1,0:T(8,128)(2,1)}), bf16[8,64,256]{2,1,0:T(8,128)(2,1)S(1)}, u32[]{:S(2)}, u32[]{:S(2)}) %all-to-all-start.1) | async-done | bytes 262176 | tf_op jit(solution)/shard_map/all_to_all | solution.py:547
  46.7 0.7 %copy.12 = bf16[1,512,256]{2,1,0:T(8,128)(2,1)} copy(bf16[1,512,256]{2,1,0:T(8,128)(2,1)S(1)} %bitcast.8) | data formatting | bytes 524288
  (19 shorter events, 0.1 us)
Async XLA Ops:
  0.6 18.5 %copy-start.6 = (s32[64,2]{0,1:T(2,128)S(1)}, s32[64,2]{0,1:T(2,128)}, u32[]{:S(2)}) copy-start(s32[64,2]{0,1:T(2,128)} %param.13) | copy-start | bytes 1540
  0.6 16.2 %all-to-all-start = ((bf16[8,64,256]{2,1,0:T(8,128)(2,1)}), bf16[8,64,256]{2,1,0:T(8,128)(2,1)S(1)}, u32[]{:S(2)}, u32[]{:S(2)}) async-start(bf16[8,64,256]{2,1,0:T(8,128)(2,1)} %bitcast.9), calls=%async_computation | async-start | bytes 524288 | tf_op jit(solution)/shard_map/all_to_all | solution.py:418
  14.1 8.9 %copy-start = (bf16[768,256]{1,0:T(8,128)(2,1)S(1)}, bf16[768,256]{1,0:T(8,128)(2,1)}, u32[]{:S(2)}) copy-start(bf16[768,256]{1,0:T(8,128)(2,1)} %constant.25.clone.col_filter_ref) | copy-start | bytes 1179652
  14.1 8.9 %copy-start.1 = (f32[64,256]{1,0:T(8,128)S(1)}, f32[64,256]{1,0:T(8,128)}, u32[]{:S(2)}) copy-start(f32[64,256]{1,0:T(8,128)} %weight_ref.1) | copy-start | bytes 196612
  14.1 8.9 %copy-start.2 = (bf16[96,224]{1,0:T(8,128)(2,1)S(1)}, bf16[96,224]{1,0:T(8,128)(2,1)}, u32[]{:S(2)}) copy-start(bf16[96,224]{1,0:T(8,128)(2,1)} %constant.24.clone.row_filter_ref) | copy-start | bytes 129028
  17.0 6.0 %collective-permute-start.1 = (bf16[8,24,256]{2,1,0:T(8,128)(2,1)S(1)}, bf16[8,24,256]{2,1,0:T(8,128)(2,1)S(1)}, u32[]{:S(2)}, u32[]{:S(2)}) collective-permute-start(bf16[8,24,256]{2,1,0:T(8,128)(2,1)S(1)} %get-tuple-element.29), channel_id=1, source_target_pairs={{0,4},{8,12},{16,20},{24,28},{4,0},{12,8},{20,16},{28,24},{1,5},{9... | collective-permute-start | bytes 294920 | tf_op jit(solution)/shard_map/ppermute | solution.py:459
  18.4 4.5 %collective-permute-start = (bf16[8,24,256]{2,1,0:T(8,128)(2,1)S(1)}, bf16[8,24,256]{2,1,0:T(8,128)(2,1)S(1)}, u32[]{:S(2)}, u32[]{:S(2)}) collective-permute-start(bf16[8,24,256]{2,1,0:T(8,128)(2,1)S(1)} %get-tuple-element.30), channel_id=1, source_target_pairs={{4,8},{12,16},{20,24},{8,4},{16,12},{24,20},{5,9},{13,17},{21,25},... | collective-permute-start | bytes 294920 | tf_op jit(solution)/shard_map/ppermute | solution.py:456
  23.0 1.7 %copy-start.3 = (s32[8,384]{1,0:T(8,128)S(1)}, s32[8,384]{1,0:T(8,128)}, u32[]{:S(2)}) copy-start(s32[8,384]{1,0:T(8,128)} %support_ref.1) | copy-start | bytes 36868
  24.6 5.0 %copy-start.4 = (bf16[384,8]{0,1:T(8,128)(2,1)S(1)}, bf16[384,8]{0,1:T(8,128)(2,1)}, u32[]{:S(2)}) copy-start(bf16[384,8]{0,1:T(8,128)(2,1)} %param.11) | copy-start | bytes 18436
  32.9 9.3 %copy-start.5 = (bf16[8,384]{1,0:T(8,128)(2,1)}, bf16[8,384]{1,0:T(8,128)(2,1)S(1)}, u32[]{:S(2)}) copy-start(bf16[8,384]{1,0:T(8,128)(2,1)S(1)} %get-tuple-element.27.refs_0_) | copy-start | bytes 18436
  32.9 13.8 %all-to-all-start.1 = ((bf16[8,64,256]{2,1,0:T(8,128)(2,1)}), bf16[8,64,256]{2,1,0:T(8,128)(2,1)S(1)}, u32[]{:S(2)}, u32[]{:S(2)}) async-start(bf16[8,64,256]{2,1,0:T(8,128)(2,1)} %get-tuple-element.28), calls=%async_computation.1 | async-start | bytes 524288 | tf_op jit(solution)/shard_map/all_to_all | solution.py:547
  38.4 3.1 %collective-permute-start.4 = (bf16[8,384]{1,0:T(8,128)(2,1)S(1)}, bf16[8,384]{1,0:T(8,128)(2,1)S(1)}, u32[]{:S(2)}, u32[]{:S(2)}) collective-permute-start(bf16[8,384]{1,0:T(8,128)(2,1)S(1)} %get-tuple-element.27.refs_0_), channel_id=1, source_target_pairs={{0,3},{1,2},{2,1},{3,0},{4,7},{5,6},{6,5},{7,4},{8,11},{9,10},{10,... | collective-permute-start | bytes 18440 | tf_op jit(solution)/shard_map/ppermute | solution.py:545
  38.4 3.7 %collective-permute-start.3 = (bf16[8,384]{1,0:T(8,128)(2,1)S(1)}, bf16[8,384]{1,0:T(8,128)(2,1)S(1)}, u32[]{:S(2)}, u32[]{:S(2)}) collective-permute-start(bf16[8,384]{1,0:T(8,128)(2,1)S(1)} %get-tuple-element.27.refs_0_), channel_id=1, source_target_pairs={{0,2},{1,3},{2,0},{3,1},{4,6},{5,7},{6,4},{7,5},{8,10},{9,11},{10,... | collective-permute-start | bytes 18440 | tf_op jit(solution)/shard_map/ppermute | solution.py:545
  40.0 2.1 %collective-permute-start.2 = (bf16[8,384]{1,0:T(8,128)(2,1)S(1)}, bf16[8,384]{1,0:T(8,128)(2,1)S(1)}, u32[]{:S(2)}, u32[]{:S(2)}) collective-permute-start(bf16[8,384]{1,0:T(8,128)(2,1)S(1)} %get-tuple-element.27.refs_0_), channel_id=1, source_target_pairs={{0,1},{1,0},{2,3},{3,2},{4,5},{5,4},{6,7},{7,6},{8,9},{9,8},{10,11... | collective-permute-start | bytes 18440 | tf_op jit(solution)/shard_map/ppermute | solution.py:545
  41.5 0.6 %copy-start.7 = (bf16[8,384]{1,0:T(8,128)(2,1)}, bf16[8,384]{1,0:T(8,128)(2,1)S(1)}, u32[]{:S(2)}) copy-start(bf16[8,384]{1,0:T(8,128)(2,1)S(1)} %collective-permute-done.4.refs_3_) | copy-start | bytes 18436
  42.1 0.6 %copy-start.8 = (bf16[8,384]{1,0:T(8,128)(2,1)}, bf16[8,384]{1,0:T(8,128)(2,1)S(1)}, u32[]{:S(2)}) copy-start(bf16[8,384]{1,0:T(8,128)(2,1)S(1)} %collective-permute-done.3.refs_2_) | copy-start | bytes 18436
  42.7 0.6 %copy-start.9 = (bf16[8,384]{1,0:T(8,128)(2,1)}, bf16[8,384]{1,0:T(8,128)(2,1)S(1)}, u32[]{:S(2)}) copy-start(bf16[8,384]{1,0:T(8,128)(2,1)S(1)} %collective-permute-done.2.refs_1_) | copy-start | bytes 18436
